TPU v7x, 512 devices: a whole 4x8x8 slice. The times are simulated.
512 devices in a mesh: res: 128 (over x_lo, z, y), seq: 4 (over x_hi, core).
Axes of the slice: x: 4 (x_hi: 2, x_lo: 2; x = x_hi * 2 + x_lo), y: 8, z: 8, core: 2. Of those that a mesh axis runs over, the one named last changes fastest.
Arguments:
- left_proj: bfloat16 [256, 2048], P('res', 'seq'), may hold values from -6 to 6
- right_proj: bfloat16 [256, 2048], P('res', 'seq'), may hold values from -6 to 6
- pair_cotangent: bfloat16 [256, 256, 128], P('res'), may hold values from -3 to 3
- out_weight: bfloat16 [1024, 128], replicated, may hold values from -1.5 to 1.5
- out_bias: float32 [128], replicated, may hold values from -1.8 to 1.8
Outputs:
- pair_update: bfloat16 [256, 256, 128], P('res', 'seq')
- grad_left: float32 [256, 2048], P('res', 'seq')
- grad_right: float32 [256, 2048], P('res', 'seq')
- grad_weight: float32 [1024, 128], P('res')
- grad_bias: float32 [128], replicated
All inputs are finite; a program needn't handle non-finite values.
Results may differ from a plain program's by a relative error of at most 0.003.
Values may be sent and summed in bfloat16 or wider, within the bound.
No kernel may reach another device: no remote copies, remote signals or barrier semaphores. Data moves between devices by JAX's collectives and lax.ppermute only.
A program may use at most 64 MiB of HBM per device.

v0:
```python
import math

import jax
import jax.numpy as jnp
from jax import lax
from jax.sharding import PartitionSpec as P

C = 32
P_SIZE = 128
SEQ_DEV = 16
RES_DEV = 2
ROW_DEV = 2


def right_terms(left_rows, cotan_rows, weight_back, seq_total):
    row_total = cotan_rows.shape[0]
    col_total = cotan_rows.shape[1]
    channels = cotan_rows.shape[2]
    seq_count = left_rows.shape[1]
    width_in = left_rows.shape[2]
    row_step = math.gcd(row_total, 32)
    col_step = math.gcd(col_total, max(256 // row_step, 1))
    left_blocks = left_rows.reshape(row_total // row_step, row_step, seq_count, width_in)
    cotan_blocks = cotan_rows.reshape(
        row_total // row_step, row_step, col_total // col_step, col_step, channels
    )
    cotan_blocks = jnp.moveaxis(cotan_blocks, 2, 0)

    def column_block(cotan_column):

        def row_block(running, inputs):
            left_block, cotan_block = inputs
            spread = jnp.dot(
                cotan_block.reshape(row_step * col_step, channels),
                weight_back,
                preferred_element_type=jnp.float32,
            ).astype(jnp.bfloat16)
            spread = spread.reshape(row_step, col_step, width_in, width_in)
            term = jnp.einsum(
                "isx,ijxy->jsy", left_block, spread, preferred_element_type=jnp.float32
            )
            return (running + term, None)

        start_sum = jnp.zeros((col_step, seq_count, width_in), jnp.float32)
        running, unused = lax.scan(row_block, start_sum, (left_blocks, cotan_column))
        return running

    stacked = lax.map(column_block, cotan_blocks)
    return stacked.reshape(col_total, seq_count, width_in) / seq_total


def on_device(left_proj, right_proj, pair_cotangent, out_weight, out_bias):
    seq_total = SEQ_DEV * lax.axis_size("seq")
    weight_wide = out_weight.astype(jnp.float32)
    weight_back = out_weight.T
    left_rows = left_proj.reshape(ROW_DEV, SEQ_DEV, C)

    def block_terms(right_block, offset, stride):
        cotan_block = lax.dynamic_slice_in_dim(pair_cotangent, offset, stride, 1)
        products = (
            jnp.einsum("isx,jsy->ijxy", left_rows, right_block, preferred_element_type=jnp.float32)
            / seq_total
        )
        flat_outer = products.reshape(ROW_DEV * stride, C * C)
        flat_cotan = cotan_block.reshape(ROW_DEV * stride, P_SIZE)
        spread = jnp.dot(flat_cotan, weight_back, preferred_element_type=jnp.float32).astype(
            jnp.bfloat16
        )
        weight_add = jnp.dot(
            flat_outer.T, flat_cotan.astype(jnp.float32), precision=lax.Precision.HIGHEST
        )
        grad_add = jnp.einsum(
            "jsy,ijxy->isx",
            right_block,
            spread.reshape(ROW_DEV, stride, C, C),
            preferred_element_type=jnp.float32,
        )
        return (flat_outer, grad_add, weight_add)

    initial = (
        jnp.zeros((ROW_DEV, SEQ_DEV, C), jnp.float32),
        jnp.zeros((C * C, P_SIZE), jnp.float32),
    )
    col_total = right_proj.shape[0] * lax.axis_size("res")
    pair_start = jnp.zeros((ROW_DEV, col_total, P_SIZE), jnp.float32)
    col_piece = lax.all_gather(right_proj, "res", axis=0, tiled=True)
    piece_rows = col_piece.shape[0]
    block_stride = math.gcd(piece_rows, max(256 // ROW_DEV, 1))
    right_blocks = col_piece.reshape(piece_rows // block_stride, block_stride, SEQ_DEV, C)
    offsets = block_stride * jnp.arange(piece_rows // block_stride, dtype=jnp.int32)
    stride, right_blocks, offsets = (block_stride, right_blocks, offsets)

    def one_block(inner_sums, inputs):
        grad_inner, weight_inner, pair_inner = inner_sums
        right_block, offset = inputs
        flat_outer, grad_add, weight_add = block_terms(right_block, offset, stride)
        mixed = jnp.dot(flat_outer, weight_wide, precision=lax.Precision.HIGHEST).reshape(
            ROW_DEV, stride, P_SIZE
        )
        pair_inner = lax.dynamic_update_slice_in_dim(pair_inner, mixed, offset, 1)
        return ((grad_inner + grad_add, weight_inner + weight_add, pair_inner), None)

    result, unused = lax.scan(
        one_block, (initial[0], initial[1], pair_start), (right_blocks, offsets)
    )
    grad_rows, weight_term, partial_pair = result
    summed = lax.psum_scatter(partial_pair, "seq", scatter_dimension=1, tiled=True)
    pair_update = (summed + out_bias).astype(jnp.bfloat16)
    grad_left = (grad_rows / seq_total).reshape(ROW_DEV, SEQ_DEV * C)
    grad_right = lax.psum_scatter(
        right_terms(left_rows, pair_cotangent, weight_back, seq_total).reshape(
            lax.axis_size("res") * RES_DEV, SEQ_DEV * C
        ),
        "res",
        scatter_dimension=0,
        tiled=True,
    )
    weight_shard = lax.psum_scatter(weight_term, "res", scatter_dimension=0, tiled=True)
    grad_weight = lax.psum(weight_shard, "seq")
    grad_bias = lax.psum(jnp.sum(pair_cotangent, axis=(0, 1), dtype=jnp.float32), "res")
    return (pair_update, grad_left, grad_right, grad_weight, grad_bias)


def solution(mesh):
    return jax.shard_map(
        on_device,
        mesh=mesh,
        in_specs=(P("res", "seq"), P("res", "seq"), P("res", None, None), P(), P()),
        out_specs=(P("res", "seq", None), P("res", "seq"), P("res", "seq"), P("res", None), P()),
        check_vma=False,
    )
```

profile of v0, /device:TPU:1, one launch (start us, length us, event | category | flops | bytes accessed | tf_op | source)
XLA Modules:
  0.0 1561.9 jit_solution(12398420144484929554)
XLA Ops:
  8.1 1.1 copy.33
  9.3 0.7 copy-done.3
  9.9 259.3 %all-gather = bf16[128,2,512]{2,1,0:T(2,128)(2,1)S(1)} all-gather(bf16[1,2,512]{2,1,0:T(2,128)(2,1)S(1)} %bitcast.122), channel_id=1, replica_groups=mesh['res'=128,'seq'=4] {'res'}, dimensions={0}, use_global_device_ids=true | all-gather | bytes 264192 | tf_op jit(solution)/shard_map/all_gather | solution.py:86
  269.2 0.5 reshape.50
  269.7 1.6 copy.34
  271.4 0.8 broadcast_in_dim.19
  272.2 24.9 %while.30 = (s32[]{:T(128)}, f32[2,16,32]{2,1,0:T(8,128)S(1)}, f32[1024,128]{1,0:T(8,128)S(1)}, f32[2,256,128]{2,1,0:T(8,128)}, s32[2]{0:T(128)S(1)}, /*index=5*...) while((s32[]{:T(128)}, f32[2,16,32]{2,1,0:T(8,128)S(1)}, ...), condition=%wide.region_1.2_spmd.clone, body=%wide.region_0.1_spmd.clone.sunk | while | flops 889980928 | bytes 13249726 | solution.py:103
  272.2 0.6 dynamic_slice.43
  274.7 0.9 constant_dynamic-slice_fusion.7
  275.7 1.2 fusion.57
  276.9 0.8 copy.69
  277.7 0.8 convolution_add_fusion.2
  278.5 0.3 convolution_convert_fusion.5
  278.8 0.2 copy.68
  279.2 1.4 fusion.56
  280.6 0.6 copy.70
  281.2 1.8 fusion.58
  283.0 1.7 dynamic_update_slice.12
  284.7 0.6 dynamic_slice.43
  287.2 0.9 constant_dynamic-slice_fusion.7
  288.1 1.2 fusion.57
  289.3 0.8 copy.69
  290.2 0.8 convolution_add_fusion.2
  291.0 0.3 convolution_convert_fusion.5
  291.6 1.4 fusion.56
  293.0 0.6 copy.70
  293.6 1.8 fusion.58
  295.4 1.6 dynamic_update_slice.12
  297.2 0.6 copy-done
  297.8 3.8 while.29
  297.8 0.8 constant_dynamic-slice_fusion.6
  298.7 0.3 convolution_convert_fusion.4
  299.3 0.4 fusion.45
  299.7 0.9 constant_dynamic-slice_fusion.6
  300.6 0.3 convolution_convert_fusion.4
  301.2 0.4 fusion.45
  301.7 0.4 copy.36
  302.1 0.8 copy.56
  303.0 1.3 dynamic-slice
  305.5 0.7 reshape.52
  306.2 1.0 convert_reduce_fusion
  307.2 252.2 %psum.15 = f32[128]{0:T(128)} all-reduce(f32[128]{0:T(128)S(1)} %convert_reduce_fusion), channel_id=1, replica_groups=mesh['res'=128,'seq'=4] {'res'}, use_global_device_ids=true, to_apply=%region_9.10 | all-reduce | flops 128 | bytes 1024 | tf_op jit(solution)/shard_map/psum | solution.py:120
  559.4 1.5 add_convert_fusion
  560.8 891.3 %all-reduce.5.cloned.1.call-done = (f32[256,512]{0,1:T(8,128)}, f32[1024,128]{1,0:T(8,128)}) async-done(((f32[256,512]{0,1:T(8,128)}, f32[1024,128]{1,0:T(8,128)}), (f32[256,512]{0,1:T(8,128)}, f32[1024,128]{1,0:T(8,128)})) %all-reduce.5.cloned.1.call-update) | async-done | bytes 1048592
  1452.1 1.1 constant_dynamic-slice_fusion.3
  1453.2 0.7 copy.37
  1453.9 0.7 constant_dynamic-slice_fusion.2
  1454.6 99.9 %psum.14 = f32[8,128]{1,0:T(8,128)} all-reduce(f32[8,128]{1,0:T(8,128)S(1)} %constant_dynamic-slice_fusion.2), channel_id=1, replica_groups=mesh['res'=128,'seq'=4] {'seq'}, use_global_device_ids=true, to_apply=%region_7.8 | all-reduce | flops 1024 | bytes 8192 | tf_op jit(solution)/shard_map/psum | solution.py:119
  (29 shorter events, 1.5 us)
Async XLA Ops:
  8.0 1.2 copy-start.1
  8.0 551.4 %reduce-scatter.3.cloned.1.call-start = ((), (), s32[]{:S(2)}) async-start(), calls=%async_computation.1 | async-start | bytes 327680 | tf_op jit(solution)/shard_map/reduce_scatter | solution.py:107
  9.3 0.7 copy-start.3
  269.7 1.7 copy-start.2
  297.1 0.8 copy-start
  297.1 1155.0 %all-reduce.5.cloned.1.call-start = ((), (), s32[]{:S(2)}) async-start(), calls=%async_computation.2 | async-start | bytes 2097152
  307.2 252.2 %copy-start.4 = (f32[128]{0:T(128)S(1)}, f32[128]{0:T(128)}, u32[]{:S(2)}) copy-start(f32[128]{0:T(128)} %param.13) | copy-start | bytes 1540
Sparse Core Ops, SparseCore 0:
  297.2 83.1 reduce-scatter.2
Sparse Core Ops, SparseCore 1:
  303.0 1149.0 all-reduce.4
where the time goes:
time: 1560 us
  waiting for transfers between devices  891 us (57%)
  blocking collectives  611 us (39%)
  local copies, waits for them, and re-layouts  23.3 us (1%)
  between operations  16.9 us (1%)
    unnamed x3, waiting for transfers between devices  891 us
    all_gather x1, blocking collectives, on_device(): col_piece = lax.all_gather(right_proj, 'res', axis=0, tiled=True)  259 us
    psum x1, blocking collectives, on_device(): lax.psum(jnp.sum(pair_cotangent, axis=(0, 1), dtype=jnp.float32), 'res')  252 us
    psum x1, blocking collectives, on_device(): grad_weight = lax.psum(weight_shard, 'seq')  99.9 us
  transfers between devices with their start and end apart: 2, of which 1 were waited for; matrix products, arithmetic and copies ran while one was open for 1% of the time, Pallas kernels for 0%

commit v1 on v0

v1 whole, which is shorter than its diff:
```python
import jax
import jax.numpy as jnp
from jax import lax
from jax.sharding import PartitionSpec as P

C = 32
P_SIZE = 128
SEQ_DEV = 16
ROW_DEV = 2
WIDE = SEQ_DEV * C


def hi_lo(value):
    high = lax.reduce_precision(value, 8, 7)
    return high.astype(jnp.bfloat16), (value - high).astype(jnp.bfloat16)


def dot32(form, a, b):
    return jnp.einsum(form, a, b, preferred_element_type=jnp.float32)


def on_device(left_proj, right_proj, pair_cotangent, out_weight, out_bias):
    res = lax.axis_size("res")
    seq = lax.axis_size("seq")
    scale = 1.0 / (SEQ_DEV * seq)
    left_rows = left_proj.reshape(ROW_DEV, SEQ_DEV, C)
    weight = out_weight.reshape(C, C, P_SIZE)

    mixed_hi, mixed_lo = hi_lo(dot32("isx,xyk->isyk", left_rows, weight))
    grad_right = dot32("ijk,isyk->jsy", pair_cotangent, mixed_hi) + dot32(
        "ijk,isyk->jsy", pair_cotangent, mixed_lo
    )
    bias_pair = jnp.stack(hi_lo(jnp.sum(pair_cotangent, axis=(0, 1), dtype=jnp.float32)))

    message = jnp.concatenate(
        [
            jnp.broadcast_to(right_proj[None], (res, ROW_DEV, WIDE)),
            grad_right.reshape(res, ROW_DEV, WIDE).astype(jnp.bfloat16),
            jnp.broadcast_to(bias_pair[None], (res, 2, P_SIZE)),
        ],
        axis=2,
    )
    arrived = lax.all_to_all(message, "res", 0, 0, tiled=True)
    right_all = arrived[:, :, :WIDE].reshape(res * ROW_DEV, SEQ_DEV, C)
    grad_right = jnp.sum(arrived[:, :, WIDE : 2 * WIDE], axis=0, dtype=jnp.float32) * scale
    grad_bias = jnp.sum(arrived[:, :, 2 * WIDE :], axis=(0, 1), dtype=jnp.float32)

    pair = dot32("jsy,isyk->ijk", right_all, mixed_hi) + dot32("jsy,isyk->ijk", right_all, mixed_lo)
    back_hi, back_lo = hi_lo(dot32("jsy,ijk->isyk", right_all, pair_cotangent))
    grad_left = dot32("isyk,xyk->isx", back_hi, weight) + dot32("isyk,xyk->isx", back_lo, weight)
    grad_weight = dot32("isx,isyk->xyk", left_rows, back_hi) + dot32("isx,isyk->xyk", left_rows, back_lo)

    rows = C * C // res
    parts = lax.all_to_all(
        grad_weight.reshape(res, rows, P_SIZE).astype(jnp.bfloat16), "res", 0, 0, tiled=True
    )
    weight_sum = jnp.sum(parts, axis=0, dtype=jnp.float32)

    cols = pair.shape[1] // seq
    pair = jnp.moveaxis(pair.reshape(ROW_DEV, seq, cols, P_SIZE), 1, 0)
    last = jnp.concatenate(
        [
            pair.reshape(seq, ROW_DEV * cols, P_SIZE),
            jnp.broadcast_to(weight_sum[None], (seq, rows, P_SIZE)),
        ],
        axis=1,
    )
    summed = jnp.sum(lax.all_to_all(last, "seq", 0, 0, tiled=True), axis=0) * scale
    pair_update = (summed[: ROW_DEV * cols].reshape(ROW_DEV, cols, P_SIZE) + out_bias).astype(jnp.bfloat16)
    return (
        pair_update,
        (grad_left * scale).reshape(ROW_DEV, WIDE),
        grad_right,
        summed[ROW_DEV * cols :],
        grad_bias,
    )


def solution(mesh):
    return jax.shard_map(
        on_device,
        mesh=mesh,
        in_specs=(P("res", "seq"), P("res", "seq"), P("res", None, None), P(), P()),
        out_specs=(P("res", "seq", None), P("res", "seq"), P("res", "seq"), P("res", None), P()),
        check_vma=False,
    )
```

time: 1560 us -> 88.7 us (0.06)
  waiting for transfers between devices: 891 us -> 17.2 us
  blocking collectives: 611 us -> 39.4 us
  local copies, waits for them, and re-layouts: 23.3 us -> 6.72 us
  between operations: 16.9 us -> 0.85 us
    unnamed x3 -> x0, waiting for transfers between devices: 891 us -> none
    psum x2 -> x0, blocking collectives: 352 us -> none  [the longest x1 252 us: on_device(): lax.psum(jnp.sum(pair_cotangent, axis=(0, 1), dtype=jnp.float32), 'res')]
    all_gather x1 -> x0, blocking collectives: 259 us -> none  [on_device(): col_piece = lax.all_gather(right_proj, 'res', axis=0, tiled=True)]
    all_to_all x0 -> x1, blocking collectives: none -> 39.4 us  [on_device(): arrived = lax.all_to_all(message, 'res', 0, 0, tiled=True)]
    all_to_all x0 -> x2, waiting for transfers between devices: none -> 17.2 us  [the longest x1 11 us: on_device(): lax.all_to_all(grad_weight.reshape(res, rows, P_SIZE).astype(jnp.bfloat16...]
  transfers between devices with their start and end apart: 2 -> 2, of which waited for: 1 -> 2; matrix products, arithmetic and copies ran while one was open for 1% -> 3% of each run, Pallas kernels for 0% -> 0%
where the time goes in v1:
time: 88.7 us; the launch traced here: 88.3 us
  blocking collectives  39.4 us (44%)
  waiting for transfers between devices  17.2 us (19%)
  starting transfers between devices  14.7 us (17%)
  local copies, waits for them, and re-layouts  6.72 us (8%)
  matrix products  4.79 us (5%)
  other arithmetic  4.66 us (5%)
    all_to_all x1, blocking collectives, on_device(): arrived = lax.all_to_all(message, 'res', 0, 0, tiled=True)  39.4 us
    all_to_all x1, waiting for transfers between devices, on_device(): lax.all_to_all(grad_weight.reshape(res, rows, P_SIZE).astype(jnp.bfloat16...  11 us
    all_to_all x1, starting transfers between devices, on_device(): lax.all_to_all(last, 'seq', 0, 0, tiled=True)  7.52 us
    all_to_all x1, starting transfers between devices, on_device(): lax.all_to_all(grad_weight.reshape(res, rows, P_SIZE).astype(jnp.bfloat16...  7.16 us
    all_to_all x1, waiting for transfers between devices, on_device(): lax.all_to_all(last, 'seq', 0, 0, tiled=True)  6.25 us
    dot_general x10, matrix products, dot32(): return jnp.einsum(form, a, b, preferred_element_type=jnp.float32)  4.79 us
  transfers between devices with their start and end apart: 2, of which 2 were waited for; matrix products, arithmetic and copies ran while one was open for 3% of the time, Pallas kernels for 0%

profile of v1, /device:TPU:1, one launch (start us, length us, event | category | flops | bytes accessed | tf_op | source)
XLA Modules:
  0.0 88.3 jit_solution(10550847482541470258)
XLA Ops:
  0.6 0.0 copy-start
  0.6 1.1 %convert_reduce_fusion.2 = f32[128]{0:T(128)S(1)} fusion(bf16[2,256,128]{2,1,0:T(8,128)(2,1)} %param.7), kind=kLoop, calls=%fused_computation.40 | loop fusion | flops 130944 | bytes 131584 | tf_op jit(solution)/shard_map/reduce_sum | solution.py:33
  1.7 0.8 reshape.66
  2.5 1.2 %reduce-precision_convert_fusion.1 = (bf16[2,16,32,128]{3,1,2,0:T(8,128)(2,1)S(1)}, bf16[2,16,32,128]{3,1,2,0:T(8,128)(2,1)S(1)}) fusion(bf16[32,32,128]{2,1,0:T(8,128)(2,1)} %bitcast.100, bf16[2,16,32,1]{2,1,0,3:T(8,128)(2,1)S(1)} %reshape.66), kind=kOutput, calls=%fused_computation.23 | convolution fusion | flops 8912896 | bytes 788480 | tf_op jit(solution)/shard_map/isx,xyk->isyk/dot_general | solution.py:19
  3.7 1.2 %convolution_bitcast_fusion.3 = f32[16,32,256]{2,1,0:T(8,128)S(1)} fusion(bf16[2,16,32,128]{3,1,2,0:T(8,128)(2,1)S(1)} %get-tuple-element.8, bf16[2,256,128]{2,1,0:T(8,128)(2,1)} %param.7), kind=kOutput, calls=%fused_computation.3 | convolution fusion | flops 67108864 | bytes 917504 | tf_op jit(solution)/shard_map/ijk,isyk->jsy/dot_general | solution.py:19
  4.8 0.0 copy-done
  4.8 0.3 fusion.4
  5.1 0.0 copy-start.2
  5.1 0.9 %copy.26 = bf16[256,16,32]{2,1,0:T(8,128)(2,1)S(1)} copy(bf16[256,16,32]{0,2,1:T(8,128)(2,1)S(1)} %fusion.4) | data formatting | bytes 524288 | tf_op jit(solution)/shard_map/convert_element_type | solution.py:38
  6.1 0.8 convert_element_type.69
  7.0 0.0 copy-done.2
  7.0 0.1 broadcast_in_dim.6
  7.1 0.5 pad_maximum_fusion
  7.7 39.4 %all_to_all.15 = bf16[128,2,1152]{2,1,0:T(2,128)(2,1)S(1)} all-to-all(bf16[128,2,1152]{2,1,0:T(2,128)(2,1)S(1)} %pad_maximum_fusion), channel_id=1, replica_groups=mesh['res'=128,'seq'=4] {'res'}, dimensions={0} | all-to-all | bytes 1179648 | tf_op jit(solution)/shard_map/all_to_all | solution.py:43
  47.1 0.2 slice.20
  47.3 0.5 reshape.61
  47.8 1.1 %copy.45 = bf16[256,16,32,1]{0,1,2,3:T(8,128)(2,1)S(1)} copy(bf16[256,16,32,1]{2,1,0,3:T(8,128)(2,1)S(1)} %bitcast.96) | data formatting | bytes 524288 | tf_op jit(solution)/shard_map/reshape | solution.py:44
  48.9 0.4 reduce-precision_convert_fusion
  49.3 0.3 convolution_bitcast_fusion.5
  49.6 0.3 fusion.7
  49.9 0.3 convolution_bitcast_fusion
  50.2 0.0 copy-start.1
  50.2 0.3 fusion.5
  50.5 0.8 copy.36
  51.3 7.2 %all-to-all-start.1 = ((bf16[128,8,128]{2,1,0:T(8,128)(2,1)}), bf16[128,8,128]{2,1,0:T(8,128)(2,1)S(1)}, u32[]{:S(2)}, u32[]{:S(2)}) async-start(bf16[128,8,128]{2,1,0:T(8,128)(2,1)} %bitcast.27), calls=%async_computation.1 | async-start | bytes 524288 | tf_op jit(solution)/shard_map/all_to_all | solution.py:54
  58.4 0.0 copy-done.1
  58.4 0.3 convolution_bitcast_fusion.7
  58.8 0.1 copy.31
  58.9 0.3 fusion.9
  59.2 0.7 reshape.65
  59.9 0.7 convert_reduce_fusion.3
  60.6 0.3 convert_reduce_fusion
  60.9 0.0 copy-start.3
  60.9 11.0 %all-to-all-done.1 = bf16[128,8,128]{2,1,0:T(8,128)(2,1)S(1)} async-done(((bf16[128,8,128]{2,1,0:T(8,128)(2,1)}), bf16[128,8,128]{2,1,0:T(8,128)(2,1)S(1)}, u32[]{:S(2)}, u32[]{:S(2)}) %all-to-all-start.1) | async-done | bytes 262176 | tf_op jit(solution)/shard_map/all_to_all | solution.py:54
  71.8 0.1 convert_reduce_fusion.1
  72.0 0.7 pad_maximum_fusion.1
  72.7 7.5 %all-to-all-start.2 = ((f32[4,136,128]{2,1,0:T(8,128)}), f32[4,136,128]{2,1,0:T(8,128)S(1)}, u32[]{:S(2)}, u32[]{:S(2)}) async-start(f32[4,136,128]{2,1,0:T(8,128)} %pad_maximum_fusion.1), calls=%async_computation.2 | async-start | bytes 557056 | tf_op jit(solution)/shard_map/all_to_all | solution.py:68
  80.2 0.6 broadcast_multiply_fusion.1
  80.8 6.3 %all-to-all-done.2 = f32[4,136,128]{2,1,0:T(8,128)S(1)} async-done(((f32[4,136,128]{2,1,0:T(8,128)}), f32[4,136,128]{2,1,0:T(8,128)S(1)}, u32[]{:S(2)}, u32[]{:S(2)}) %all-to-all-start.2) | async-done | bytes 278560 | tf_op jit(solution)/shard_map/all_to_all | solution.py:68
  87.1 0.6 slice.23
  87.7 0.0 copy-done.3
  87.7 0.6 add_convert_fusion
  (8 shorter events, 0.1 us)
Async XLA Ops:
  0.6 4.2 %copy-start = (bf16[2,256,128]{2,1,0:T(8,128)(2,1)S(1)}, bf16[2,256,128]{2,1,0:T(8,128)(2,1)}, u32[]{:S(2)}) copy-start(bf16[2,256,128]{2,1,0:T(8,128)(2,1)} %param.7) | copy-start | bytes 393220
  5.1 1.8 %copy-start.2 = (bf16[2,512]{1,0:T(2,128)(2,1)S(1)}, bf16[2,512]{1,0:T(2,128)(2,1)}, u32[]{:S(2)}) copy-start(bf16[2,512]{1,0:T(2,128)(2,1)} %param.6) | copy-start | bytes 6148
  50.2 8.3 %copy-start.1 = (bf16[1024,128]{1,0:T(8,128)(2,1)S(1)}, bf16[1024,128]{1,0:T(8,128)(2,1)}, u32[]{:S(2)}) copy-start(bf16[1024,128]{1,0:T(8,128)(2,1)} %param.8) | copy-start | bytes 786436
  51.3 20.6 %all-to-all-start.1 = ((bf16[128,8,128]{2,1,0:T(8,128)(2,1)}), bf16[128,8,128]{2,1,0:T(8,128)(2,1)S(1)}, u32[]{:S(2)}, u32[]{:S(2)}) async-start(bf16[128,8,128]{2,1,0:T(8,128)(2,1)} %bitcast.27), calls=%async_computation.1 | async-start | bytes 524288 | tf_op jit(solution)/shard_map/all_to_all | solution.py:54
  60.9 26.9 %copy-start.3 = (f32[128]{0:T(128)S(1)}, f32[128]{0:T(128)}, u32[]{:S(2)}) copy-start(f32[128]{0:T(128)} %param.9) | copy-start | bytes 1540
  72.7 14.4 %all-to-all-start.2 = ((f32[4,136,128]{2,1,0:T(8,128)}), f32[4,136,128]{2,1,0:T(8,128)S(1)}, u32[]{:S(2)}, u32[]{:S(2)}) async-start(f32[4,136,128]{2,1,0:T(8,128)} %pad_maximum_fusion.1), calls=%async_computation.2 | async-start | bytes 557056 | tf_op jit(solution)/shard_map/all_to_all | solution.py:68

commit v2 on v1

v2 whole, which is shorter than its diff:
```python
import jax
import jax.numpy as jnp
from jax import lax
from jax.sharding import PartitionSpec as P

C = 32
P_SIZE = 128
SEQ_DEV = 16
ROW_DEV = 2
WIDE = SEQ_DEV * C


def hi_lo(value):
    high = lax.reduce_precision(value, 8, 7)
    return high.astype(jnp.bfloat16), (value - high).astype(jnp.bfloat16)


def dot32(form, a, b):
    return jnp.einsum(form, a, b, preferred_element_type=jnp.float32)


def on_device(left_proj, right_proj, pair_cotangent, out_weight, out_bias):
    res = lax.axis_size("res")
    seq = lax.axis_size("seq")
    scale = 1.0 / (SEQ_DEV * seq)
    left_rows = left_proj.reshape(ROW_DEV, SEQ_DEV, C)
    weight = out_weight.reshape(C, C, P_SIZE)

    right_all = lax.all_to_all(
        jnp.broadcast_to(right_proj[None], (res, ROW_DEV, WIDE)), "res", 0, 0, tiled=True
    ).reshape(res * ROW_DEV, SEQ_DEV, C)

    mixed_hi, mixed_lo = hi_lo(dot32("isx,xyk->isyk", left_rows, weight))
    grad_right = dot32("ijk,isyk->jsy", pair_cotangent, mixed_hi) + dot32(
        "ijk,isyk->jsy", pair_cotangent, mixed_lo
    )
    grad_right = grad_right.astype(jnp.bfloat16).reshape(res, ROW_DEV, WIDE)
    bias_pair = jnp.stack(hi_lo(jnp.sum(pair_cotangent, axis=(0, 1), dtype=jnp.float32)))
    bias_pair = jnp.broadcast_to(bias_pair[None], (res, 2, P_SIZE))

    back_hi, back_lo = hi_lo(dot32("jsy,ijk->isyk", right_all, pair_cotangent))
    grad_weight = dot32("isx,isyk->xyk", left_rows, back_hi) + dot32("isx,isyk->xyk", left_rows, back_lo)
    rows = C * C // res
    grad_weight = grad_weight.astype(jnp.bfloat16).reshape(res, ROW_DEV, rows * P_SIZE // ROW_DEV)

    parts = lax.all_to_all(
        jnp.concatenate([grad_right, grad_weight, bias_pair], axis=2), "res", 0, 0, tiled=True
    )

    grad_left = dot32("isyk,xyk->isx", back_hi, weight) + dot32("isyk,xyk->isx", back_lo, weight)
    pair = dot32("jsy,isyk->ijk", right_all, mixed_hi) + dot32("jsy,isyk->ijk", right_all, mixed_lo)
    cols = pair.shape[1] // seq
    pair = jnp.moveaxis(pair.reshape(ROW_DEV, seq, cols, P_SIZE), 1, 0).reshape(seq, ROW_DEV * cols, P_SIZE)
    pair_sent, pair_rest = hi_lo(pair)
    pair_rest = lax.dynamic_index_in_dim(pair_rest, lax.axis_index("seq"), 0, keepdims=False)

    totals = jnp.sum(parts, axis=0, dtype=jnp.float32)
    grad_right = totals[:, :WIDE] * scale
    weight_hi, weight_lo = hi_lo(totals[:, WIDE : WIDE + rows * P_SIZE // ROW_DEV].reshape(rows, P_SIZE))
    grad_bias = totals[0, -P_SIZE:] + totals[1, -P_SIZE:]

    last = jnp.concatenate(
        [
            pair_sent,
            jnp.broadcast_to(weight_hi[None], (seq, rows, P_SIZE)),
            jnp.broadcast_to(weight_lo[None], (seq, rows, P_SIZE)),
        ],
        axis=1,
    )
    summed = jnp.sum(lax.all_to_all(last, "seq", 0, 0, tiled=True), axis=0, dtype=jnp.float32) * scale
    split = ROW_DEV * cols
    pair_update = (summed[:split] + pair_rest * scale).reshape(ROW_DEV, cols, P_SIZE) + out_bias
    return (
        pair_update.astype(jnp.bfloat16),
        (grad_left * scale).reshape(ROW_DEV, WIDE),
        grad_right,
        summed[split : split + rows] + summed[split + rows :],
        grad_bias,
    )


def solution(mesh):
    return jax.shard_map(
        on_device,
        mesh=mesh,
        in_specs=(P("res", "seq"), P("res", "seq"), P("res", None, None), P(), P()),
        out_specs=(P("res", "seq", None), P("res", "seq"), P("res", "seq"), P("res", None), P()),
        check_vma=False,
    )
```

time: 88.7 us -> 82.1 us (0.926)
  blocking collectives: 39.4 us -> 0 us
  starting transfers between devices: 14.7 us -> 34.3 us
  waiting for transfers between devices: 17.2 us -> 29.7 us
  local copies, waits for them, and re-layouts: 6.72 us -> 8.11 us
  matrix products: 4.79 us -> 3.57 us
    all_to_all x1 -> x0, blocking collectives: 39.4 us -> none  [on_device(): arrived = lax.all_to_all(message, 'res', 0, 0, tiled=True)]
    all_to_all x1 -> x2, starting transfers between devices: 7.16 us -> 25.7 us  [the longest x1 19.3 us: on_device(): lax.all_to_all(jnp.broadcast_to(right_proj[None], (res, ROW_DEV, WIDE)),...]
    all_to_all x1 -> x2, waiting for transfers between devices: 11 us -> 25 us  [the longest x1 15.2 us: on_device(): lax.all_to_all(jnp.concatenate([grad_right, grad_weight, bias_pair], axis...]
    reshape x2 -> x6, local copies, waits for them, and re-layouts: 1.59 us -> 3.35 us  [the longest x3 2.42 us: on_device(): right_all = lax.all_to_all(jnp.broadcast_to(right_proj[None], (res, ROW_D...]
    all_to_all x1, waiting for transfers between devices: 6.25 us -> 4.72 us  [on_device(): lax.all_to_all(last, 'seq', 0, 0, tiled=True)]
    convert_element_type x3 -> x2, local copies, waits for them, and re-layouts: 2.55 us -> 1.05 us  [the longest x1 0.95 us: on_device(): grad_right = grad_right.astype(jnp.bfloat16).reshape(res, ROW_DEV, WIDE)]
    broadcast_in_dim x1, local copies, waits for them, and re-layouts: 0.14 us -> 1.56 us  [on_device(): jnp.broadcast_to(right_proj[None], (res, ROW_DEV, WIDE))]
    dot_general x10, matrix products: 4.79 us -> 3.57 us  [dot32(): return jnp.einsum(form, a, b, preferred_element_type=jnp.float32)]
  transfers between devices with their start and end apart: 2 -> 3, of which waited for: 2 -> 3; matrix products, arithmetic and copies ran while one was open for 3% -> 10% of each run, Pallas kernels for 0% -> 0%
where the time goes in v2:
time: 82.1 us; the launch traced here: 81.6 us
  starting transfers between devices  34.3 us (42%)
  waiting for transfers between devices  29.7 us (36%)
  local copies, waits for them, and re-layouts  8.11 us (10%)
  other arithmetic  5.08 us (6%)
  matrix products  3.57 us (4%)
  between operations  0.84 us (1%)
    all_to_all x1, starting transfers between devices, on_device(): lax.all_to_all(jnp.broadcast_to(right_proj[None], (res, ROW_DEV, WIDE)),...  19.3 us
    all_to_all x1, waiting for transfers between devices, on_device(): lax.all_to_all(jnp.concatenate([grad_right, grad_weight, bias_pair], axis...  15.2 us
    all_to_all x1, waiting for transfers between devices, on_device(): lax.all_to_all(jnp.broadcast_to(right_proj[None], (res, ROW_DEV, WIDE)),...  9.76 us
    all_to_all x1, starting transfers between devices, on_device(): lax.all_to_all(last, 'seq', 0, 0, tiled=True)  8.61 us
    all_to_all x1, starting transfers between devices, on_device(): lax.all_to_all(jnp.concatenate([grad_right, grad_weight, bias_pair], axis...  6.42 us
    all_to_all x1, waiting for transfers between devices, on_device(): lax.all_to_all(last, 'seq', 0, 0, tiled=True)  4.72 us
    dot_general x10, matrix products, dot32(): return jnp.einsum(form, a, b, preferred_element_type=jnp.float32)  3.57 us
    reshape x3, local copies, waits for them, and re-layouts, on_device(): right_all = lax.all_to_all(jnp.broadcast_to(right_proj[None], (res, ROW_D...  2.42 us
  transfers between devices with their start and end apart: 3, of which 3 were waited for; matrix products, arithmetic and copies ran while one was open for 10% of the time, Pallas kernels for 0%

profile of v2, /device:TPU:1, one launch (start us, length us, event | category | flops | bytes accessed | tf_op | source)
XLA Modules:
  0.0 81.6 jit_solution(12931028253237295495)
XLA Ops:
  0.6 0.0 copy-start
  0.6 1.6 %broadcast_in_dim.8 = bf16[128,2,512]{2,1,0:T(2,128)(2,1)} broadcast(bf16[2,512]{1,0:T(2,128)(2,1)} %param.6), dimensions={1,2} | broadcast | bytes 264192 | tf_op jit(solution)/shard_map/broadcast_in_dim | solution.py:30
  2.2 19.3 %all-to-all-start = ((bf16[128,2,512]{2,1,0:T(2,128)(2,1)}), bf16[128,2,512]{2,1,0:T(2,128)(2,1)S(1)}, u32[]{:S(2)}, u32[]{:S(2)}) async-start(bf16[128,2,512]{2,1,0:T(2,128)(2,1)} %broadcast_in_dim.8), calls=%async_computation | async-start | bytes 524288 | tf_op jit(solution)/shard_map/all_to_all | solution.py:29
  21.5 0.8 reshape.93
  22.3 1.2 %reduce-precision_convert_fusion.1 = (bf16[2,16,32,128]{3,1,2,0:T(8,128)(2,1)S(1)}, bf16[2,16,32,128]{3,1,2,0:T(8,128)(2,1)S(1)}) fusion(bf16[32,32,128]{2,1,0:T(8,128)(2,1)} %bitcast.115, bf16[2,16,32,1]{2,1,0,3:T(8,128)(2,1)S(1)} %reshape.93), kind=kOutput, calls=%fused_computation.23 | convolution fusion | flops 8912896 | bytes 788480 | tf_op jit(solution)/shard_map/isx,xyk->isyk/dot_general | solution.py:19
  23.4 0.0 copy-done
  23.5 0.3 convolution_bitcast_fusion.3
  23.7 0.3 fusion.4
  24.0 0.9 %copy.48 = bf16[256,16,32]{2,1,0:T(8,128)(2,1)S(1)} copy(bf16[256,16,32]{0,2,1:T(8,128)(2,1)S(1)} %fusion.4) | data formatting | bytes 524288 | tf_op jit(solution)/shard_map/convert_element_type | solution.py:37
  25.0 0.8 reshape.87
  25.8 0.1 convert_reduce_fusion.2
  25.9 9.8 %all-to-all-done = bf16[128,2,512]{2,1,0:T(2,128)(2,1)S(1)} async-done(((bf16[128,2,512]{2,1,0:T(2,128)(2,1)}), bf16[128,2,512]{2,1,0:T(2,128)(2,1)S(1)}, u32[]{:S(2)}, u32[]{:S(2)}) %all-to-all-start) | async-done | bytes 262176 | tf_op jit(solution)/shard_map/all_to_all | solution.py:29
  35.6 0.5 reshape.84
  36.1 0.8 %copy.49 = bf16[256,16,32]{0,2,1:T(8,128)(2,1)S(1)} copy(bf16[256,16,32]{2,1,0:T(8,128)(2,1)S(1)} %reshape.84) | data formatting | bytes 524288 | tf_op jit(solution)/shard_map/reshape | solution.py:31
  37.0 0.2 reduce-precision_convert_fusion
  37.2 0.3 convolution_bitcast_fusion
  37.5 0.3 fusion.5
  37.8 0.1 copy.52
  37.9 0.1 reshape.88
  38.1 1.4 %pad_maximum_fusion = bf16[128,2,1152]{2,1,0:T(2,128)(2,1)} fusion(bf16[128,2,128]{2,1,0:T(2,128)(2,1)S(1)} %broadcast_in_dim.9, bf16[128,2,512]{2,1,0:T(2,128)(2,1)S(1)} %reshape.88, bf16[128,2,512]{2,1,0:T(2,128)(2,1)S(1)} %reshape.87), kind=kLoop, calls=%fused_computation.24 | loop fusion | flops 1769472 | bytes 1179648 | tf_op jit(solution)/shard_map/concatenate | solution.py:47
  39.4 6.4 %all-to-all-start.1 = ((bf16[128,2,1152]{2,1,0:T(2,128)(2,1)}), bf16[128,2,1152]{2,1,0:T(2,128)(2,1)S(1)}, u32[]{:S(2)}, u32[]{:S(2)}) async-start(bf16[128,2,1152]{2,1,0:T(2,128)(2,1)} %pad_maximum_fusion), calls=%async_computation.1 | async-start | bytes 1179648 | tf_op jit(solution)/shard_map/all_to_all | solution.py:46
  45.9 1.1 %copy.42 = bf16[256,16,32]{0,1,2:T(8,128)(2,1)S(1)} copy(bf16[256,16,32]{2,1,0:T(8,128)(2,1)S(1)} %reshape.84) | data formatting | bytes 524288 | tf_op jit(solution)/shard_map/reshape | solution.py:31
  46.9 0.3 convolution_bitcast_fusion.5
  47.2 0.0 copy-start.1
  47.2 0.3 fusion.7
  47.5 0.1 copy.44
  47.7 0.5 copy-done.1
  48.2 0.3 convolution_bitcast_fusion.7
  48.4 0.3 fusion.9
  48.7 0.7 reshape.91
  49.4 0.0 copy-start.2
  49.4 15.2 %all-to-all-done.1 = bf16[128,2,1152]{2,1,0:T(2,128)(2,1)S(1)} async-done(((bf16[128,2,1152]{2,1,0:T(2,128)(2,1)}), bf16[128,2,1152]{2,1,0:T(2,128)(2,1)S(1)}, u32[]{:S(2)}, u32[]{:S(2)}) %all-to-all-start.1) | async-done | bytes 589856 | tf_op jit(solution)/shard_map/all_to_all | solution.py:46
  64.7 0.5 convert_reduce_fusion
  65.2 0.6 slice_multiply_fusion
  65.8 0.7 pad_maximum_fusion.1
  66.5 8.6 %all-to-all-start.2 = ((bf16[4,144,128]{2,1,0:T(8,128)(2,1)}), bf16[4,144,128]{2,1,0:T(8,128)(2,1)S(1)}, u32[]{:S(2)}, u32[]{:S(2)}) async-start(bf16[4,144,128]{2,1,0:T(8,128)(2,1)} %pad_maximum_fusion.1), calls=%async_computation.2 | async-start | bytes 294912 | tf_op jit(solution)/shard_map/all_to_all | solution.py:70
  75.1 0.5 fusion.37
  75.6 4.7 %all-to-all-done.2 = bf16[4,144,128]{2,1,0:T(8,128)(2,1)S(1)} async-done(((bf16[4,144,128]{2,1,0:T(8,128)(2,1)}), bf16[4,144,128]{2,1,0:T(8,128)(2,1)S(1)}, u32[]{:S(2)}, u32[]{:S(2)}) %all-to-all-start.2) | async-done | bytes 147488 | tf_op jit(solution)/shard_map/all_to_all | solution.py:70
  80.4 0.6 slice_add_fusion.1
  81.0 0.0 copy-done.2
  81.0 0.6 add_convert_fusion
  (12 shorter events, 0.2 us)
Async XLA Ops:
  0.6 22.8 %copy-start = (bf16[2,256,128]{2,1,0:T(8,128)(2,1)S(1)}, bf16[2,256,128]{2,1,0:T(8,128)(2,1)}, u32[]{:S(2)}) copy-start(bf16[2,256,128]{2,1,0:T(8,128)(2,1)} %param.7) | copy-start | bytes 393220
  2.2 33.4 %all-to-all-start = ((bf16[128,2,512]{2,1,0:T(2,128)(2,1)}), bf16[128,2,512]{2,1,0:T(2,128)(2,1)S(1)}, u32[]{:S(2)}, u32[]{:S(2)}) async-start(bf16[128,2,512]{2,1,0:T(2,128)(2,1)} %broadcast_in_dim.8), calls=%async_computation | async-start | bytes 524288 | tf_op jit(solution)/shard_map/all_to_all | solution.py:29
  39.4 25.2 %all-to-all-start.1 = ((bf16[128,2,1152]{2,1,0:T(2,128)(2,1)}), bf16[128,2,1152]{2,1,0:T(2,128)(2,1)S(1)}, u32[]{:S(2)}, u32[]{:S(2)}) async-start(bf16[128,2,1152]{2,1,0:T(2,128)(2,1)} %pad_maximum_fusion), calls=%async_computation.1 | async-start | bytes 1179648 | tf_op jit(solution)/shard_map/all_to_all | solution.py:46
  47.2 1.0 %copy-start.1 = (bf16[1024,128]{1,0:T(8,128)(2,1)S(1)}, bf16[1024,128]{1,0:T(8,128)(2,1)}, u32[]{:S(2)}) copy-start(bf16[1024,128]{1,0:T(8,128)(2,1)} %param.8) | copy-start | bytes 786436
  49.4 31.6 %copy-start.2 = (f32[128]{0:T(128)S(1)}, f32[128]{0:T(128)}, u32[]{:S(2)}) copy-start(f32[128]{0:T(128)} %param.9) | copy-start | bytes 1540
  66.5 13.8 %all-to-all-start.2 = ((bf16[4,144,128]{2,1,0:T(8,128)(2,1)}), bf16[4,144,128]{2,1,0:T(8,128)(2,1)S(1)}, u32[]{:S(2)}, u32[]{:S(2)}) async-start(bf16[4,144,128]{2,1,0:T(8,128)(2,1)} %pad_maximum_fusion.1), calls=%async_computation.2 | async-start | bytes 294912 | tf_op jit(solution)/shard_map/all_to_all | solution.py:70

commit v3 on v2

--- a/solution.py
+++ b/solution.py
@@ -43,39 +43,34 @@
     rows = C * C // res
     grad_weight = grad_weight.astype(jnp.bfloat16).reshape(res, ROW_DEV, rows * P_SIZE // ROW_DEV)
 
-    parts = lax.all_to_all(
-        jnp.concatenate([grad_right, grad_weight, bias_pair], axis=2), "res", 0, 0, tiled=True
-    )
+    message = jnp.concatenate([grad_right, grad_weight, bias_pair], axis=2)
+    message, right_all = lax.optimization_barrier((message, right_all))
+    parts = lax.all_to_all(message, "res", 0, 0, tiled=True)
 
     grad_left = dot32("isyk,xyk->isx", back_hi, weight) + dot32("isyk,xyk->isx", back_lo, weight)
     pair = dot32("jsy,isyk->ijk", right_all, mixed_hi) + dot32("jsy,isyk->ijk", right_all, mixed_lo)
     cols = pair.shape[1] // seq
-    pair = jnp.moveaxis(pair.reshape(ROW_DEV, seq, cols, P_SIZE), 1, 0).reshape(seq, ROW_DEV * cols, P_SIZE)
-    pair_sent, pair_rest = hi_lo(pair)
-    pair_rest = lax.dynamic_index_in_dim(pair_rest, lax.axis_index("seq"), 0, keepdims=False)
+    here = lax.axis_index("seq")
+
+    def columns_of(owner):
+        return lax.dynamic_slice_in_dim(pair, owner * cols, cols, 1)
+
+    pair_sum = columns_of(here)
+    for step in range(1, seq):
+        sent = columns_of(lax.rem(here + step, seq))
+        pair_sum = pair_sum + lax.ppermute(sent, "seq", [(q, (q + step) % seq) for q in range(seq)])
+    pair_update = (pair_sum * scale + out_bias).astype(jnp.bfloat16)
 
     totals = jnp.sum(parts, axis=0, dtype=jnp.float32)
-    grad_right = totals[:, :WIDE] * scale
-    weight_hi, weight_lo = hi_lo(totals[:, WIDE : WIDE + rows * P_SIZE // ROW_DEV].reshape(rows, P_SIZE))
-    grad_bias = totals[0, -P_SIZE:] + totals[1, -P_SIZE:]
+    weight_sum = totals[:, WIDE : WIDE + rows * P_SIZE // ROW_DEV].reshape(rows, P_SIZE)
 
-    last = jnp.concatenate(
-        [
-            pair_sent,
-            jnp.broadcast_to(weight_hi[None], (seq, rows, P_SIZE)),
-            jnp.broadcast_to(weight_lo[None], (seq, rows, P_SIZE)),
-        ],
-        axis=1,
-    )
-    summed = jnp.sum(lax.all_to_all(last, "seq", 0, 0, tiled=True), axis=0, dtype=jnp.float32) * scale
-    split = ROW_DEV * cols
-    pair_update = (summed[:split] + pair_rest * scale).reshape(ROW_DEV, cols, P_SIZE) + out_bias
+    last = lax.all_to_all(jnp.broadcast_to(weight_sum[None], (seq, rows, P_SIZE)), "seq", 0, 0, tiled=True)
     return (
-        pair_update.astype(jnp.bfloat16),
+        pair_update,
         (grad_left * scale).reshape(ROW_DEV, WIDE),
-        grad_right,
-        summed[split : split + rows] + summed[split + rows :],
-        grad_bias,
+        totals[:, :WIDE] * scale,
+        jnp.sum(last, axis=0) * scale,
+        totals[0, -P_SIZE:] + totals[1, -P_SIZE:],
     )
 
 

time: 82.1 us -> 80.7 us (0.983)
  waiting for transfers between devices: 29.7 us -> 20.2 us
  starting transfers between devices: 34.3 us -> 42.8 us
  other arithmetic: 5.08 us -> 3.83 us
    all_to_all x2, waiting for transfers between devices: 20 us -> 4.12 us  [the longest x1 4.12 us: on_device(): lax.all_to_all(jnp.broadcast_to(weight_sum[None], (seq, rows, P_SIZE)), '...]
    ppermute x0 -> x3, starting transfers between devices: none -> 11.1 us  [on_device(): lax.ppermute(sent, 'seq', [(q, (q + step) % seq) for q in range(seq)])]
    ppermute x0 -> x3, waiting for transfers between devices: none -> 6.37 us  [on_device(): lax.ppermute(sent, 'seq', [(q, (q + step) % seq) for q in range(seq)])]
    all_to_all x2, starting transfers between devices: 15 us -> 12.4 us  [the longest x1 6.42 us: on_device(): parts = lax.all_to_all(message, 'res', 0, 0, tiled=True)]
    reshape x3 -> x2, local copies, waits for them, and re-layouts: 2.42 us -> 1.34 us  [on_device(): right_all = lax.all_to_all(jnp.broadcast_to(right_proj[None], (res, ROW_D...]
    optimization_barrier x0 -> x1, local copies, waits for them, and re-layouts: none -> 1.08 us  [on_device(): message, right_all = lax.optimization_barrier((message, right_all))]
    concatenate x2 -> x1, other arithmetic: 2.04 us -> 1.37 us  [on_device(): message = jnp.concatenate([grad_right, grad_weight, bias_pair], axis=2)]
  transfers between devices with their start and end apart: 3 -> 6, of which waited for: 3 -> 4; matrix products, arithmetic and copies ran while one was open for 10% -> 11% of each run, Pallas kernels for 0% -> 0%
where the time goes in v3:
time: 80.7 us; the launch traced here: 80.3 us
  starting transfers between devices  42.8 us (53%)
  waiting for transfers between devices  20.2 us (25%)
  local copies, waits for them, and re-layouts  8.93 us (11%)
  other arithmetic  3.83 us (5%)
  matrix products  3.57 us (4%)
  between operations  0.86 us (1%)
    all_to_all x1, starting transfers between devices, on_device(): lax.all_to_all(jnp.broadcast_to(right_proj[None], (res, ROW_DEV, WIDE)),...  19.3 us
    ppermute x3, starting transfers between devices, on_device(): lax.ppermute(sent, 'seq', [(q, (q + step) % seq) for q in range(seq)])  11.1 us
    all_to_all x1, waiting for transfers between devices, on_device(): lax.all_to_all(jnp.broadcast_to(right_proj[None], (res, ROW_DEV, WIDE)),...  9.76 us
    all_to_all x1, starting transfers between devices, on_device(): parts = lax.all_to_all(message, 'res', 0, 0, tiled=True)  6.42 us
    ppermute x3, waiting for transfers between devices, on_device(): lax.ppermute(sent, 'seq', [(q, (q + step) % seq) for q in range(seq)])  6.37 us
    all_to_all x1, starting transfers between devices, on_device(): lax.all_to_all(jnp.broadcast_to(weight_sum[None], (seq, rows, P_SIZE)), '...  6.02 us
    all_to_all x1, waiting for transfers between devices, on_device(): lax.all_to_all(jnp.broadcast_to(weight_sum[None], (seq, rows, P_SIZE)), '...  4.12 us
    dot_general x10, matrix products, dot32(): return jnp.einsum(form, a, b, preferred_element_type=jnp.float32)  3.57 us
  transfers between devices with their start and end apart: 6, of which 4 were waited for; matrix products, arithmetic and copies ran while one was open for 11% of the time, Pallas kernels for 0%

profile of v3, /device:TPU:1, one launch (start us, length us, event | category | flops | bytes accessed | tf_op | source)
XLA Modules:
  0.0 80.3 jit_solution(69587946183028671)
XLA Ops:
  0.6 0.0 copy-start
  0.6 1.5 %broadcast_in_dim.8 = bf16[128,2,512]{2,1,0:T(2,128)(2,1)} broadcast(bf16[2,512]{1,0:T(2,128)(2,1)} %param.6), dimensions={1,2} | broadcast | bytes 264192 | tf_op jit(solution)/shard_map/broadcast_in_dim | solution.py:30
  2.2 19.3 %all-to-all-start = ((bf16[128,2,512]{2,1,0:T(2,128)(2,1)}), bf16[128,2,512]{2,1,0:T(2,128)(2,1)S(1)}, u32[]{:S(2)}, u32[]{:S(2)}) async-start(bf16[128,2,512]{2,1,0:T(2,128)(2,1)} %broadcast_in_dim.8), calls=%async_computation | async-start | bytes 524288 | tf_op jit(solution)/shard_map/all_to_all | solution.py:29
  21.5 0.8 reshape.59
  22.2 1.2 %reduce-precision_convert_fusion.1 = (bf16[2,16,32,128]{3,1,2,0:T(8,128)(2,1)S(1)}, bf16[2,16,32,128]{3,1,2,0:T(8,128)(2,1)S(1)}) fusion(bf16[32,32,128]{2,1,0:T(8,128)(2,1)} %bitcast.114, bf16[2,16,32,1]{2,1,0,3:T(8,128)(2,1)S(1)} %reshape.59), kind=kOutput, calls=%fused_computation.22 | convolution fusion | flops 8912896 | bytes 788480 | tf_op jit(solution)/shard_map/isx,xyk->isyk/dot_general | solution.py:19
  23.4 0.0 copy-done
  23.4 0.3 convolution_bitcast_fusion.3
  23.7 0.3 fusion.4
  24.0 0.9 %copy.44 = bf16[256,16,32]{2,1,0:T(8,128)(2,1)S(1)} copy(bf16[256,16,32]{0,2,1:T(8,128)(2,1)S(1)} %fusion.4) | data formatting | bytes 524288 | tf_op jit(solution)/shard_map/convert_element_type | solution.py:37
  24.9 0.8 %reshape.55 = bf16[128,2,512]{2,1,0:T(2,128)(2,1)S(1)} reshape(bf16[256,16,32]{2,1,0:T(8,128)(2,1)S(1)} %copy.44) | data formatting | bytes 524288 | tf_op jit(solution)/shard_map/reshape | solution.py:37
  25.8 0.1 convert_reduce_fusion.1
  25.9 9.8 %all-to-all-done = bf16[128,2,512]{2,1,0:T(2,128)(2,1)S(1)} async-done(((bf16[128,2,512]{2,1,0:T(2,128)(2,1)}), bf16[128,2,512]{2,1,0:T(2,128)(2,1)S(1)}, u32[]{:S(2)}, u32[]{:S(2)}) %all-to-all-start) | async-done | bytes 262176 | tf_op jit(solution)/shard_map/all_to_all | solution.py:29
  35.6 0.5 reshape.56
  36.1 0.8 %copy.45 = bf16[256,16,32]{0,2,1:T(8,128)(2,1)S(1)} copy(bf16[256,16,32]{2,1,0:T(8,128)(2,1)S(1)} %reshape.56) | data formatting | bytes 524288 | tf_op jit(solution)/shard_map/reshape | solution.py:31
  37.0 0.2 reduce-precision_convert_fusion
  37.2 0.3 convolution_bitcast_fusion
  37.5 0.3 fusion.5
  37.8 0.1 copy.48
  37.9 0.1 reshape.57
  38.1 1.4 %pad_maximum_fusion = bf16[128,2,1152]{2,1,0:T(2,128)(2,1)} fusion(bf16[128,2,128]{2,1,0:T(2,128)(2,1)S(1)} %broadcast_in_dim.9, bf16[128,2,512]{2,1,0:T(2,128)(2,1)S(1)} %reshape.57, bf16[128,2,512]{2,1,0:T(2,128)(2,1)S(1)} %reshape.55), kind=kLoop, calls=%fused_computation.23 | loop fusion | flops 1769472 | bytes 1179648 | tf_op jit(solution)/shard_map/concatenate | solution.py:46
  39.4 6.4 %all-to-all-start.1 = ((bf16[128,2,1152]{2,1,0:T(2,128)(2,1)}), bf16[128,2,1152]{2,1,0:T(2,128)(2,1)S(1)}, u32[]{:S(2)}, u32[]{:S(2)}) async-start(bf16[128,2,1152]{2,1,0:T(2,128)(2,1)} %pad_maximum_fusion), calls=%async_computation.1 | async-start | bytes 1179648 | tf_op jit(solution)/shard_map/all_to_all | solution.py:48
  45.9 1.1 %copy.49 = bf16[256,16,32]{0,1,2:T(8,128)(2,1)S(1)} copy(bf16[256,16,32]{2,1,0:T(8,128)(2,1)S(1)} %reshape.56) | data formatting | bytes 524288 | tf_op jit(solution)/shard_map/optimization_barrier | solution.py:47
  47.0 0.3 convolution_bitcast_fusion.5
  47.2 0.0 copy-start.1
  47.2 0.3 fusion.6
  47.5 0.0 copy-start.2
  47.5 0.2 dynamic-slice_bitcast_fusion.2
  47.7 6.7 %collective-permute-start = (f32[2,64,128]{1,2,0:T(8,128)S(1)}, f32[2,64,128]{1,2,0:T(8,128)S(1)}, u32[]{:S(2)}, u32[]{:S(2)}) collective-permute-start(f32[2,64,128]{1,2,0:T(8,128)S(1)} %get-tuple-element.28), channel_id=1, source_target_pairs={{0,1},{1,2},{2,3},{3,0},{4,5},{5,6},{6,7},{7,4},{8,9},{9,10},{10,1... | collective-permute-start | bytes 196616 | tf_op jit(solution)/shard_map/ppermute | solution.py:61
  54.5 1.9 %collective-permute-start.2 = (f32[2,64,128]{1,2,0:T(8,128)S(1)}, f32[2,64,128]{1,2,0:T(8,128)S(1)}, u32[]{:S(2)}, u32[]{:S(2)}) collective-permute-start(f32[2,64,128]{1,2,0:T(8,128)S(1)} %get-tuple-element.29), channel_id=1, source_target_pairs={{0,3},{1,0},{2,1},{3,2},{4,7},{5,4},{6,5},{7,6},{8,11},{9,8},{10,9... | collective-permute-start | bytes 196616 | tf_op jit(solution)/shard_map/ppermute | solution.py:61
  56.4 2.4 %collective-permute-start.1 = (f32[2,64,128]{1,2,0:T(8,128)S(1)}, f32[2,64,128]{1,2,0:T(8,128)S(1)}, u32[]{:S(2)}, u32[]{:S(2)}) collective-permute-start(f32[2,64,128]{1,2,0:T(8,128)S(1)} %get-tuple-element.30), channel_id=1, source_target_pairs={{0,2},{1,3},{2,0},{3,1},{4,6},{5,7},{6,4},{7,5},{8,10},{9,11},{10,... | collective-permute-start | bytes 196616 | tf_op jit(solution)/shard_map/ppermute | solution.py:61
  58.8 0.0 copy-done.1
  58.8 0.3 convolution_bitcast_fusion.7
  59.1 0.3 fusion.8
  59.4 0.7 reshape.58
  60.0 0.0 collective-permute-done
  60.1 4.4 %collective-permute-done.2 = f32[2,64,128]{1,2,0:T(8,128)S(1)} collective-permute-done((f32[2,64,128]{1,2,0:T(8,128)S(1)}, f32[2,64,128]{1,2,0:T(8,128)S(1)}, u32[]{:S(2)}, u32[]{:S(2)}) %collective-permute-start.2) | collective-permute-done | bytes 65568 | tf_op jit(solution)/shard_map/ppermute | solution.py:61
  64.4 2.0 %collective-permute-done.1 = f32[2,64,128]{1,2,0:T(8,128)S(1)} collective-permute-done((f32[2,64,128]{1,2,0:T(8,128)S(1)}, f32[2,64,128]{1,2,0:T(8,128)S(1)}, u32[]{:S(2)}, u32[]{:S(2)}) %collective-permute-start.1) | collective-permute-done | bytes 65568 | tf_op jit(solution)/shard_map/ppermute | solution.py:61
  66.4 0.0 copy-done.2
  66.4 0.1 fusion.32
  66.5 0.7 copy.55
  67.3 0.0 all-to-all-done.1
  67.3 0.5 convert_reduce_fusion
  67.8 0.6 fusion.38
  68.4 0.6 broadcast_in_dim.11
  69.0 6.0 %all-to-all-start.2 = ((f32[4,8,128]{2,1,0:T(8,128)}), f32[4,8,128]{2,1,0:T(8,128)S(1)}, u32[]{:S(2)}, u32[]{:S(2)}) async-start(f32[4,8,128]{2,1,0:T(8,128)} %broadcast_in_dim.11), calls=%async_computation.2 | async-start | bytes 32768 | tf_op jit(solution)/shard_map/all_to_all | solution.py:67
  75.0 0.5 fusion.37
  75.5 4.1 %all-to-all-done.2 = f32[4,8,128]{2,1,0:T(8,128)S(1)} async-done(((f32[4,8,128]{2,1,0:T(8,128)}), f32[4,8,128]{2,1,0:T(8,128)S(1)}, u32[]{:S(2)}, u32[]{:S(2)}) %all-to-all-start.2) | async-done | bytes 16416 | tf_op jit(solution)/shard_map/all_to_all | solution.py:67
  79.7 0.6 broadcast_multiply_fusion
  (5 shorter events, 0.1 us)
Async XLA Ops:
  0.6 22.8 %copy-start = (bf16[2,256,128]{2,1,0:T(8,128)(2,1)S(1)}, bf16[2,256,128]{2,1,0:T(8,128)(2,1)}, u32[]{:S(2)}) copy-start(bf16[2,256,128]{2,1,0:T(8,128)(2,1)} %param.7) | copy-start | bytes 393220
  2.2 33.4 %all-to-all-start = ((bf16[128,2,512]{2,1,0:T(2,128)(2,1)}), bf16[128,2,512]{2,1,0:T(2,128)(2,1)S(1)}, u32[]{:S(2)}, u32[]{:S(2)}) async-start(bf16[128,2,512]{2,1,0:T(2,128)(2,1)} %broadcast_in_dim.8), calls=%async_computation | async-start | bytes 524288 | tf_op jit(solution)/shard_map/all_to_all | solution.py:29
  39.4 27.8 %all-to-all-start.1 = ((bf16[128,2,1152]{2,1,0:T(2,128)(2,1)}), bf16[128,2,1152]{2,1,0:T(2,128)(2,1)S(1)}, u32[]{:S(2)}, u32[]{:S(2)}) async-start(bf16[128,2,1152]{2,1,0:T(2,128)(2,1)} %pad_maximum_fusion), calls=%async_computation.1 | async-start | bytes 1179648 | tf_op jit(solution)/shard_map/all_to_all | solution.py:48
  47.2 11.6 %copy-start.1 = (bf16[1024,128]{1,0:T(8,128)(2,1)S(1)}, bf16[1024,128]{1,0:T(8,128)(2,1)}, u32[]{:S(2)}) copy-start(bf16[1024,128]{1,0:T(8,128)(2,1)} %param.8) | copy-start | bytes 786436
  47.5 18.9 %copy-start.2 = (f32[128]{0:T(128)S(1)}, f32[128]{0:T(128)}, u32[]{:S(2)}) copy-start(f32[128]{0:T(128)} %param.9) | copy-start | bytes 1540
  47.7 12.3 %collective-permute-start = (f32[2,64,128]{1,2,0:T(8,128)S(1)}, f32[2,64,128]{1,2,0:T(8,128)S(1)}, u32[]{:S(2)}, u32[]{:S(2)}) collective-permute-start(f32[2,64,128]{1,2,0:T(8,128)S(1)} %get-tuple-element.28), channel_id=1, source_target_pairs={{0,1},{1,2},{2,3},{3,0},{4,5},{5,6},{6,7},{7,4},{8,9},{9,10},{10,1... | collective-permute-start | bytes 196616 | tf_op jit(solution)/shard_map/ppermute | solution.py:61
  54.5 10.0 %collective-permute-start.2 = (f32[2,64,128]{1,2,0:T(8,128)S(1)}, f32[2,64,128]{1,2,0:T(8,128)S(1)}, u32[]{:S(2)}, u32[]{:S(2)}) collective-permute-start(f32[2,64,128]{1,2,0:T(8,128)S(1)} %get-tuple-element.29), channel_id=1, source_target_pairs={{0,3},{1,0},{2,1},{3,2},{4,7},{5,4},{6,5},{7,6},{8,11},{9,8},{10,9... | collective-permute-start | bytes 196616 | tf_op jit(solution)/shard_map/ppermute | solution.py:61
  56.4 10.0 %collective-permute-start.1 = (f32[2,64,128]{1,2,0:T(8,128)S(1)}, f32[2,64,128]{1,2,0:T(8,128)S(1)}, u32[]{:S(2)}, u32[]{:S(2)}) collective-permute-start(f32[2,64,128]{1,2,0:T(8,128)S(1)} %get-tuple-element.30), channel_id=1, source_target_pairs={{0,2},{1,3},{2,0},{3,1},{4,6},{5,7},{6,4},{7,5},{8,10},{9,11},{10,... | collective-permute-start | bytes 196616 | tf_op jit(solution)/shard_map/ppermute | solution.py:61
  69.0 10.7 %all-to-all-start.2 = ((f32[4,8,128]{2,1,0:T(8,128)}), f32[4,8,128]{2,1,0:T(8,128)S(1)}, u32[]{:S(2)}, u32[]{:S(2)}) async-start(f32[4,8,128]{2,1,0:T(8,128)} %broadcast_in_dim.11), calls=%async_computation.2 | async-start | bytes 32768 | tf_op jit(solution)/shard_map/all_to_all | solution.py:67

commit v4 on v3

--- a/solution.py
+++ b/solution.py
@@ -1,6 +1,8 @@
 import jax
 import jax.numpy as jnp
 from jax import lax
+from jax.experimental import pallas as pl
+from jax.experimental.pallas import tpu as pltpu
 from jax.sharding import PartitionSpec as P
 
 C = 32
@@ -19,6 +21,52 @@
     return jnp.einsum(form, a, b, preferred_element_type=jnp.float32)
 
 
+def products_kernel(right, cotan, mixed_hi, mixed_lo, left_cols, pair, weight_out, back_hi, back_lo, back, weight_sum):
+    rows = right[...]
+    both = jnp.concatenate([cotan[0], cotan[1]], axis=1)
+    terms = lax.dot_general(rows, both, (((0,), (0,)), ((), ())), preferred_element_type=jnp.float32)
+    back[0] = terms[:, :P_SIZE]
+    back[1] = terms[:, P_SIZE:]
+    lhs = left_cols[...]
+    for y in range(C):
+        parts = []
+        for i in range(ROW_DEV):
+            term = back[i, pl.ds(y, SEQ_DEV, stride=C), :]
+            high = term.astype(jnp.bfloat16)
+            parts += [high, (term - high.astype(jnp.float32)).astype(jnp.bfloat16)]
+        weight_sum[pl.ds(y, C, stride=C), :] = jnp.dot(
+            lhs, jnp.concatenate(parts, axis=0), preferred_element_type=jnp.float32
+        )
+    weight_out[...] = weight_sum[...].astype(jnp.bfloat16)
+    for i in range(ROW_DEV):
+        pair[i] = jnp.dot(rows, mixed_hi[i], preferred_element_type=jnp.float32) + jnp.dot(
+            rows, mixed_lo[i], preferred_element_type=jnp.float32
+        )
+        term = back[i]
+        high = term.astype(jnp.bfloat16)
+        back_hi[i] = high
+        back_lo[i] = (term - high.astype(jnp.float32)).astype(jnp.bfloat16)
+
+
+def products(right, cotan, mixed_hi, mixed_lo, left_cols):
+    whole = pl.BlockSpec(memory_space=pltpu.VMEM)
+    back = (ROW_DEV, WIDE, P_SIZE)
+    return pl.pallas_call(
+        products_kernel,
+        out_shape=(
+            jax.ShapeDtypeStruct((ROW_DEV, right.shape[0], P_SIZE), jnp.float32),
+            jax.ShapeDtypeStruct((C * C, P_SIZE), jnp.bfloat16),
+            jax.ShapeDtypeStruct(back, jnp.bfloat16),
+            jax.ShapeDtypeStruct(back, jnp.bfloat16),
+        ),
+        in_specs=[whole] * 5,
+        out_specs=(whole,) * 4,
+        scratch_shapes=[pltpu.VMEM(back, jnp.float32), pltpu.VMEM((C * C, P_SIZE), jnp.float32)],
+        compiler_params=pltpu.CompilerParams(vmem_limit_bytes=16 * 1024 * 1024),
+        cost_estimate=pl.CostEstimate(flops=300_000_000, bytes_accessed=3_000_000, transcendentals=0),
+    )(right, cotan, mixed_hi, mixed_lo, left_cols)
+
+
 def on_device(left_proj, right_proj, pair_cotangent, out_weight, out_bias):
     res = lax.axis_size("res")
     seq = lax.axis_size("seq")
@@ -28,7 +76,7 @@
 
     right_all = lax.all_to_all(
         jnp.broadcast_to(right_proj[None], (res, ROW_DEV, WIDE)), "res", 0, 0, tiled=True
-    ).reshape(res * ROW_DEV, SEQ_DEV, C)
+    ).reshape(res * ROW_DEV, WIDE)
 
     mixed_hi, mixed_lo = hi_lo(dot32("isx,xyk->isyk", left_rows, weight))
     grad_right = dot32("ijk,isyk->jsy", pair_cotangent, mixed_hi) + dot32(
@@ -37,18 +85,22 @@
     grad_right = grad_right.astype(jnp.bfloat16).reshape(res, ROW_DEV, WIDE)
     bias_pair = jnp.stack(hi_lo(jnp.sum(pair_cotangent, axis=(0, 1), dtype=jnp.float32)))
     bias_pair = jnp.broadcast_to(bias_pair[None], (res, 2, P_SIZE))
+    rows = C * C // res
+    blank = jnp.zeros((res, ROW_DEV, rows * P_SIZE // ROW_DEV), jnp.bfloat16)
+    body = lax.optimization_barrier(jnp.concatenate([blank, grad_right, bias_pair], axis=2))
+    left_cols = jnp.broadcast_to(left_rows.transpose(2, 0, 1)[:, :, None], (C, ROW_DEV, 2, SEQ_DEV))
+    left_cols = left_cols.reshape(C, ROW_DEV * 2 * SEQ_DEV)
+    mixed = (ROW_DEV, WIDE, P_SIZE)
 
-    back_hi, back_lo = hi_lo(dot32("jsy,ijk->isyk", right_all, pair_cotangent))
-    grad_weight = dot32("isx,isyk->xyk", left_rows, back_hi) + dot32("isx,isyk->xyk", left_rows, back_lo)
-    rows = C * C // res
-    grad_weight = grad_weight.astype(jnp.bfloat16).reshape(res, ROW_DEV, rows * P_SIZE // ROW_DEV)
+    pair, grad_weight, back_hi, back_lo = products(
+        right_all, pair_cotangent, mixed_hi.reshape(mixed), mixed_lo.reshape(mixed), left_cols
+    )
 
-    message = jnp.concatenate([grad_right, grad_weight, bias_pair], axis=2)
-    message, right_all = lax.optimization_barrier((message, right_all))
-    parts = lax.all_to_all(message, "res", 0, 0, tiled=True)
+    grad_weight = grad_weight.reshape(blank.shape)
+    parts = lax.all_to_all(lax.dynamic_update_slice(body, grad_weight, (0, 0, 0)), "res", 0, 0, tiled=True)
 
+    back_hi, back_lo = (term.reshape(ROW_DEV, SEQ_DEV, C, P_SIZE) for term in (back_hi, back_lo))
     grad_left = dot32("isyk,xyk->isx", back_hi, weight) + dot32("isyk,xyk->isx", back_lo, weight)
-    pair = dot32("jsy,isyk->ijk", right_all, mixed_hi) + dot32("jsy,isyk->ijk", right_all, mixed_lo)
     cols = pair.shape[1] // seq
     here = lax.axis_index("seq")
 
@@ -62,13 +114,13 @@
     pair_update = (pair_sum * scale + out_bias).astype(jnp.bfloat16)
 
     totals = jnp.sum(parts, axis=0, dtype=jnp.float32)
-    weight_sum = totals[:, WIDE : WIDE + rows * P_SIZE // ROW_DEV].reshape(rows, P_SIZE)
+    weight_sum = totals[:, : rows * P_SIZE // ROW_DEV].reshape(rows, P_SIZE)
 
     last = lax.all_to_all(jnp.broadcast_to(weight_sum[None], (seq, rows, P_SIZE)), "seq", 0, 0, tiled=True)
     return (
         pair_update,
         (grad_left * scale).reshape(ROW_DEV, WIDE),
-        totals[:, :WIDE] * scale,
+        totals[:, rows * P_SIZE // ROW_DEV : -P_SIZE] * scale,
         jnp.sum(last, axis=0) * scale,
         totals[0, -P_SIZE:] + totals[1, -P_SIZE:],
     )

time: 80.7 us -> 79.4 us (0.984)
  starting transfers between devices: 42.8 us -> 45.4 us
  waiting for transfers between devices: 20.2 us -> 17.9 us
  matrix products: 3.57 us -> 1.29 us
  local copies, waits for them, and re-layouts: 8.93 us -> 7 us
  Pallas kernels: 0 us -> 1.37 us
  other arithmetic: 3.83 us -> 5.2 us
    ppermute x3, waiting for transfers between devices: 6.37 us -> 3.76 us  [on_device(): lax.ppermute(sent, 'seq', [(q, (q + step) % seq) for q in range(seq)])]
    all_to_all x1, starting transfers between devices: 6.02 us -> 8.61 us  [on_device(): lax.all_to_all(jnp.broadcast_to(weight_sum[None], (seq, rows, P_SIZE)), '...]
    dot_general x10 -> x5, matrix products: 3.57 us -> 1.29 us  [dot32(): return jnp.einsum(form, a, b, preferred_element_type=jnp.float32)]
    all_to_all x1, waiting for transfers between devices: 0.01 us -> 2.02 us  [on_device(): lax.all_to_all(lax.dynamic_update_slice(body, grad_weight, (0, 0, 0)), 'r...]
    all_to_all x1, waiting for transfers between devices: 9.76 us -> 7.95 us  [on_device(): lax.all_to_all(jnp.broadcast_to(right_proj[None], (res, ROW_DEV, WIDE)),...]
    pallas_call x0 -> x1, Pallas kernels: none -> 1.37 us  [products(): pl.pallas_call(products_kernel, out_shape=(jax.ShapeDtypeStruct((ROW_DEV,...]
    reshape x2 -> x1, local copies, waits for them, and re-layouts: 1.34 us -> 0.1 us  [on_device(): right_all = lax.all_to_all(jnp.broadcast_to(right_proj[None], (res, ROW_D...]
    optimization_barrier x1 -> x0, local copies, waits for them, and re-layouts: 1.08 us -> none  [on_device(): message, right_all = lax.optimization_barrier((message, right_all))]
  transfers between devices with their start and end apart: 6 -> 6, of which waited for: 4 -> 5; matrix products, arithmetic and copies ran while one was open for 11% -> 11% of each run, Pallas kernels for 0% -> 0%
where the time goes in v4:
time: 79.4 us; the launch traced here: 79 us
  starting transfers between devices  45.4 us (57%)
  waiting for transfers between devices  17.9 us (23%)
  local copies, waits for them, and re-layouts  7 us (9%)
  other arithmetic  5.2 us (7%)
  Pallas kernels  1.37 us (2%)
  matrix products  1.29 us (2%)
  between operations  0.85 us (1%)
    all_to_all x1, starting transfers between devices, on_device(): lax.all_to_all(jnp.broadcast_to(right_proj[None], (res, ROW_DEV, WIDE)),...  19.3 us
    ppermute x3, starting transfers between devices, on_device(): lax.ppermute(sent, 'seq', [(q, (q + step) % seq) for q in range(seq)])  11.1 us
    all_to_all x1, starting transfers between devices, on_device(): lax.all_to_all(jnp.broadcast_to(weight_sum[None], (seq, rows, P_SIZE)), '...  8.61 us
    all_to_all x1, waiting for transfers between devices, on_device(): lax.all_to_all(jnp.broadcast_to(right_proj[None], (res, ROW_DEV, WIDE)),...  7.95 us
    all_to_all x1, starting transfers between devices, on_device(): lax.all_to_all(lax.dynamic_update_slice(body, grad_weight, (0, 0, 0)), 'r...  6.42 us
    all_to_all x1, waiting for transfers between devices, on_device(): lax.all_to_all(jnp.broadcast_to(weight_sum[None], (seq, rows, P_SIZE)), '...  4.12 us
    ppermute x3, waiting for transfers between devices, on_device(): lax.ppermute(sent, 'seq', [(q, (q + step) % seq) for q in range(seq)])  3.76 us
    all_to_all x1, waiting for transfers between devices, on_device(): lax.all_to_all(lax.dynamic_update_slice(body, grad_weight, (0, 0, 0)), 'r...  2.02 us
  transfers between devices with their start and end apart: 6, of which 5 were waited for; matrix products, arithmetic and copies ran while one was open for 11% of the time, Pallas kernels for 0%

profile of v4, /device:TPU:1, one launch (start us, length us, event | category | flops | bytes accessed | tf_op | source)
XLA Modules:
  0.0 79.0 jit_solution(14806984197329639117)
XLA Ops:
  0.6 0.0 copy-start
  0.6 0.0 copy-start.1
  0.7 1.6 %broadcast_in_dim.12 = bf16[128,2,512]{2,1,0:T(2,128)(2,1)} broadcast(bf16[2,512]{1,0:T(2,128)(2,1)} %param.6), dimensions={1,2} | broadcast | bytes 264192 | tf_op jit(solution)/shard_map/broadcast_in_dim | solution.py:78
  2.2 19.3 %all-to-all-start = ((bf16[128,2,512]{2,1,0:T(2,128)(2,1)}), bf16[128,2,512]{2,1,0:T(2,128)(2,1)S(1)}, u32[]{:S(2)}, u32[]{:S(2)}) async-start(bf16[128,2,512]{2,1,0:T(2,128)(2,1)} %broadcast_in_dim.12), calls=%async_computation | async-start | bytes 524288 | tf_op jit(solution)/shard_map/all_to_all | solution.py:77
  21.5 1.0 %convert_reduce_fusion.1 = f32[128]{0:T(128)S(1)} fusion(bf16[2,256,128]{2,1,0:T(8,128)(2,1)} %cotan.1), kind=kLoop, calls=%fused_computation.22 | loop fusion | flops 130944 | bytes 131584 | tf_op jit(solution)/shard_map/reduce_sum | solution.py:86
  22.5 0.8 reshape.80
  23.3 0.0 copy-done.1
  23.3 0.2 fusion.5
  23.5 0.0 copy-done
  23.5 0.0 copy-start.2
  23.5 0.3 convolution_bitcast_fusion
  23.8 0.3 fusion.2
  24.1 0.1 copy-done.2
  24.2 0.1 reshape.70
  24.3 0.1 copy.35
  24.4 0.1 copy.34
  24.5 0.1 copy.36.left_cols
  24.5 1.0 %copy.43 = bf16[256,16,32]{2,1,0:T(8,128)(2,1)S(1)} copy(bf16[256,16,32]{0,2,1:T(8,128)(2,1)S(1)} %fusion.2) | data formatting | bytes 524288 | tf_op jit(solution)/shard_map/convert_element_type | solution.py:85
  25.5 0.8 %reshape.78 = bf16[128,2,512]{2,1,0:T(2,128)(2,1)S(1)} reshape(bf16[256,16,32]{2,1,0:T(8,128)(2,1)S(1)} %copy.43) | data formatting | bytes 524288 | tf_op jit(solution)/shard_map/reshape | solution.py:85
  26.4 1.3 %pad_maximum_fusion = bf16[128,2,1152]{2,1,0:T(2,128)(2,1)} fusion(bf16[128,2,128]{2,1,0:T(2,128)(2,1)S(1)} %broadcast_in_dim.15, bf16[128,2,512]{2,1,0:T(2,128)(2,1)S(1)} %reshape.78, bf16[1152]{0:T(1024)(128)(2,1)S(1)} %pad.clone), kind=kLoop, calls=%fused_computation.12 | loop fusion | flops 1769472 | bytes 919808 | tf_op jit(solution)/shard_map/concatenate | solution.py:90
  27.7 7.9 %all-to-all-done = bf16[128,2,512]{2,1,0:T(2,128)(2,1)S(1)} async-done(((bf16[128,2,512]{2,1,0:T(2,128)(2,1)}), bf16[128,2,512]{2,1,0:T(2,128)(2,1)S(1)}, u32[]{:S(2)}, u32[]{:S(2)}) %all-to-all-start) | async-done | bytes 262176 | tf_op jit(solution)/shard_map/all_to_all | solution.py:77
  35.7 0.1 reshape.69.right
  35.8 1.4 %shard_map.92 = (f32[2,256,128]{2,1,0:T(8,128)S(1)}, bf16[1024,128]{1,0:T(8,128)(2,1)S(1)}, bf16[2,512,128]{2,1,0:T(8,128)(2,1)S(1)}, bf16[2,512,128]{2,1,0:T(8,128)(2,1)S(1)}) custom-call(bf16[256,512]{1,0:T(8,128)(2,1)S(1)} %reshape.69.right, bf16[2,256,128]{2,1,0:T(8,128)(2,1)S(1)} %copy-done, bf16[2,512,128]{2,1,0:T(8,128)(2,1)S(1)} %bitcast.58, ...), custom_call_target="tpu_custom_call" | custom-call | flops 300000000 | bytes 3000000 | tf_op jit(solution)/shard_map/pallas_call | solution.py:54
  37.1 0.1 reshape.79
  37.2 0.9 %constant_dynamic-update-slice_fusion = bf16[128,2,1152]{2,1,0:T(2,128)(2,1)} fusion(bf16[128,2,1152]{2,1,0:T(2,128)(2,1)} %pad_maximum_fusion, bf16[128,2,512]{2,1,0:T(2,128)(2,1)S(1)} %reshape.79), kind=kLoop, calls=%fused_computation.32 | loop fusion | bytes 524288 | tf_op jit(solution)/shard_map/dynamic_update_slice | solution.py:100
  38.1 6.4 %all-to-all-start.1 = ((bf16[128,2,1152]{2,1,0:T(2,128)(2,1)}), bf16[128,2,1152]{2,1,0:T(2,128)(2,1)S(1)}, u32[]{:S(2)}, u32[]{:S(2)}) async-start(bf16[128,2,1152]{2,1,0:T(2,128)(2,1)} %constant_dynamic-update-slice_fusion), calls=%async_computation.1 | async-start | bytes 1179648 | tf_op jit(solution)/shard_map/all_to_all | solution.py:100
  44.6 0.0 copy-start.3
  44.6 6.7 %collective-permute-start = (f32[2,64,128]{2,1,0:T(8,128)S(1)}, f32[2,64,128]{2,1,0:T(8,128)S(1)}, u32[]{:S(2)}, u32[]{:S(2)}) collective-permute-start(f32[2,64,128]{2,1,0:T(8,128)S(1)} %get-tuple-element.15), channel_id=1, source_target_pairs={{0,1},{1,2},{2,3},{3,0},{4,5},{5,6},{6,7},{7,4},{8,9},{9,10},{10,1... | collective-permute-start | bytes 196616 | tf_op jit(solution)/shard_map/ppermute | solution.py:113
  51.4 1.9 %collective-permute-start.2 = (f32[2,64,128]{2,1,0:T(8,128)S(1)}, f32[2,64,128]{2,1,0:T(8,128)S(1)}, u32[]{:S(2)}, u32[]{:S(2)}) collective-permute-start(f32[2,64,128]{2,1,0:T(8,128)S(1)} %get-tuple-element.16), channel_id=1, source_target_pairs={{0,3},{1,0},{2,1},{3,2},{4,7},{5,4},{6,5},{7,6},{8,11},{9,8},{10,9... | collective-permute-start | bytes 196616 | tf_op jit(solution)/shard_map/ppermute | solution.py:113
  53.3 2.4 %collective-permute-start.1 = (f32[2,64,128]{2,1,0:T(8,128)S(1)}, f32[2,64,128]{2,1,0:T(8,128)S(1)}, u32[]{:S(2)}, u32[]{:S(2)}) collective-permute-start(f32[2,64,128]{2,1,0:T(8,128)S(1)} %get-tuple-element.17), channel_id=1, source_target_pairs={{0,2},{1,3},{2,0},{3,1},{4,6},{5,7},{6,4},{7,5},{8,10},{9,11},{10,... | collective-permute-start | bytes 196616 | tf_op jit(solution)/shard_map/ppermute | solution.py:113
  55.8 0.3 convolution_bitcast_fusion.2
  56.0 0.3 fusion.4
  56.3 0.7 reshape.77
  57.0 0.0 collective-permute-done
  57.0 2.4 %collective-permute-done.2 = f32[2,64,128]{2,1,0:T(8,128)S(1)} collective-permute-done((f32[2,64,128]{2,1,0:T(8,128)S(1)}, f32[2,64,128]{2,1,0:T(8,128)S(1)}, u32[]{:S(2)}, u32[]{:S(2)}) %collective-permute-start.2) | collective-permute-done | bytes 65568 | tf_op jit(solution)/shard_map/ppermute | solution.py:113
  59.3 1.4 %collective-permute-done.1 = f32[2,64,128]{2,1,0:T(8,128)S(1)} collective-permute-done((f32[2,64,128]{2,1,0:T(8,128)S(1)}, f32[2,64,128]{2,1,0:T(8,128)S(1)}, u32[]{:S(2)}, u32[]{:S(2)}) %collective-permute-start.1) | collective-permute-done | bytes 65568 | tf_op jit(solution)/shard_map/ppermute | solution.py:113
  60.7 0.0 copy-done.3
  60.7 0.6 add_convert_fusion
  61.4 2.0 %all-to-all-done.1 = bf16[128,2,1152]{2,1,0:T(2,128)(2,1)S(1)} async-done(((bf16[128,2,1152]{2,1,0:T(2,128)(2,1)}), bf16[128,2,1152]{2,1,0:T(2,128)(2,1)S(1)}, u32[]{:S(2)}, u32[]{:S(2)}) %all-to-all-start.1) | async-done | bytes 589856 | tf_op jit(solution)/shard_map/all_to_all | solution.py:100
  63.4 0.5 convert_reduce_fusion
  63.9 0.6 fusion.22
  64.5 0.6 broadcast_in_dim.34
  65.1 8.6 %all-to-all-start.2 = ((f32[4,8,128]{2,1,0:T(8,128)}), f32[4,8,128]{2,1,0:T(8,128)S(1)}, u32[]{:S(2)}, u32[]{:S(2)}) async-start(f32[4,8,128]{2,1,0:T(8,128)} %broadcast_in_dim.34), calls=%async_computation.2 | async-start | bytes 32768 | tf_op jit(solution)/shard_map/all_to_all | solution.py:119
  73.7 0.5 fusion.21
  74.3 4.1 %all-to-all-done.2 = f32[4,8,128]{2,1,0:T(8,128)S(1)} async-done(((f32[4,8,128]{2,1,0:T(8,128)}), f32[4,8,128]{2,1,0:T(8,128)S(1)}, u32[]{:S(2)}, u32[]{:S(2)}) %all-to-all-start.2) | async-done | bytes 16416 | tf_op jit(solution)/shard_map/all_to_all | solution.py:119
  78.4 0.6 broadcast_multiply_fusion
  (9 shorter events, 0.1 us)
Async XLA Ops:
  0.6 22.9 %copy-start = (bf16[2,256,128]{2,1,0:T(8,128)(2,1)S(1)}, bf16[2,256,128]{2,1,0:T(8,128)(2,1)}, u32[]{:S(2)}) copy-start(bf16[2,256,128]{2,1,0:T(8,128)(2,1)} %cotan.1) | copy-start | bytes 393220
  0.6 22.6 %copy-start.1 = (bf16[1024,128]{1,0:T(8,128)(2,1)S(1)}, bf16[1024,128]{1,0:T(8,128)(2,1)}, u32[]{:S(2)}) copy-start(bf16[1024,128]{1,0:T(8,128)(2,1)} %param.8) | copy-start | bytes 786436
  2.2 33.4 %all-to-all-start = ((bf16[128,2,512]{2,1,0:T(2,128)(2,1)}), bf16[128,2,512]{2,1,0:T(2,128)(2,1)S(1)}, u32[]{:S(2)}, u32[]{:S(2)}) async-start(bf16[128,2,512]{2,1,0:T(2,128)(2,1)} %broadcast_in_dim.12), calls=%async_computation | async-start | bytes 524288 | tf_op jit(solution)/shard_map/all_to_all | solution.py:77
  23.5 0.7 copy-start.2
  38.1 25.3 %all-to-all-start.1 = ((bf16[128,2,1152]{2,1,0:T(2,128)(2,1)}), bf16[128,2,1152]{2,1,0:T(2,128)(2,1)S(1)}, u32[]{:S(2)}, u32[]{:S(2)}) async-start(bf16[128,2,1152]{2,1,0:T(2,128)(2,1)} %constant_dynamic-update-slice_fusion), calls=%async_computation.1 | async-start | bytes 1179648 | tf_op jit(solution)/shard_map/all_to_all | solution.py:100
  44.6 16.2 %copy-start.3 = (f32[128]{0:T(128)S(1)}, f32[128]{0:T(128)}, u32[]{:S(2)}) copy-start(f32[128]{0:T(128)} %param.9) | copy-start | bytes 1540
  44.6 12.3 %collective-permute-start = (f32[2,64,128]{2,1,0:T(8,128)S(1)}, f32[2,64,128]{2,1,0:T(8,128)S(1)}, u32[]{:S(2)}, u32[]{:S(2)}) collective-permute-start(f32[2,64,128]{2,1,0:T(8,128)S(1)} %get-tuple-element.15), channel_id=1, source_target_pairs={{0,1},{1,2},{2,3},{3,0},{4,5},{5,6},{6,7},{7,4},{8,9},{9,10},{10,1... | collective-permute-start | bytes 196616 | tf_op jit(solution)/shard_map/ppermute | solution.py:113
  51.4 8.0 %collective-permute-start.2 = (f32[2,64,128]{2,1,0:T(8,128)S(1)}, f32[2,64,128]{2,1,0:T(8,128)S(1)}, u32[]{:S(2)}, u32[]{:S(2)}) collective-permute-start(f32[2,64,128]{2,1,0:T(8,128)S(1)} %get-tuple-element.16), channel_id=1, source_target_pairs={{0,3},{1,0},{2,1},{3,2},{4,7},{5,4},{6,5},{7,6},{8,11},{9,8},{10,9... | collective-permute-start | bytes 196616 | tf_op jit(solution)/shard_map/ppermute | solution.py:113
  53.3 7.4 %collective-permute-start.1 = (f32[2,64,128]{2,1,0:T(8,128)S(1)}, f32[2,64,128]{2,1,0:T(8,128)S(1)}, u32[]{:S(2)}, u32[]{:S(2)}) collective-permute-start(f32[2,64,128]{2,1,0:T(8,128)S(1)} %get-tuple-element.17), channel_id=1, source_target_pairs={{0,2},{1,3},{2,0},{3,1},{4,6},{5,7},{6,4},{7,5},{8,10},{9,11},{10,... | collective-permute-start | bytes 196616 | tf_op jit(solution)/shard_map/ppermute | solution.py:113
  65.1 13.2 %all-to-all-start.2 = ((f32[4,8,128]{2,1,0:T(8,128)}), f32[4,8,128]{2,1,0:T(8,128)S(1)}, u32[]{:S(2)}, u32[]{:S(2)}) async-start(f32[4,8,128]{2,1,0:T(8,128)} %broadcast_in_dim.34), calls=%async_computation.2 | async-start | bytes 32768 | tf_op jit(solution)/shard_map/all_to_all | solution.py:119

commit v5 on v3

v5 whole, which is shorter than its diff:
```python
import jax
import jax.numpy as jnp
from jax import lax
from jax.experimental import pallas as pl
from jax.experimental.pallas import tpu as pltpu
from jax.sharding import Mesh
from jax.sharding import PartitionSpec as P

C = 32
P_SIZE = 128
SEQ_DEV = 16
ROW_DEV = 2
WIDE = SEQ_DEV * C
HALVES = 2
WHOLE = pl.BlockSpec(memory_space=pltpu.VMEM)


def split_in_two(value):
    high = value.astype(jnp.bfloat16)
    return high, (value - high.astype(jnp.float32)).astype(jnp.bfloat16)


def dot32(form, a, b):
    return jnp.einsum(form, a, b, preferred_element_type=jnp.float32)


def opening_kernel(right, cotan, out):
    total = jnp.sum(cotan[...].astype(jnp.float32), axis=(0, 1))[None]
    high = total.astype(jnp.bfloat16).astype(jnp.float32)
    upper = lax.broadcasted_iota(jnp.int32, (ROW_DEV, P_SIZE), 0) == 0
    bias = jnp.where(upper, high, total - high).astype(jnp.bfloat16)
    out[:, :, :WIDE] = jnp.broadcast_to(right[...][None], (out.shape[0], ROW_DEV, WIDE))
    out[:, :, WIDE:] = jnp.broadcast_to(bias[None], (out.shape[0], ROW_DEV, P_SIZE))


def products_kernel(right, cotan, mixed_hi, mixed_lo, left_cols, grad_right, pair, message, back_hi, back_lo, back, weight):
    rows = right[...]
    both = jnp.concatenate([cotan[0], cotan[1]], axis=1)
    terms = lax.dot_general(rows, both, (((0,), (0,)), ((), ())), preferred_element_type=jnp.float32)
    back[0] = terms[:, :P_SIZE]
    back[1] = terms[:, P_SIZE:]
    lhs = left_cols[...]
    for y in range(C):
        parts = []
        for i in range(ROW_DEV):
            parts += split_in_two(back[i, pl.ds(y, SEQ_DEV, stride=C), :])
        weight[pl.ds(y, C, stride=C), :] = jnp.dot(
            lhs, jnp.concatenate(parts, axis=0), preferred_element_type=jnp.float32
        )
    planes = message.shape[0]
    own = message.shape[1] // 2
    halves = weight[...].reshape(HALVES, planes, own // HALVES, P_SIZE)
    message[:, :own, :] = jnp.concatenate([halves[0], halves[1]], axis=1).astype(jnp.bfloat16)
    message[:, own:, :] = grad_right[...]
    for i in range(ROW_DEV):
        pair[i] = jnp.dot(rows, mixed_hi[i], preferred_element_type=jnp.float32) + jnp.dot(
            rows, mixed_lo[i], preferred_element_type=jnp.float32
        )
        back_hi[i], back_lo[i] = split_in_two(back[i])


def middle_kernel(place, parts, out):
    total = jnp.sum(parts[...].astype(jnp.float32), axis=0)
    rows = total.shape[0] // 4
    seq = out.shape[0] // HALVES
    for half in range(HALVES):
        mine = total[half * rows : (half + 1) * rows]
        right = total[(half + 2) * rows : (half + 3) * rows]
        for q in range(seq):
            out[half * seq + q, :rows] = mine
            out[half * seq + q, rows:] = jnp.where(place[0] == q, right, 0.0)


def closing_kernel(scale, parts, weight, right):
    total = jnp.sum(parts[...], axis=0) * scale
    rows = weight.shape[0]
    weight[...] = total[:rows]
    for t in range(ROW_DEV):
        for m in range(rows // ROW_DEV):
            at = rows + t * (rows // ROW_DEV) + m
            right[t : t + 1, m * P_SIZE : (m + 1) * P_SIZE] = total[at : at + 1]


def on_device(left_proj, right_proj, pair_cotangent, out_weight, out_bias):
    planes = lax.axis_size("plane")
    seq = lax.axis_size("seq")
    res = HALVES * planes
    scale = 1.0 / (SEQ_DEV * seq)
    rows = C * C // res
    columns = res * ROW_DEV
    left_rows = left_proj.reshape(ROW_DEV, SEQ_DEV, C)
    weight = out_weight.reshape(C, C, P_SIZE)

    opening = pl.pallas_call(
        opening_kernel,
        out_shape=jax.ShapeDtypeStruct((res, ROW_DEV, WIDE + P_SIZE), jnp.bfloat16),
        in_specs=[WHOLE] * 2,
        out_specs=WHOLE,
        compiler_params=pltpu.CompilerParams(vmem_limit_bytes=8 * 1024 * 1024),
    )(right_proj, pair_cotangent)
    arrived = lax.all_to_all(opening, ("half", "plane"), 0, 0, tiled=True)
    right_all = arrived[:, :, :WIDE].reshape(columns, WIDE)
    grad_bias = jnp.sum(arrived[:, :, WIDE:], axis=(0, 1), dtype=jnp.float32)

    mixed = dot32("isx,xyk->isyk", left_rows, weight)
    high = lax.reduce_precision(mixed, 8, 7)
    mixed_hi, mixed_lo = high.astype(jnp.bfloat16), (mixed - high).astype(jnp.bfloat16)
    grad_right = dot32("ijk,isyk->jsy", pair_cotangent, mixed_hi) + dot32("ijk,isyk->jsy", pair_cotangent, mixed_lo)
    grad_right = grad_right.astype(jnp.bfloat16).reshape(HALVES, planes, rows, P_SIZE)
    grad_right = jnp.moveaxis(grad_right, 0, 1).reshape(planes, HALVES * rows, P_SIZE)
    left_cols = jnp.broadcast_to(left_rows.transpose(2, 0, 1)[:, :, None], (C, ROW_DEV, 2, SEQ_DEV))
    left_cols = left_cols.reshape(C, ROW_DEV * 2 * SEQ_DEV)

    back = (ROW_DEV, WIDE, P_SIZE)
    pair, message, back_hi, back_lo = pl.pallas_call(
        products_kernel,
        out_shape=(
            jax.ShapeDtypeStruct((ROW_DEV, columns, P_SIZE), jnp.float32),
            jax.ShapeDtypeStruct((planes, 2 * HALVES * rows, P_SIZE), jnp.bfloat16),
            jax.ShapeDtypeStruct(back, jnp.bfloat16),
            jax.ShapeDtypeStruct(back, jnp.bfloat16),
        ),
        in_specs=[WHOLE] * 6,
        out_specs=(WHOLE,) * 4,
        scratch_shapes=[pltpu.VMEM(back, jnp.float32), pltpu.VMEM((C * C, P_SIZE), jnp.float32)],
        compiler_params=pltpu.CompilerParams(vmem_limit_bytes=16 * 1024 * 1024),
        cost_estimate=pl.CostEstimate(flops=300_000_000, bytes_accessed=3_000_000, transcendentals=0),
    )(right_all, pair_cotangent, mixed_hi.reshape(back), mixed_lo.reshape(back), left_cols, grad_right)

    parts = lax.all_to_all(message, "plane", 0, 0, tiled=True)

    back_hi, back_lo = (term.reshape(ROW_DEV, SEQ_DEV, C, P_SIZE) for term in (back_hi, back_lo))
    grad_left = dot32("isyk,xyk->isx", back_hi, weight) + dot32("isyk,xyk->isx", back_lo, weight)
    cols = columns // seq
    here = lax.axis_index("seq")

    def columns_of(owner):
        return lax.dynamic_slice_in_dim(pair, owner * cols, cols, 1)

    pair_sum = columns_of(here)
    for step in range(1, seq):
        sent = columns_of(lax.bitwise_xor(here, jnp.int32(step)))
        pair_sum = pair_sum + lax.ppermute(sent, "seq", [(q, q ^ step) for q in range(seq)])
    pair_update = (pair_sum * scale + out_bias).astype(jnp.bfloat16)

    last = pl.pallas_call(
        middle_kernel,
        out_shape=jax.ShapeDtypeStruct((HALVES * seq, 2 * rows, P_SIZE), jnp.float32),
        in_specs=[pl.BlockSpec(memory_space=pltpu.SMEM), WHOLE],
        out_specs=WHOLE,
        compiler_params=pltpu.CompilerParams(vmem_limit_bytes=8 * 1024 * 1024),
    )(here.reshape(1), parts)
    last = lax.all_to_all(last, ("half", "seq"), 0, 0, tiled=True)
    grad_weight, grad_right = pl.pallas_call(
        lambda *refs: closing_kernel(scale, *refs),
        out_shape=(
            jax.ShapeDtypeStruct((rows, P_SIZE), jnp.float32),
            jax.ShapeDtypeStruct((ROW_DEV, WIDE), jnp.float32),
        ),
        in_specs=[WHOLE],
        out_specs=(WHOLE,) * 2,
        compiler_params=pltpu.CompilerParams(vmem_limit_bytes=8 * 1024 * 1024),
    )(last)
    return pair_update, (grad_left * scale).reshape(ROW_DEV, WIDE), grad_right, grad_weight, grad_bias


def solution(mesh):
    res, seq = mesh.devices.shape
    fine = Mesh(mesh.devices.reshape(HALVES, res // HALVES, seq), ("half", "plane", "seq"))
    across = ("half", "plane")
    return jax.shard_map(
        on_device,
        mesh=fine,
        in_specs=(P(across, "seq"), P(across, "seq"), P(across, None, None), P(), P()),
        out_specs=(P(across, "seq", None), P(across, "seq"), P(across, "seq"), P(across, None), P()),
        check_vma=False,
    )
```

time: 80.7 us -> 77 us (0.954)
  Pallas kernels: 0 us -> 4.32 us
  local copies, waits for them, and re-layouts: 8.93 us -> 5.3 us
  other arithmetic: 3.83 us -> 1.3 us
  matrix products: 3.57 us -> 1.29 us
  starting transfers between devices: 42.8 us -> 44.6 us
  waiting for transfers between devices: 20.2 us -> 19 us
    ppermute x3, waiting for transfers between devices: 6.37 us -> 0.01 us  [on_device(): lax.ppermute(sent, 'seq', [(q, q ^ step) for q in range(seq)])]
    all_to_all x3, waiting for transfers between devices: 13.9 us -> 19 us  [the longest x1 11.8 us: on_device(): arrived = lax.all_to_all(opening, ('half', 'plane'), 0, 0, tiled=True)]
    pallas_call x0 -> x4, Pallas kernels: none -> 4.32 us  [the longest x1 2.11 us: on_device(): pl.pallas_call(products_kernel, out_shape=(jax.ShapeDtypeStruct((ROW_DEV,...]
    dot_general x10 -> x5, matrix products: 3.57 us -> 1.29 us  [dot32(): return jnp.einsum(form, a, b, preferred_element_type=jnp.float32)]
    all_to_all x3, starting transfers between devices: 31.7 us -> 34 us  [the longest x1 19.4 us: on_device(): arrived = lax.all_to_all(opening, ('half', 'plane'), 0, 0, tiled=True)]
    broadcast_in_dim x4 -> x1, local copies, waits for them, and re-layouts: 2.19 us -> 0.01 us  [on_device(): jnp.broadcast_to(left_rows.transpose(2, 0, 1)[:, :, None], (C, ROW_DEV, 2...]
    unnamed x7 -> x12, local copies, waits for them, and re-layouts: 0.73 us -> 2.41 us
    reshape x4, local copies, waits for them, and re-layouts: 2.26 us -> 0.74 us  [the longest x1 0.51 us: on_device(): grad_right.astype(jnp.bfloat16).reshape(HALVES, planes, rows, P_SIZE)]
  transfers between devices with their start and end apart: 6 -> 6, of which waited for: 4 -> 3; matrix products, arithmetic and copies ran while one was open for 11% -> 7% of each run, Pallas kernels for 0% -> 1%
where the time goes in v5:
time: 77 us; the launch traced here: 76.6 us
  starting transfers between devices  44.6 us (58%)
  waiting for transfers between devices  19 us (25%)
  local copies, waits for them, and re-layouts  5.3 us (7%)
  Pallas kernels  4.32 us (6%)
  other arithmetic  1.3 us (2%)
  matrix products  1.29 us (2%)
  between operations  0.82 us (1%)
    all_to_all x1, starting transfers between devices, on_device(): arrived = lax.all_to_all(opening, ('half', 'plane'), 0, 0, tiled=True)  19.4 us
    all_to_all x1, waiting for transfers between devices, on_device(): arrived = lax.all_to_all(opening, ('half', 'plane'), 0, 0, tiled=True)  11.8 us
    ppermute x3, starting transfers between devices, on_device(): lax.ppermute(sent, 'seq', [(q, q ^ step) for q in range(seq)])  10.6 us
    all_to_all x1, starting transfers between devices, on_device(): last = lax.all_to_all(last, ('half', 'seq'), 0, 0, tiled=True)  9.11 us
    all_to_all x1, starting transfers between devices, on_device(): parts = lax.all_to_all(message, 'plane', 0, 0, tiled=True)  5.46 us
    all_to_all x1, waiting for transfers between devices, on_device(): last = lax.all_to_all(last, ('half', 'seq'), 0, 0, tiled=True)  4.02 us
    all_to_all x1, waiting for transfers between devices, on_device(): parts = lax.all_to_all(message, 'plane', 0, 0, tiled=True)  3.17 us
    unnamed x12, local copies, waits for them, and re-layouts  2.41 us
  transfers between devices with their start and end apart: 6, of which 3 were waited for; matrix products, arithmetic and copies ran while one was open for 7% of the time, Pallas kernels for 1%

profile of v5, /device:TPU:1, one launch (start us, length us, event | category | flops | bytes accessed | tf_op | source)
XLA Modules:
  0.0 76.6 jit_solution(6099943919364747234)
XLA Ops:
  0.6 0.0 copy-start
  0.6 0.9 %copy-done = bf16[2,256,128]{2,1,0:T(8,128)(2,1)S(1)} copy-done((bf16[2,256,128]{2,1,0:T(8,128)(2,1)S(1)}, bf16[2,256,128]{2,1,0:T(8,128)(2,1)}, u32[]{:S(2)}) %copy-start) | copy-done | bytes 131096
  1.5 0.0 copy-start.2
  1.5 0.7 copy-done.2
  2.2 0.9 %shard_map.92 = bf16[128,2,640]{2,1,0:T(2,128)(2,1)} custom-call(bf16[2,512]{1,0:T(2,128)(2,1)S(1)} %copy-done.2, bf16[2,256,128]{2,1,0:T(8,128)(2,1)S(1)} %copy-done), custom_call_target="tpu_custom_call" | custom-call | tf_op jit(solution)/shard_map/pallas_call | solution.py:94
  3.1 0.0 copy-start.4
  3.1 0.0 copy-start.3
  3.1 19.4 %all-to-all-start = ((bf16[128,2,640]{2,1,0:T(2,128)(2,1)}), bf16[128,2,640]{2,1,0:T(2,128)(2,1)S(1)}, u32[]{:S(2)}, u32[]{:S(2)}) async-start(bf16[128,2,640]{2,1,0:T(2,128)(2,1)} %shard_map.92), calls=%async_computation | async-start | bytes 655360 | tf_op jit(solution)/shard_map/all_to_all | solution.py:101
  22.5 0.0 copy-done.4
  22.5 0.1 reshape.60
  22.6 0.0 copy-done.3
  22.6 0.2 fusion.5
  22.9 0.1 reshape.49
  23.0 0.1 copy.27.left_cols
  23.0 0.1 copy.22
  23.1 0.0 copy-start.1
  23.1 0.1 copy.21
  23.2 0.8 %copy-done.1 = bf16[2,256,128]{2,1,0:T(8,128)(2,1)S(1)} copy-done((bf16[2,256,128]{2,1,0:T(8,128)(2,1)S(1)}, bf16[2,256,128]{2,1,0:T(8,128)(2,1)}, u32[]{:S(2)}) %copy-start.1) | copy-done | bytes 131096
  24.0 0.3 convolution_bitcast_fusion
  24.3 0.3 fusion.2
  24.6 0.9 %copy.25 = bf16[256,16,32]{2,1,0:T(8,128)(2,1)S(1)} copy(bf16[256,16,32]{0,2,1:T(8,128)(2,1)S(1)} %fusion.2) | data formatting | bytes 524288 | tf_op jit(solution)/shard_map/convert_element_type | solution.py:109
  25.5 0.5 reshape.54
  26.1 11.8 %all-to-all-done = bf16[128,2,640]{2,1,0:T(2,128)(2,1)S(1)} async-done(((bf16[128,2,640]{2,1,0:T(2,128)(2,1)}), bf16[128,2,640]{2,1,0:T(2,128)(2,1)S(1)}, u32[]{:S(2)}, u32[]{:S(2)}) %all-to-all-start) | async-done | bytes 327712 | tf_op jit(solution)/shard_map/all_to_all | solution.py:101
  37.9 0.2 slice.8
  38.0 0.1 reshape.48.right
  38.1 2.1 %shard_map.93 = (f32[2,256,128]{2,1,0:T(8,128)S(1)}, bf16[64,32,128]{2,1,0:T(8,128)(2,1)}, bf16[2,512,128]{2,1,0:T(8,128)(2,1)S(1)}, bf16[2,512,128]{2,1,0:T(8,128)(2,1)S(1)}) custom-call(bf16[256,512]{1,0:T(8,128)(2,1)S(1)} %reshape.48.right, bf16[2,256,128]{2,1,0:T(8,128)(2,1)S(1)} %copy-done.1, bf16[2,512,128]{2,1,0:T(8,128)(2,1)S(1)} %bitcast.59, ...), custom_call_target="tpu_custom_call" | custom-call | flops 300000000 | bytes 3000000 | tf_op jit(solution)/shard_map/pallas_call | solution.py:115
  40.3 5.5 %all-to-all-start.1 = ((bf16[64,32,128]{2,1,0:T(8,128)(2,1)}), bf16[64,32,128]{2,1,0:T(8,128)(2,1)S(1)}, u32[]{:S(2)}, u32[]{:S(2)}) async-start(bf16[64,32,128]{2,1,0:T(8,128)(2,1)} %get-tuple-element.14), calls=%async_computation.1 | async-start | bytes 1048576 | tf_op jit(solution)/shard_map/all_to_all | solution.py:130
  45.7 0.3 convolution_bitcast_fusion.2
  46.0 0.3 fusion.4
  46.3 0.7 reshape.58
  47.0 3.9 %collective-permute-start = (f32[2,64,128]{2,1,0:T(8,128)S(1)}, f32[2,64,128]{2,1,0:T(8,128)S(1)}, u32[]{:S(2)}, u32[]{:S(2)}) collective-permute-start(f32[2,64,128]{2,1,0:T(8,128)S(1)} %get-tuple-element.19), channel_id=1, source_target_pairs={{0,1},{1,0},{2,3},{3,2},{4,5},{5,4},{6,7},{7,6},{8,9},{9,8},{10,11... | collective-permute-start | bytes 196616 | tf_op jit(solution)/shard_map/ppermute | solution.py:143
  50.9 4.3 %collective-permute-start.2 = (f32[2,64,128]{2,1,0:T(8,128)S(1)}, f32[2,64,128]{2,1,0:T(8,128)S(1)}, u32[]{:S(2)}, u32[]{:S(2)}) collective-permute-start(f32[2,64,128]{2,1,0:T(8,128)S(1)} %get-tuple-element.20), channel_id=1, source_target_pairs={{0,3},{1,2},{2,1},{3,0},{4,7},{5,6},{6,5},{7,4},{8,11},{9,10},{10,... | collective-permute-start | bytes 196616 | tf_op jit(solution)/shard_map/ppermute | solution.py:143
  55.1 2.4 %collective-permute-start.1 = (f32[2,64,128]{2,1,0:T(8,128)S(1)}, f32[2,64,128]{2,1,0:T(8,128)S(1)}, u32[]{:S(2)}, u32[]{:S(2)}) collective-permute-start(f32[2,64,128]{2,1,0:T(8,128)S(1)} %get-tuple-element.21), channel_id=1, source_target_pairs={{0,2},{1,3},{2,0},{3,1},{4,6},{5,7},{6,4},{7,5},{8,10},{9,11},{10,... | collective-permute-start | bytes 196616 | tf_op jit(solution)/shard_map/ppermute | solution.py:143
  57.6 0.7 convert_reduce_fusion
  58.2 3.2 %all-to-all-done.1.parts = bf16[64,32,128]{2,1,0:T(8,128)(2,1)S(1)} async-done(((bf16[64,32,128]{2,1,0:T(8,128)(2,1)}), bf16[64,32,128]{2,1,0:T(8,128)(2,1)S(1)}, u32[]{:S(2)}, u32[]{:S(2)}) %all-to-all-start.1) | async-done | bytes 524320 | tf_op jit(solution)/shard_map/all_to_all | solution.py:130
  61.4 0.7 shard_map.94
  62.1 0.0 copy-start.5
  62.1 9.1 %all-to-all-start.2 = ((f32[8,16,128]{2,1,0:T(8,128)}), f32[8,16,128]{2,1,0:T(8,128)S(1)}, u32[]{:S(2)}, u32[]{:S(2)}) async-start(f32[8,16,128]{2,1,0:T(8,128)} %shard_map.94), calls=%async_computation.2 | async-start | bytes 131072 | tf_op jit(solution)/shard_map/all_to_all | solution.py:153
  71.3 0.0 collective-permute-done
  71.3 0.0 collective-permute-done.2
  71.3 0.0 collective-permute-done.1
  71.3 0.0 copy-done.5
  71.3 0.6 add_convert_fusion
  71.9 4.0 %all-to-all-done.2.refs_0_ = f32[8,16,128]{2,1,0:T(8,128)S(1)} async-done(((f32[8,16,128]{2,1,0:T(8,128)}), f32[8,16,128]{2,1,0:T(8,128)S(1)}, u32[]{:S(2)}, u32[]{:S(2)}) %all-to-all-start.2) | async-done | bytes 65568 | tf_op jit(solution)/shard_map/all_to_all | solution.py:153
  76.0 0.6 shard_map.95
  (3 shorter events, 0.1 us)
Async XLA Ops:
  0.6 0.9 %copy-start = (bf16[2,256,128]{2,1,0:T(8,128)(2,1)S(1)}, bf16[2,256,128]{2,1,0:T(8,128)(2,1)}, u32[]{:S(2)}) copy-start(bf16[2,256,128]{2,1,0:T(8,128)(2,1)} %cotan.3) | copy-start | bytes 393220
  1.5 0.7 copy-start.2
  3.1 19.4 %copy-start.4 = (bf16[2,512]{1,0:T(2,128)(2,1)S(1)}, bf16[2,512]{1,0:T(2,128)(2,1)}, u32[]{:S(2)}) copy-start(bf16[2,512]{1,0:T(2,128)(2,1)} %param.5) | copy-start | bytes 6148
  3.1 19.5 %copy-start.3 = (bf16[1024,128]{1,0:T(8,128)(2,1)S(1)}, bf16[1024,128]{1,0:T(8,128)(2,1)}, u32[]{:S(2)}) copy-start(bf16[1024,128]{1,0:T(8,128)(2,1)} %param.8) | copy-start | bytes 786436
  3.1 34.8 %all-to-all-start = ((bf16[128,2,640]{2,1,0:T(2,128)(2,1)}), bf16[128,2,640]{2,1,0:T(2,128)(2,1)S(1)}, u32[]{:S(2)}, u32[]{:S(2)}) async-start(bf16[128,2,640]{2,1,0:T(2,128)(2,1)} %shard_map.92), calls=%async_computation | async-start | bytes 655360 | tf_op jit(solution)/shard_map/all_to_all | solution.py:101
  23.1 0.9 %copy-start.1 = (bf16[2,256,128]{2,1,0:T(8,128)(2,1)S(1)}, bf16[2,256,128]{2,1,0:T(8,128)(2,1)}, u32[]{:S(2)}) copy-start(bf16[2,256,128]{2,1,0:T(8,128)(2,1)} %cotan.3) | copy-start | bytes 393220
  40.3 21.2 %all-to-all-start.1 = ((bf16[64,32,128]{2,1,0:T(8,128)(2,1)}), bf16[64,32,128]{2,1,0:T(8,128)(2,1)S(1)}, u32[]{:S(2)}, u32[]{:S(2)}) async-start(bf16[64,32,128]{2,1,0:T(8,128)(2,1)} %get-tuple-element.14), calls=%async_computation.1 | async-start | bytes 1048576 | tf_op jit(solution)/shard_map/all_to_all | solution.py:130
  47.0 24.3 %collective-permute-start = (f32[2,64,128]{2,1,0:T(8,128)S(1)}, f32[2,64,128]{2,1,0:T(8,128)S(1)}, u32[]{:S(2)}, u32[]{:S(2)}) collective-permute-start(f32[2,64,128]{2,1,0:T(8,128)S(1)} %get-tuple-element.19), channel_id=1, source_target_pairs={{0,1},{1,0},{2,3},{3,2},{4,5},{5,4},{6,7},{7,6},{8,9},{9,8},{10,11... | collective-permute-start | bytes 196616 | tf_op jit(solution)/shard_map/ppermute | solution.py:143
  50.9 20.4 %collective-permute-start.2 = (f32[2,64,128]{2,1,0:T(8,128)S(1)}, f32[2,64,128]{2,1,0:T(8,128)S(1)}, u32[]{:S(2)}, u32[]{:S(2)}) collective-permute-start(f32[2,64,128]{2,1,0:T(8,128)S(1)} %get-tuple-element.20), channel_id=1, source_target_pairs={{0,3},{1,2},{2,1},{3,0},{4,7},{5,6},{6,5},{7,4},{8,11},{9,10},{10,... | collective-permute-start | bytes 196616 | tf_op jit(solution)/shard_map/ppermute | solution.py:143
  55.1 16.1 %collective-permute-start.1 = (f32[2,64,128]{2,1,0:T(8,128)S(1)}, f32[2,64,128]{2,1,0:T(8,128)S(1)}, u32[]{:S(2)}, u32[]{:S(2)}) collective-permute-start(f32[2,64,128]{2,1,0:T(8,128)S(1)} %get-tuple-element.21), channel_id=1, source_target_pairs={{0,2},{1,3},{2,0},{3,1},{4,6},{5,7},{6,4},{7,5},{8,10},{9,11},{10,... | collective-permute-start | bytes 196616 | tf_op jit(solution)/shard_map/ppermute | solution.py:143
  62.1 9.1 %copy-start.5 = (f32[128]{0:T(128)S(1)}, f32[128]{0:T(128)}, u32[]{:S(2)}) copy-start(f32[128]{0:T(128)} %param.9) | copy-start | bytes 1540
  62.1 13.8 %all-to-all-start.2 = ((f32[8,16,128]{2,1,0:T(8,128)}), f32[8,16,128]{2,1,0:T(8,128)S(1)}, u32[]{:S(2)}, u32[]{:S(2)}) async-start(f32[8,16,128]{2,1,0:T(8,128)} %shard_map.94), calls=%async_computation.2 | async-start | bytes 131072 | tf_op jit(solution)/shard_map/all_to_all | solution.py:153

commit v6 on v5

--- a/solution.py
+++ b/solution.py
@@ -33,7 +33,7 @@
     out[:, :, WIDE:] = jnp.broadcast_to(bias[None], (out.shape[0], ROW_DEV, P_SIZE))
 
 
-def products_kernel(right, cotan, mixed_hi, mixed_lo, left_cols, grad_right, pair, message, back_hi, back_lo, back, weight):
+def products_kernel(right, cotan, left_cols, grad_right, message, back, weight):
     rows = right[...]
     both = jnp.concatenate([cotan[0], cotan[1]], axis=1)
     terms = lax.dot_general(rows, both, (((0,), (0,)), ((), ())), preferred_element_type=jnp.float32)
@@ -52,6 +52,10 @@
     halves = weight[...].reshape(HALVES, planes, own // HALVES, P_SIZE)
     message[:, :own, :] = jnp.concatenate([halves[0], halves[1]], axis=1).astype(jnp.bfloat16)
     message[:, own:, :] = grad_right[...]
+
+
+def pair_kernel(right, mixed_hi, mixed_lo, back, pair, back_hi, back_lo):
+    rows = right[...]
     for i in range(ROW_DEV):
         pair[i] = jnp.dot(rows, mixed_hi[i], preferred_element_type=jnp.float32) + jnp.dot(
             rows, mixed_lo[i], preferred_element_type=jnp.float32
@@ -96,7 +100,6 @@
         out_shape=jax.ShapeDtypeStruct((res, ROW_DEV, WIDE + P_SIZE), jnp.bfloat16),
         in_specs=[WHOLE] * 2,
         out_specs=WHOLE,
-        compiler_params=pltpu.CompilerParams(vmem_limit_bytes=8 * 1024 * 1024),
     )(right_proj, pair_cotangent)
     arrived = lax.all_to_all(opening, ("half", "plane"), 0, 0, tiled=True)
     right_all = arrived[:, :, :WIDE].reshape(columns, WIDE)
@@ -112,23 +115,33 @@
     left_cols = left_cols.reshape(C, ROW_DEV * 2 * SEQ_DEV)
 
     back = (ROW_DEV, WIDE, P_SIZE)
-    pair, message, back_hi, back_lo = pl.pallas_call(
+    message, terms = pl.pallas_call(
         products_kernel,
         out_shape=(
+            jax.ShapeDtypeStruct((planes, 2 * HALVES * rows, P_SIZE), jnp.bfloat16),
+            jax.ShapeDtypeStruct(back, jnp.float32),
+        ),
+        in_specs=[WHOLE] * 4,
+        out_specs=(WHOLE,) * 2,
+        scratch_shapes=[pltpu.VMEM((C * C, P_SIZE), jnp.float32)],
+        compiler_params=pltpu.CompilerParams(vmem_limit_bytes=16 * 1024 * 1024),
+        cost_estimate=pl.CostEstimate(flops=200_000_000, bytes_accessed=2_000_000, transcendentals=0),
+    )(right_all, pair_cotangent, left_cols, grad_right)
+
+    parts = lax.all_to_all(message, "plane", 0, 0, tiled=True)
+
+    pair, back_hi, back_lo = pl.pallas_call(
+        pair_kernel,
+        out_shape=(
             jax.ShapeDtypeStruct((ROW_DEV, columns, P_SIZE), jnp.float32),
-            jax.ShapeDtypeStruct((planes, 2 * HALVES * rows, P_SIZE), jnp.bfloat16),
             jax.ShapeDtypeStruct(back, jnp.bfloat16),
             jax.ShapeDtypeStruct(back, jnp.bfloat16),
         ),
-        in_specs=[WHOLE] * 6,
-        out_specs=(WHOLE,) * 4,
-        scratch_shapes=[pltpu.VMEM(back, jnp.float32), pltpu.VMEM((C * C, P_SIZE), jnp.float32)],
+        in_specs=[WHOLE] * 4,
+        out_specs=(WHOLE,) * 3,
         compiler_params=pltpu.CompilerParams(vmem_limit_bytes=16 * 1024 * 1024),
-        cost_estimate=pl.CostEstimate(flops=300_000_000, bytes_accessed=3_000_000, transcendentals=0),
-    )(right_all, pair_cotangent, mixed_hi.reshape(back), mixed_lo.reshape(back), left_cols, grad_right)
-
-    parts = lax.all_to_all(message, "plane", 0, 0, tiled=True)
-
+        cost_estimate=pl.CostEstimate(flops=150_000_000, bytes_accessed=2_000_000, transcendentals=0),
+    )(right_all, mixed_hi.reshape(back), mixed_lo.reshape(back), terms)
     back_hi, back_lo = (term.reshape(ROW_DEV, SEQ_DEV, C, P_SIZE) for term in (back_hi, back_lo))
     grad_left = dot32("isyk,xyk->isx", back_hi, weight) + dot32("isyk,xyk->isx", back_lo, weight)
     cols = columns // seq

time: 77 us -> 76 us (0.987)
  local copies, waits for them, and re-layouts: 5.3 us -> 3.38 us
  Pallas kernels: 4.32 us -> 5.35 us
    unnamed x12 -> x8, local copies, waits for them, and re-layouts: 2.41 us -> 0.5 us
    pallas_call x1, Pallas kernels: 0.87 us -> 1.76 us  [on_device(): pl.pallas_call(opening_kernel, out_shape=jax.ShapeDtypeStruct((res, ROW_D...]
    pallas_call x1 -> x2, Pallas kernels: 2.11 us -> 2.26 us  [the longest x1 1.82 us: on_device(): pl.pallas_call(products_kernel, out_shape=(jax.ShapeDtypeStruct((planes,...]
  transfers between devices with their start and end apart: 6 -> 6, of which waited for: 3 -> 3; matrix products, arithmetic and copies ran while one was open for 7% -> 7% of each run, Pallas kernels for 1% -> 2%
where the time goes in v6:
time: 76 us; the launch traced here: 75.6 us
  starting transfers between devices  44.6 us (59%)
  waiting for transfers between devices  18.9 us (25%)
  Pallas kernels  5.35 us (7%)
  local copies, waits for them, and re-layouts  3.38 us (4%)
  other arithmetic  1.3 us (2%)
  matrix products  1.29 us (2%)
  between operations  0.82 us (1%)
    all_to_all x1, starting transfers between devices, on_device(): arrived = lax.all_to_all(opening, ('half', 'plane'), 0, 0, tiled=True)  19.4 us
    all_to_all x1, waiting for transfers between devices, on_device(): arrived = lax.all_to_all(opening, ('half', 'plane'), 0, 0, tiled=True)  12.3 us
    ppermute x3, starting transfers between devices, on_device(): lax.ppermute(sent, 'seq', [(q, q ^ step) for q in range(seq)])  10.6 us
    all_to_all x1, starting transfers between devices, on_device(): last = lax.all_to_all(last, ('half', 'seq'), 0, 0, tiled=True)  9.11 us
    all_to_all x1, starting transfers between devices, on_device(): parts = lax.all_to_all(message, 'plane', 0, 0, tiled=True)  5.46 us
    all_to_all x1, waiting for transfers between devices, on_device(): last = lax.all_to_all(last, ('half', 'seq'), 0, 0, tiled=True)  4.02 us
    all_to_all x1, waiting for transfers between devices, on_device(): parts = lax.all_to_all(message, 'plane', 0, 0, tiled=True)  2.56 us
    pallas_call x1, Pallas kernels, on_device(): pl.pallas_call(products_kernel, out_shape=(jax.ShapeDtypeStruct((planes,...  1.82 us
  transfers between devices with their start and end apart: 6, of which 3 were waited for; matrix products, arithmetic and copies ran while one was open for 7% of the time, Pallas kernels for 2%

profile of v6, /device:TPU:1, one launch (start us, length us, event | category | flops | bytes accessed | tf_op | source)
XLA Modules:
  0.0 75.6 jit_solution(5416270465504295303)
XLA Ops:
  0.6 1.8 %shard_map.92 = bf16[128,2,640]{2,1,0:T(2,128)(2,1)} custom-call(bf16[2,512]{1,0:T(2,128)(2,1)} %right.1, bf16[2,256,128]{2,1,0:T(8,128)(2,1)} %cotan.3), custom_call_target="tpu_custom_call" | custom-call | tf_op jit(solution)/shard_map/pallas_call | solution.py:98
  2.4 0.0 copy-start.2
  2.4 0.0 copy-start.1
  2.4 19.4 %all-to-all-start = ((bf16[128,2,640]{2,1,0:T(2,128)(2,1)}), bf16[128,2,640]{2,1,0:T(2,128)(2,1)S(1)}, u32[]{:S(2)}, u32[]{:S(2)}) async-start(bf16[128,2,640]{2,1,0:T(2,128)(2,1)} %shard_map.92), calls=%async_computation | async-start | bytes 655360 | tf_op jit(solution)/shard_map/all_to_all | solution.py:104
  21.8 0.0 copy-done.2
  21.8 0.1 reshape.60
  21.9 0.0 copy-done.1
  21.9 0.0 copy-start
  21.9 0.2 fusion.5
  22.2 0.1 reshape.49
  22.3 0.1 copy.27.left_cols
  22.3 0.5 copy-done
  22.8 0.3 convolution_bitcast_fusion
  23.1 0.3 fusion.2
  23.4 0.9 %copy.25 = bf16[256,16,32]{2,1,0:T(8,128)(2,1)S(1)} copy(bf16[256,16,32]{0,2,1:T(8,128)(2,1)S(1)} %fusion.2) | data formatting | bytes 524288 | tf_op jit(solution)/shard_map/convert_element_type | solution.py:112
  24.3 0.5 reshape.54
  24.9 12.3 %all-to-all-done = bf16[128,2,640]{2,1,0:T(2,128)(2,1)S(1)} async-done(((bf16[128,2,640]{2,1,0:T(2,128)(2,1)}), bf16[128,2,640]{2,1,0:T(2,128)(2,1)S(1)}, u32[]{:S(2)}, u32[]{:S(2)}) %all-to-all-start) | async-done | bytes 327712 | tf_op jit(solution)/shard_map/all_to_all | solution.py:104
  37.2 0.2 slice.8
  37.3 0.1 reshape.48.right
  37.4 1.8 %shard_map.93 = (bf16[64,32,128]{2,1,0:T(8,128)(2,1)}, f32[2,512,128]{2,1,0:T(8,128)S(1)}) custom-call(bf16[256,512]{1,0:T(8,128)(2,1)S(1)} %reshape.48.right, bf16[2,256,128]{2,1,0:T(8,128)(2,1)S(1)} %copy-done, bf16[32,64]{1,0:T(8,128)(2,1)S(1)} %copy.27.left_cols, bf16[64,16,128]{2,1,0:T(8,128)(2,1)S(1)} %copy_bitcast_fusion.grad_right), custom_call_target="tpu_custom_call" | custom-call | flops 200000000 | bytes 2000000 | tf_op jit(solution)/shard_map/pallas_call | solution.py:118
  39.3 5.5 %all-to-all-start.1 = ((bf16[64,32,128]{2,1,0:T(8,128)(2,1)}), bf16[64,32,128]{2,1,0:T(8,128)(2,1)S(1)}, u32[]{:S(2)}, u32[]{:S(2)}) async-start(bf16[64,32,128]{2,1,0:T(8,128)(2,1)} %get-tuple-element.16), calls=%async_computation.1 | async-start | bytes 1048576 | tf_op jit(solution)/shard_map/all_to_all | solution.py:131
  44.8 0.1 copy.22
  44.8 0.1 copy.21
  44.9 0.4 shard_map.94
  45.4 0.3 convolution_bitcast_fusion.2
  45.6 0.3 fusion.4
  45.9 0.7 reshape.58
  46.6 3.9 %collective-permute-start = (f32[2,64,128]{2,1,0:T(8,128)S(1)}, f32[2,64,128]{2,1,0:T(8,128)S(1)}, u32[]{:S(2)}, u32[]{:S(2)}) collective-permute-start(f32[2,64,128]{2,1,0:T(8,128)S(1)} %get-tuple-element.21), channel_id=1, source_target_pairs={{0,1},{1,0},{2,3},{3,2},{4,5},{5,4},{6,7},{7,6},{8,9},{9,8},{10,11... | collective-permute-start | bytes 196616 | tf_op jit(solution)/shard_map/ppermute | solution.py:156
  50.5 4.3 %collective-permute-start.2 = (f32[2,64,128]{2,1,0:T(8,128)S(1)}, f32[2,64,128]{2,1,0:T(8,128)S(1)}, u32[]{:S(2)}, u32[]{:S(2)}) collective-permute-start(f32[2,64,128]{2,1,0:T(8,128)S(1)} %get-tuple-element.22), channel_id=1, source_target_pairs={{0,3},{1,2},{2,1},{3,0},{4,7},{5,6},{6,5},{7,4},{8,11},{9,10},{10,... | collective-permute-start | bytes 196616 | tf_op jit(solution)/shard_map/ppermute | solution.py:156
  54.8 2.4 %collective-permute-start.1 = (f32[2,64,128]{2,1,0:T(8,128)S(1)}, f32[2,64,128]{2,1,0:T(8,128)S(1)}, u32[]{:S(2)}, u32[]{:S(2)}) collective-permute-start(f32[2,64,128]{2,1,0:T(8,128)S(1)} %get-tuple-element.23), channel_id=1, source_target_pairs={{0,2},{1,3},{2,0},{3,1},{4,6},{5,7},{6,4},{7,5},{8,10},{9,11},{10,... | collective-permute-start | bytes 196616 | tf_op jit(solution)/shard_map/ppermute | solution.py:156
  57.2 0.7 convert_reduce_fusion
  57.9 2.6 %all-to-all-done.1.parts = bf16[64,32,128]{2,1,0:T(8,128)(2,1)S(1)} async-done(((bf16[64,32,128]{2,1,0:T(8,128)(2,1)}), bf16[64,32,128]{2,1,0:T(8,128)(2,1)S(1)}, u32[]{:S(2)}, u32[]{:S(2)}) %all-to-all-start.1) | async-done | bytes 524320 | tf_op jit(solution)/shard_map/all_to_all | solution.py:131
  60.4 0.7 shard_map.95
  61.2 0.0 copy-start.3
  61.2 9.1 %all-to-all-start.2 = ((f32[8,16,128]{2,1,0:T(8,128)}), f32[8,16,128]{2,1,0:T(8,128)S(1)}, u32[]{:S(2)}, u32[]{:S(2)}) async-start(f32[8,16,128]{2,1,0:T(8,128)} %shard_map.95), calls=%async_computation.2 | async-start | bytes 131072 | tf_op jit(solution)/shard_map/all_to_all | solution.py:166
  70.3 0.0 collective-permute-done
  70.3 0.0 collective-permute-done.2
  70.3 0.0 collective-permute-done.1
  70.3 0.0 copy-done.3
  70.3 0.6 add_convert_fusion
  70.9 4.0 %all-to-all-done.2.refs_0_ = f32[8,16,128]{2,1,0:T(8,128)S(1)} async-done(((f32[8,16,128]{2,1,0:T(8,128)}), f32[8,16,128]{2,1,0:T(8,128)S(1)}, u32[]{:S(2)}, u32[]{:S(2)}) %all-to-all-start.2) | async-done | bytes 65568 | tf_op jit(solution)/shard_map/all_to_all | solution.py:166
  75.0 0.6 shard_map.96
  (3 shorter events, 0.1 us)
Async XLA Ops:
  2.4 19.4 %copy-start.2 = (bf16[2,512]{1,0:T(2,128)(2,1)S(1)}, bf16[2,512]{1,0:T(2,128)(2,1)}, u32[]{:S(2)}) copy-start(bf16[2,512]{1,0:T(2,128)(2,1)} %param.5) | copy-start | bytes 6148
  2.4 19.5 %copy-start.1 = (bf16[1024,128]{1,0:T(8,128)(2,1)S(1)}, bf16[1024,128]{1,0:T(8,128)(2,1)}, u32[]{:S(2)}) copy-start(bf16[1024,128]{1,0:T(8,128)(2,1)} %param.8) | copy-start | bytes 786436
  2.4 34.8 %all-to-all-start = ((bf16[128,2,640]{2,1,0:T(2,128)(2,1)}), bf16[128,2,640]{2,1,0:T(2,128)(2,1)S(1)}, u32[]{:S(2)}, u32[]{:S(2)}) async-start(bf16[128,2,640]{2,1,0:T(2,128)(2,1)} %shard_map.92), calls=%async_computation | async-start | bytes 655360 | tf_op jit(solution)/shard_map/all_to_all | solution.py:104
  21.9 0.9 %copy-start = (bf16[2,256,128]{2,1,0:T(8,128)(2,1)S(1)}, bf16[2,256,128]{2,1,0:T(8,128)(2,1)}, u32[]{:S(2)}) copy-start(bf16[2,256,128]{2,1,0:T(8,128)(2,1)} %cotan.3) | copy-start | bytes 393220
  39.3 21.2 %all-to-all-start.1 = ((bf16[64,32,128]{2,1,0:T(8,128)(2,1)}), bf16[64,32,128]{2,1,0:T(8,128)(2,1)S(1)}, u32[]{:S(2)}, u32[]{:S(2)}) async-start(bf16[64,32,128]{2,1,0:T(8,128)(2,1)} %get-tuple-element.16), calls=%async_computation.1 | async-start | bytes 1048576 | tf_op jit(solution)/shard_map/all_to_all | solution.py:131
  46.6 23.7 %collective-permute-start = (f32[2,64,128]{2,1,0:T(8,128)S(1)}, f32[2,64,128]{2,1,0:T(8,128)S(1)}, u32[]{:S(2)}, u32[]{:S(2)}) collective-permute-start(f32[2,64,128]{2,1,0:T(8,128)S(1)} %get-tuple-element.21), channel_id=1, source_target_pairs={{0,1},{1,0},{2,3},{3,2},{4,5},{5,4},{6,7},{7,6},{8,9},{9,8},{10,11... | collective-permute-start | bytes 196616 | tf_op jit(solution)/shard_map/ppermute | solution.py:156
  50.5 19.8 %collective-permute-start.2 = (f32[2,64,128]{2,1,0:T(8,128)S(1)}, f32[2,64,128]{2,1,0:T(8,128)S(1)}, u32[]{:S(2)}, u32[]{:S(2)}) collective-permute-start(f32[2,64,128]{2,1,0:T(8,128)S(1)} %get-tuple-element.22), channel_id=1, source_target_pairs={{0,3},{1,2},{2,1},{3,0},{4,7},{5,6},{6,5},{7,4},{8,11},{9,10},{10,... | collective-permute-start | bytes 196616 | tf_op jit(solution)/shard_map/ppermute | solution.py:156
  54.8 15.5 %collective-permute-start.1 = (f32[2,64,128]{2,1,0:T(8,128)S(1)}, f32[2,64,128]{2,1,0:T(8,128)S(1)}, u32[]{:S(2)}, u32[]{:S(2)}) collective-permute-start(f32[2,64,128]{2,1,0:T(8,128)S(1)} %get-tuple-element.23), channel_id=1, source_target_pairs={{0,2},{1,3},{2,0},{3,1},{4,6},{5,7},{6,4},{7,5},{8,10},{9,11},{10,... | collective-permute-start | bytes 196616 | tf_op jit(solution)/shard_map/ppermute | solution.py:156
  61.2 9.1 %copy-start.3 = (f32[128]{0:T(128)S(1)}, f32[128]{0:T(128)}, u32[]{:S(2)}) copy-start(f32[128]{0:T(128)} %param.9) | copy-start | bytes 1540
  61.2 13.8 %all-to-all-start.2 = ((f32[8,16,128]{2,1,0:T(8,128)}), f32[8,16,128]{2,1,0:T(8,128)S(1)}, u32[]{:S(2)}, u32[]{:S(2)}) async-start(f32[8,16,128]{2,1,0:T(8,128)} %shard_map.95), calls=%async_computation.2 | async-start | bytes 131072 | tf_op jit(solution)/shard_map/all_to_all | solution.py:166

commit v7 on v6

--- a/solution.py
+++ b/solution.py
@@ -31,6 +31,30 @@
     bias = jnp.where(upper, high, total - high).astype(jnp.bfloat16)
     out[:, :, :WIDE] = jnp.broadcast_to(right[...][None], (out.shape[0], ROW_DEV, WIDE))
     out[:, :, WIDE:] = jnp.broadcast_to(bias[None], (out.shape[0], ROW_DEV, P_SIZE))
+
+
+def right_kernel(place, cotan, mixed_hi, mixed_lo, kept, sent):
+    total = jnp.zeros((cotan.shape[1], WIDE), jnp.float32)
+    for i in range(ROW_DEV):
+        for mixed in (mixed_hi, mixed_lo):
+            total += lax.dot_general(cotan[i], mixed[i], (((1,), (1,)), ((), ())), preferred_element_type=jnp.float32)
+    low, high = total[:, : WIDE // 2], total[:, WIDE // 2 :]
+    kept[...] = jnp.where(place[0] == 0, low, high)
+    sent[...] = jnp.where(place[0] == 0, high, low)
+
+
+def packing_kernel(kept, got, out, total):
+    blocks = kept.shape[1] // P_SIZE
+    lines = ROW_DEV * blocks * HALVES
+    planes = out.shape[0] // lines
+    for m in range(blocks):
+        cut = slice(m * P_SIZE, (m + 1) * P_SIZE)
+        total[m] = kept[:, cut] + got[:, cut]
+        for half in range(HALVES):
+            for t in range(ROW_DEV):
+                out[pl.ds((half * ROW_DEV + t) * blocks + m, planes, stride=lines), :] = total[
+                    m, pl.ds(half * planes * ROW_DEV + t, planes, stride=ROW_DEV), :
+                ]
 
 
 def products_kernel(right, cotan, left_cols, grad_right, message, back, weight):
@@ -48,10 +72,9 @@
             lhs, jnp.concatenate(parts, axis=0), preferred_element_type=jnp.float32
         )
     planes = message.shape[0]
-    own = message.shape[1] // 2
-    halves = weight[...].reshape(HALVES, planes, own // HALVES, P_SIZE)
-    message[:, :own, :] = jnp.concatenate([halves[0], halves[1]], axis=1).astype(jnp.bfloat16)
-    message[:, own:, :] = grad_right[...]
+    halves = weight[...].reshape(HALVES, planes, C * C // (HALVES * planes), P_SIZE)
+    own = grad_right[...].reshape(planes, grad_right.shape[0] // planes, P_SIZE)
+    message[...] = jnp.concatenate([halves[0], halves[1], own], axis=1).astype(jnp.bfloat16)
 
 
 def pair_kernel(right, mixed_hi, mixed_lo, back, pair, back_hi, back_lo):
@@ -65,24 +88,28 @@
 
 def middle_kernel(place, parts, out):
     total = jnp.sum(parts[...].astype(jnp.float32), axis=0)
-    rows = total.shape[0] // 4
+    rows = total.shape[0] // 3
     seq = out.shape[0] // HALVES
+    right = total[2 * rows :]
+    swapped = jnp.concatenate([right[rows // 2 :], right[: rows // 2]], axis=0)
     for half in range(HALVES):
         mine = total[half * rows : (half + 1) * rows]
-        right = total[(half + 2) * rows : (half + 3) * rows]
         for q in range(seq):
             out[half * seq + q, :rows] = mine
-            out[half * seq + q, rows:] = jnp.where(place[0] == q, right, 0.0)
+            out[half * seq + q, rows:] = jnp.where(place[0] == q, swapped if half else right, 0.0)
 
 
 def closing_kernel(scale, parts, weight, right):
-    total = jnp.sum(parts[...], axis=0) * scale
     rows = weight.shape[0]
-    weight[...] = total[:rows]
-    for t in range(ROW_DEV):
-        for m in range(rows // ROW_DEV):
-            at = rows + t * (rows // ROW_DEV) + m
-            right[t : t + 1, m * P_SIZE : (m + 1) * P_SIZE] = total[at : at + 1]
+    seq = parts.shape[0] // HALVES
+    sums = [jnp.sum(parts[half * seq : (half + 1) * seq], axis=0) * scale for half in range(HALVES)]
+    weight[...] = sums[0][:rows] + sums[1][:rows]
+    blocks = WIDE // HALVES // P_SIZE
+    for half in range(HALVES):
+        for t in range(ROW_DEV):
+            for m in range(blocks):
+                at, to = rows + t * blocks + m, (half * blocks + m) * P_SIZE
+                right[t : t + 1, to : to + P_SIZE] = sums[half][at : at + 1]
 
 
 def on_device(left_proj, right_proj, pair_cotangent, out_weight, out_bias):
@@ -103,22 +130,38 @@
     )(right_proj, pair_cotangent)
     arrived = lax.all_to_all(opening, ("half", "plane"), 0, 0, tiled=True)
     right_all = arrived[:, :, :WIDE].reshape(columns, WIDE)
-    grad_bias = jnp.sum(arrived[:, :, WIDE:], axis=(0, 1), dtype=jnp.float32)
 
     mixed = dot32("isx,xyk->isyk", left_rows, weight)
     high = lax.reduce_precision(mixed, 8, 7)
     mixed_hi, mixed_lo = high.astype(jnp.bfloat16), (mixed - high).astype(jnp.bfloat16)
-    grad_right = dot32("ijk,isyk->jsy", pair_cotangent, mixed_hi) + dot32("ijk,isyk->jsy", pair_cotangent, mixed_lo)
-    grad_right = grad_right.astype(jnp.bfloat16).reshape(HALVES, planes, rows, P_SIZE)
-    grad_right = jnp.moveaxis(grad_right, 0, 1).reshape(planes, HALVES * rows, P_SIZE)
+    back = (ROW_DEV, WIDE, P_SIZE)
+    mixed_hi, mixed_lo = mixed_hi.reshape(back), mixed_lo.reshape(back)
+    half_wide = jax.ShapeDtypeStruct((columns, WIDE // HALVES), jnp.float32)
+    kept, sent = pl.pallas_call(
+        right_kernel,
+        out_shape=(half_wide, half_wide),
+        in_specs=[pl.BlockSpec(memory_space=pltpu.SMEM)] + [WHOLE] * 3,
+        out_specs=(WHOLE,) * 2,
+        compiler_params=pltpu.CompilerParams(vmem_limit_bytes=16 * 1024 * 1024),
+        cost_estimate=pl.CostEstimate(flops=150_000_000, bytes_accessed=1_000_000, transcendentals=0),
+    )(lax.axis_index("half").reshape(1), pair_cotangent, mixed_hi, mixed_lo)
+    got = lax.ppermute(sent, "half", [(0, 1), (1, 0)])
+    grad_right = pl.pallas_call(
+        packing_kernel,
+        out_shape=jax.ShapeDtypeStruct((columns * WIDE // HALVES // P_SIZE, P_SIZE), jnp.float32),
+        in_specs=[WHOLE] * 2,
+        out_specs=WHOLE,
+        scratch_shapes=[pltpu.VMEM((WIDE // HALVES // P_SIZE, columns, P_SIZE), jnp.float32)],
+        compiler_params=pltpu.CompilerParams(vmem_limit_bytes=16 * 1024 * 1024),
+        cost_estimate=pl.CostEstimate(flops=100_000, bytes_accessed=1_000_000, transcendentals=0),
+    )(kept, got)
     left_cols = jnp.broadcast_to(left_rows.transpose(2, 0, 1)[:, :, None], (C, ROW_DEV, 2, SEQ_DEV))
     left_cols = left_cols.reshape(C, ROW_DEV * 2 * SEQ_DEV)
 
-    back = (ROW_DEV, WIDE, P_SIZE)
     message, terms = pl.pallas_call(
         products_kernel,
         out_shape=(
-            jax.ShapeDtypeStruct((planes, 2 * HALVES * rows, P_SIZE), jnp.bfloat16),
+            jax.ShapeDtypeStruct((planes, 3 * rows, P_SIZE), jnp.bfloat16),
             jax.ShapeDtypeStruct(back, jnp.float32),
         ),
         in_specs=[WHOLE] * 4,
@@ -141,21 +184,21 @@
         out_specs=(WHOLE,) * 3,
         compiler_params=pltpu.CompilerParams(vmem_limit_bytes=16 * 1024 * 1024),
         cost_estimate=pl.CostEstimate(flops=150_000_000, bytes_accessed=2_000_000, transcendentals=0),
-    )(right_all, mixed_hi.reshape(back), mixed_lo.reshape(back), terms)
-    back_hi, back_lo = (term.reshape(ROW_DEV, SEQ_DEV, C, P_SIZE) for term in (back_hi, back_lo))
-    grad_left = dot32("isyk,xyk->isx", back_hi, weight) + dot32("isyk,xyk->isx", back_lo, weight)
+    )(right_all, mixed_hi, mixed_lo, terms)
     cols = columns // seq
     here = lax.axis_index("seq")
 
     def columns_of(owner):
         return lax.dynamic_slice_in_dim(pair, owner * cols, cols, 1)
 
-    pair_sum = columns_of(here)
+    others = []
     for step in range(1, seq):
         sent = columns_of(lax.bitwise_xor(here, jnp.int32(step)))
-        pair_sum = pair_sum + lax.ppermute(sent, "seq", [(q, q ^ step) for q in range(seq)])
-    pair_update = (pair_sum * scale + out_bias).astype(jnp.bfloat16)
-
+        others.append(lax.ppermute(sent, "seq", [(q, q ^ step) for q in range(seq)]))
+
+    parts, arrived, back_hi, back_lo, pair_sum = lax.optimization_barrier(
+        (parts, arrived, back_hi, back_lo, columns_of(here))
+    )
     last = pl.pallas_call(
         middle_kernel,
         out_shape=jax.ShapeDtypeStruct((HALVES * seq, 2 * rows, P_SIZE), jnp.float32),
@@ -174,6 +217,12 @@
         out_specs=(WHOLE,) * 2,
         compiler_params=pltpu.CompilerParams(vmem_limit_bytes=8 * 1024 * 1024),
     )(last)
+    for other in others:
+        pair_sum = pair_sum + other
+    pair_update = (pair_sum * scale + out_bias).astype(jnp.bfloat16)
+    back_hi, back_lo = (term.reshape(ROW_DEV, SEQ_DEV, C, P_SIZE) for term in (back_hi, back_lo))
+    grad_left = dot32("isyk,xyk->isx", back_hi, weight) + dot32("isyk,xyk->isx", back_lo, weight)
+    grad_bias = jnp.sum(arrived[:, :, WIDE:], axis=(0, 1), dtype=jnp.float32)
     return pair_update, (grad_left * scale).reshape(ROW_DEV, WIDE), grad_right, grad_weight, grad_bias
 
 

time: 76 us -> 77.3 us (1.017)
  starting transfers between devices: 44.6 us -> 49.9 us
  waiting for transfers between devices: 18.9 us -> 15.7 us
  local copies, waits for them, and re-layouts: 3.38 us -> 2.57 us
    all_to_all x1, waiting for transfers between devices: 12.3 us -> 1.64 us  [on_device(): arrived = lax.all_to_all(opening, ('half', 'plane'), 0, 0, tiled=True)]
    ppermute x0 -> x1, waiting for transfers between devices: none -> 8.86 us  [on_device(): got = lax.ppermute(sent, 'half', [(0, 1), (1, 0)])]
    all_to_all x1, starting transfers between devices: 5.46 us -> 9.07 us  [on_device(): parts = lax.all_to_all(message, 'plane', 0, 0, tiled=True)]
    ppermute x0 -> x1, starting transfers between devices: none -> 2.8 us  [on_device(): got = lax.ppermute(sent, 'half', [(0, 1), (1, 0)])]
    all_to_all x1, waiting for transfers between devices: 4.02 us -> 2.06 us  [on_device(): last = lax.all_to_all(last, ('half', 'seq'), 0, 0, tiled=True)]
    convert_element_type x1 -> x0, local copies, waits for them, and re-layouts: 0.95 us -> none  [on_device(): grad_right.astype(jnp.bfloat16).reshape(HALVES, planes, rows, P_SIZE)]
    all_to_all x1, starting transfers between devices: 9.11 us -> 8.2 us  [on_device(): last = lax.all_to_all(last, ('half', 'seq'), 0, 0, tiled=True)]
  transfers between devices with their start and end apart: 6 -> 7, of which waited for: 3 -> 4; matrix products, arithmetic and copies ran while one was open for 7% -> 4% of each run, Pallas kernels for 2% -> 2%
where the time goes in v7:
time: 77.3 us; the launch traced here: 76.8 us
  starting transfers between devices  49.9 us (65%)
  waiting for transfers between devices  15.7 us (20%)
  Pallas kernels  5.8 us (8%)
  local copies, waits for them, and re-layouts  2.57 us (3%)
  other arithmetic  1.3 us (2%)
  between operations  0.82 us (1%)
    all_to_all x1, starting transfers between devices, on_device(): arrived = lax.all_to_all(opening, ('half', 'plane'), 0, 0, tiled=True)  19.4 us
    ppermute x3, starting transfers between devices, on_device(): lax.ppermute(sent, 'seq', [(q, q ^ step) for q in range(seq)])  10.4 us
    all_to_all x1, starting transfers between devices, on_device(): parts = lax.all_to_all(message, 'plane', 0, 0, tiled=True)  9.07 us
    ppermute x1, waiting for transfers between devices, on_device(): got = lax.ppermute(sent, 'half', [(0, 1), (1, 0)])  8.86 us
    all_to_all x1, starting transfers between devices, on_device(): last = lax.all_to_all(last, ('half', 'seq'), 0, 0, tiled=True)  8.2 us
    all_to_all x1, waiting for transfers between devices, on_device(): parts = lax.all_to_all(message, 'plane', 0, 0, tiled=True)  3.14 us
    ppermute x1, starting transfers between devices, on_device(): got = lax.ppermute(sent, 'half', [(0, 1), (1, 0)])  2.8 us
    all_to_all x1, waiting for transfers between devices, on_device(): last = lax.all_to_all(last, ('half', 'seq'), 0, 0, tiled=True)  2.06 us
  transfers between devices with their start and end apart: 7, of which 4 were waited for; matrix products, arithmetic and copies ran while one was open for 4% of the time, Pallas kernels for 2%

profile of v7, /device:TPU:1, one launch (start us, length us, event | category | flops | bytes accessed | tf_op | source)
XLA Modules:
  0.0 76.8 jit_solution(2797581224874936747)
XLA Ops:
  0.6 1.8 %shard_map.92 = bf16[128,2,640]{2,1,0:T(2,128)(2,1)} custom-call(bf16[2,512]{1,0:T(2,128)(2,1)} %right.1, bf16[2,256,128]{2,1,0:T(8,128)(2,1)} %cotan.5), custom_call_target="tpu_custom_call" | custom-call | tf_op jit(solution)/shard_map/pallas_call | solution.py:125
  2.4 0.0 copy-start.2
  2.4 0.0 copy-start.1
  2.4 19.4 %all-to-all-start = ((bf16[128,2,640]{2,1,0:T(2,128)(2,1)}), bf16[128,2,640]{2,1,0:T(2,128)(2,1)S(1)}, u32[]{:S(2)}, u32[]{:S(2)}) async-start(bf16[128,2,640]{2,1,0:T(2,128)(2,1)} %shard_map.92), calls=%async_computation | async-start | bytes 655360 | tf_op jit(solution)/shard_map/all_to_all | solution.py:131
  21.8 0.0 copy-done.2
  21.8 0.1 reshape.56
  21.9 0.0 copy-done.1
  21.9 0.2 fusion.2
  22.2 0.1 copy.19
  22.2 0.0 copy-start
  22.2 0.1 copy.20
  22.3 0.8 %copy-done = bf16[2,256,128]{2,1,0:T(8,128)(2,1)S(1)} copy-done((bf16[2,256,128]{2,1,0:T(8,128)(2,1)S(1)}, bf16[2,256,128]{2,1,0:T(8,128)(2,1)}, u32[]{:S(2)}) %copy-start) | copy-done | bytes 131096
  23.1 0.4 shard_map.93
  23.6 2.8 %collective-permute-start = (f32[256,256]{1,0:T(8,128)S(1)}, f32[256,256]{1,0:T(8,128)S(1)}, u32[]{:S(2)}, u32[]{:S(2)}) collective-permute-start(f32[256,256]{1,0:T(8,128)S(1)} %get-tuple-element.20), channel_id=1, source_target_pairs={{0,256},{256,0},{1,257},{257,1},{2,258},{258,2},{3,259},{259,3},{4... | collective-permute-start | bytes 786440 | tf_op jit(solution)/shard_map/ppermute | solution.py:148
  26.4 0.1 reshape.46
  26.5 0.1 copy.21.left_cols
  26.6 8.9 %collective-permute-done.got = f32[256,256]{1,0:T(8,128)S(1)} collective-permute-done((f32[256,256]{1,0:T(8,128)S(1)}, f32[256,256]{1,0:T(8,128)S(1)}, u32[]{:S(2)}, u32[]{:S(2)}) %collective-permute-start) | collective-permute-done | bytes 262176 | tf_op jit(solution)/shard_map/ppermute | solution.py:148
  35.4 0.1 shard_map.94.grad_right
  35.5 1.6 %all-to-all-done = bf16[128,2,640]{2,1,0:T(2,128)(2,1)S(1)} async-done(((bf16[128,2,640]{2,1,0:T(2,128)(2,1)}), bf16[128,2,640]{2,1,0:T(2,128)(2,1)S(1)}, u32[]{:S(2)}, u32[]{:S(2)}) %all-to-all-start) | async-done | bytes 327712 | tf_op jit(solution)/shard_map/all_to_all | solution.py:131
  37.1 0.2 slice.8
  37.3 0.1 reshape.45.right
  37.4 1.8 %shard_map.95 = (bf16[64,24,128]{2,1,0:T(8,128)(2,1)}, f32[2,512,128]{2,1,0:T(8,128)S(1)}) custom-call(bf16[256,512]{1,0:T(8,128)(2,1)S(1)} %reshape.45.right, bf16[2,256,128]{2,1,0:T(8,128)(2,1)S(1)} %copy-done, bf16[32,64]{1,0:T(8,128)(2,1)S(1)} %copy.21.left_cols, f32[512,128]{1,0:T(8,128)S(1)} %shard_map.94.grad_right), custom_call_target="tpu_custom_call" | custom-call | flops 200000000 | bytes 2000000 | tf_op jit(solution)/shard_map/pallas_call | solution.py:161
  39.2 9.1 %all-to-all-start.1 = ((bf16[64,24,128]{2,1,0:T(8,128)(2,1)}), bf16[64,24,128]{2,1,0:T(8,128)(2,1)S(1)}, u32[]{:S(2)}, u32[]{:S(2)}) async-start(bf16[64,24,128]{2,1,0:T(8,128)(2,1)} %get-tuple-element.21), calls=%async_computation.1 | async-start | bytes 786432 | tf_op jit(solution)/shard_map/all_to_all | solution.py:174
  48.3 0.4 shard_map.96
  48.8 3.4 %collective-permute-start.1 = (f32[2,64,128]{2,1,0:T(8,128)S(1)}, f32[2,64,128]{2,1,0:T(8,128)S(1)}, u32[]{:S(2)}, u32[]{:S(2)}) collective-permute-start(f32[2,64,128]{2,1,0:T(8,128)S(1)} %get-tuple-element.35), channel_id=1, source_target_pairs={{0,1},{1,0},{2,3},{3,2},{4,5},{5,4},{6,7},{7,6},{8,9},{9,8},{10,11... | collective-permute-start | bytes 196616 | tf_op jit(solution)/shard_map/ppermute | solution.py:197
  52.2 4.4 %collective-permute-start.2 = (f32[2,64,128]{2,1,0:T(8,128)S(1)}, f32[2,64,128]{2,1,0:T(8,128)S(1)}, u32[]{:S(2)}, u32[]{:S(2)}) collective-permute-start(f32[2,64,128]{2,1,0:T(8,128)S(1)} %get-tuple-element.37), channel_id=1, source_target_pairs={{0,2},{1,3},{2,0},{3,1},{4,6},{5,7},{6,4},{7,5},{8,10},{9,11},{10,... | collective-permute-start | bytes 196616 | tf_op jit(solution)/shard_map/ppermute | solution.py:197
  56.6 2.6 %collective-permute-start.3 = (f32[2,64,128]{2,1,0:T(8,128)S(1)}, f32[2,64,128]{2,1,0:T(8,128)S(1)}, u32[]{:S(2)}, u32[]{:S(2)}) collective-permute-start(f32[2,64,128]{2,1,0:T(8,128)S(1)} %get-tuple-element.36), channel_id=1, source_target_pairs={{0,3},{1,2},{2,1},{3,0},{4,7},{5,6},{6,5},{7,4},{8,11},{9,10},{10,... | collective-permute-start | bytes 196616 | tf_op jit(solution)/shard_map/ppermute | solution.py:197
  59.2 3.1 %all-to-all-done.1.parts = bf16[64,24,128]{2,1,0:T(8,128)(2,1)S(1)} async-done(((bf16[64,24,128]{2,1,0:T(8,128)(2,1)}), bf16[64,24,128]{2,1,0:T(8,128)(2,1)S(1)}, u32[]{:S(2)}, u32[]{:S(2)}) %all-to-all-start.1) | async-done | bytes 393248 | tf_op jit(solution)/shard_map/all_to_all | solution.py:174
  62.4 0.3 convolution_bitcast_fusion
  62.6 0.7 shard_map.97
  63.3 8.2 %all-to-all-start.2 = ((f32[8,16,128]{2,1,0:T(8,128)}), f32[8,16,128]{2,1,0:T(8,128)S(1)}, u32[]{:S(2)}, u32[]{:S(2)}) async-start(f32[8,16,128]{2,1,0:T(8,128)} %shard_map.97), calls=%async_computation.2 | async-start | bytes 131072 | tf_op jit(solution)/shard_map/all_to_all | solution.py:209
  71.5 0.0 copy-start.3
  71.5 0.3 fusion.1
  71.8 0.0 collective-permute-done.1
  71.8 0.0 collective-permute-done.2
  71.8 0.0 collective-permute-done.3
  71.8 0.4 copy-done.3
  72.2 0.6 add_convert_fusion
  72.8 0.7 convert_reduce_fusion
  73.5 0.7 reshape.54
  74.2 2.1 %all-to-all-done.2.refs_0_ = f32[8,16,128]{2,1,0:T(8,128)S(1)} async-done(((f32[8,16,128]{2,1,0:T(8,128)}), f32[8,16,128]{2,1,0:T(8,128)S(1)}, u32[]{:S(2)}, u32[]{:S(2)}) %all-to-all-start.2) | async-done | bytes 65568 | tf_op jit(solution)/shard_map/all_to_all | solution.py:209
  76.2 0.6 shard_map.98
  (2 shorter events, 0.0 us)
Async XLA Ops:
  2.4 19.4 %copy-start.2 = (bf16[2,512]{1,0:T(2,128)(2,1)S(1)}, bf16[2,512]{1,0:T(2,128)(2,1)}, u32[]{:S(2)}) copy-start(bf16[2,512]{1,0:T(2,128)(2,1)} %param.5) | copy-start | bytes 6148
  2.4 19.5 %copy-start.1 = (bf16[1024,128]{1,0:T(8,128)(2,1)S(1)}, bf16[1024,128]{1,0:T(8,128)(2,1)}, u32[]{:S(2)}) copy-start(bf16[1024,128]{1,0:T(8,128)(2,1)} %param.8) | copy-start | bytes 786436
  2.4 34.8 %all-to-all-start = ((bf16[128,2,640]{2,1,0:T(2,128)(2,1)}), bf16[128,2,640]{2,1,0:T(2,128)(2,1)S(1)}, u32[]{:S(2)}, u32[]{:S(2)}) async-start(bf16[128,2,640]{2,1,0:T(2,128)(2,1)} %shard_map.92), calls=%async_computation | async-start | bytes 655360 | tf_op jit(solution)/shard_map/all_to_all | solution.py:131
  22.2 0.9 %copy-start = (bf16[2,256,128]{2,1,0:T(8,128)(2,1)S(1)}, bf16[2,256,128]{2,1,0:T(8,128)(2,1)}, u32[]{:S(2)}) copy-start(bf16[2,256,128]{2,1,0:T(8,128)(2,1)} %cotan.5) | copy-start | bytes 393220
  23.6 11.8 %collective-permute-start = (f32[256,256]{1,0:T(8,128)S(1)}, f32[256,256]{1,0:T(8,128)S(1)}, u32[]{:S(2)}, u32[]{:S(2)}) collective-permute-start(f32[256,256]{1,0:T(8,128)S(1)} %get-tuple-element.20), channel_id=1, source_target_pairs={{0,256},{256,0},{1,257},{257,1},{2,258},{258,2},{3,259},{259,3},{4... | collective-permute-start | bytes 786440 | tf_op jit(solution)/shard_map/ppermute | solution.py:148
  39.2 23.1 %all-to-all-start.1 = ((bf16[64,24,128]{2,1,0:T(8,128)(2,1)}), bf16[64,24,128]{2,1,0:T(8,128)(2,1)S(1)}, u32[]{:S(2)}, u32[]{:S(2)}) async-start(bf16[64,24,128]{2,1,0:T(8,128)(2,1)} %get-tuple-element.21), calls=%async_computation.1 | async-start | bytes 786432 | tf_op jit(solution)/shard_map/all_to_all | solution.py:174
  48.8 23.0 %collective-permute-start.1 = (f32[2,64,128]{2,1,0:T(8,128)S(1)}, f32[2,64,128]{2,1,0:T(8,128)S(1)}, u32[]{:S(2)}, u32[]{:S(2)}) collective-permute-start(f32[2,64,128]{2,1,0:T(8,128)S(1)} %get-tuple-element.35), channel_id=1, source_target_pairs={{0,1},{1,0},{2,3},{3,2},{4,5},{5,4},{6,7},{7,6},{8,9},{9,8},{10,11... | collective-permute-start | bytes 196616 | tf_op jit(solution)/shard_map/ppermute | solution.py:197
  52.2 19.6 %collective-permute-start.2 = (f32[2,64,128]{2,1,0:T(8,128)S(1)}, f32[2,64,128]{2,1,0:T(8,128)S(1)}, u32[]{:S(2)}, u32[]{:S(2)}) collective-permute-start(f32[2,64,128]{2,1,0:T(8,128)S(1)} %get-tuple-element.37), channel_id=1, source_target_pairs={{0,2},{1,3},{2,0},{3,1},{4,6},{5,7},{6,4},{7,5},{8,10},{9,11},{10,... | collective-permute-start | bytes 196616 | tf_op jit(solution)/shard_map/ppermute | solution.py:197
  56.6 15.2 %collective-permute-start.3 = (f32[2,64,128]{2,1,0:T(8,128)S(1)}, f32[2,64,128]{2,1,0:T(8,128)S(1)}, u32[]{:S(2)}, u32[]{:S(2)}) collective-permute-start(f32[2,64,128]{2,1,0:T(8,128)S(1)} %get-tuple-element.36), channel_id=1, source_target_pairs={{0,3},{1,2},{2,1},{3,0},{4,7},{5,6},{6,5},{7,4},{8,11},{9,10},{10,... | collective-permute-start | bytes 196616 | tf_op jit(solution)/shard_map/ppermute | solution.py:197
  63.3 12.9 %all-to-all-start.2 = ((f32[8,16,128]{2,1,0:T(8,128)}), f32[8,16,128]{2,1,0:T(8,128)S(1)}, u32[]{:S(2)}, u32[]{:S(2)}) async-start(f32[8,16,128]{2,1,0:T(8,128)} %shard_map.97), calls=%async_computation.2 | async-start | bytes 131072 | tf_op jit(solution)/shard_map/all_to_all | solution.py:209
  71.5 0.7 copy-start.3

commit v8 on v7

--- a/solution.py
+++ b/solution.py
@@ -24,13 +24,8 @@
     return jnp.einsum(form, a, b, preferred_element_type=jnp.float32)
 
 
-def opening_kernel(right, cotan, out):
-    total = jnp.sum(cotan[...].astype(jnp.float32), axis=(0, 1))[None]
-    high = total.astype(jnp.bfloat16).astype(jnp.float32)
-    upper = lax.broadcasted_iota(jnp.int32, (ROW_DEV, P_SIZE), 0) == 0
-    bias = jnp.where(upper, high, total - high).astype(jnp.bfloat16)
-    out[:, :, :WIDE] = jnp.broadcast_to(right[...][None], (out.shape[0], ROW_DEV, WIDE))
-    out[:, :, WIDE:] = jnp.broadcast_to(bias[None], (out.shape[0], ROW_DEV, P_SIZE))
+def opening_kernel(right, out):
+    out[...] = jnp.broadcast_to(right[...][None], out.shape)
 
 
 def right_kernel(place, cotan, mixed_hi, mixed_lo, kept, sent):
@@ -40,7 +35,7 @@
             total += lax.dot_general(cotan[i], mixed[i], (((1,), (1,)), ((), ())), preferred_element_type=jnp.float32)
     low, high = total[:, : WIDE // 2], total[:, WIDE // 2 :]
     kept[...] = jnp.where(place[0] == 0, low, high)
-    sent[...] = jnp.where(place[0] == 0, high, low)
+    sent[...] = jnp.where(place[0] == 0, high, low).astype(jnp.bfloat16)
 
 
 def packing_kernel(kept, got, out, total):
@@ -49,7 +44,7 @@
     planes = out.shape[0] // lines
     for m in range(blocks):
         cut = slice(m * P_SIZE, (m + 1) * P_SIZE)
-        total[m] = kept[:, cut] + got[:, cut]
+        total[m] = kept[:, cut] + got[:, cut].astype(jnp.float32)
         for half in range(HALVES):
             for t in range(ROW_DEV):
                 out[pl.ds((half * ROW_DEV + t) * blocks + m, planes, stride=lines), :] = total[
@@ -74,7 +69,13 @@
     planes = message.shape[0]
     halves = weight[...].reshape(HALVES, planes, C * C // (HALVES * planes), P_SIZE)
     own = grad_right[...].reshape(planes, grad_right.shape[0] // planes, P_SIZE)
-    message[...] = jnp.concatenate([halves[0], halves[1], own], axis=1).astype(jnp.bfloat16)
+    total = jnp.sum(both.astype(jnp.float32), axis=0, keepdims=True)
+    total = total[:, :P_SIZE] + total[:, P_SIZE:]
+    high = total.astype(jnp.bfloat16).astype(jnp.float32)
+    line = lax.broadcasted_iota(jnp.int32, halves.shape[2:], 0)
+    bias = jnp.where(line == 0, high, jnp.where(line == 1, total - high, 0.0))
+    bias = jnp.broadcast_to(bias[None], halves.shape[1:])
+    message[...] = jnp.concatenate([halves[0], halves[1], own, bias], axis=1).astype(jnp.bfloat16)
 
 
 def pair_kernel(right, mixed_hi, mixed_lo, back, pair, back_hi, back_lo):
@@ -88,22 +89,25 @@
 
 def middle_kernel(place, parts, out):
     total = jnp.sum(parts[...].astype(jnp.float32), axis=0)
-    rows = total.shape[0] // 3
+    rows = total.shape[0] // 4
     seq = out.shape[0] // HALVES
-    right = total[2 * rows :]
-    swapped = jnp.concatenate([right[rows // 2 :], right[: rows // 2]], axis=0)
+    right, bias = total[2 * rows : 3 * rows], total[3 * rows : 3 * rows + rows // 2]
+    rights = [right[: rows // 2], right[rows // 2 :]]
     for half in range(HALVES):
         mine = total[half * rows : (half + 1) * rows]
         for q in range(seq):
             out[half * seq + q, :rows] = mine
-            out[half * seq + q, rows:] = jnp.where(place[0] == q, swapped if half else right, 0.0)
-
-
-def closing_kernel(scale, parts, weight, right):
+            mine_too = jnp.where(place[0] == q, rights[half], 0.0)
+            out[half * seq + q, rows:] = jnp.concatenate([mine_too, bias], axis=0)
+
+
+def closing_kernel(scale, parts, weight, right, bias):
     rows = weight.shape[0]
     seq = parts.shape[0] // HALVES
     sums = [jnp.sum(parts[half * seq : (half + 1) * seq], axis=0) * scale for half in range(HALVES)]
     weight[...] = sums[0][:rows] + sums[1][:rows]
+    pieces = (sums[0] + sums[1])[rows + rows // 2 :]
+    bias[...] = (pieces[0:1] + pieces[1:2]) * (1.0 / (scale * seq))
     blocks = WIDE // HALVES // P_SIZE
     for half in range(HALVES):
         for t in range(ROW_DEV):
@@ -124,12 +128,12 @@
 
     opening = pl.pallas_call(
         opening_kernel,
-        out_shape=jax.ShapeDtypeStruct((res, ROW_DEV, WIDE + P_SIZE), jnp.bfloat16),
-        in_specs=[WHOLE] * 2,
+        out_shape=jax.ShapeDtypeStruct((res, ROW_DEV, WIDE), jnp.bfloat16),
+        in_specs=[WHOLE],
         out_specs=WHOLE,
-    )(right_proj, pair_cotangent)
+    )(right_proj)
     arrived = lax.all_to_all(opening, ("half", "plane"), 0, 0, tiled=True)
-    right_all = arrived[:, :, :WIDE].reshape(columns, WIDE)
+    right_all = arrived.reshape(columns, WIDE)
 
     mixed = dot32("isx,xyk->isyk", left_rows, weight)
     high = lax.reduce_precision(mixed, 8, 7)
@@ -139,7 +143,7 @@
     half_wide = jax.ShapeDtypeStruct((columns, WIDE // HALVES), jnp.float32)
     kept, sent = pl.pallas_call(
         right_kernel,
-        out_shape=(half_wide, half_wide),
+        out_shape=(half_wide, jax.ShapeDtypeStruct(half_wide.shape, jnp.bfloat16)),
         in_specs=[pl.BlockSpec(memory_space=pltpu.SMEM)] + [WHOLE] * 3,
         out_specs=(WHOLE,) * 2,
         compiler_params=pltpu.CompilerParams(vmem_limit_bytes=16 * 1024 * 1024),
@@ -161,7 +165,7 @@
     message, terms = pl.pallas_call(
         products_kernel,
         out_shape=(
-            jax.ShapeDtypeStruct((planes, 3 * rows, P_SIZE), jnp.bfloat16),
+            jax.ShapeDtypeStruct((planes, 4 * rows, P_SIZE), jnp.bfloat16),
             jax.ShapeDtypeStruct(back, jnp.float32),
         ),
         in_specs=[WHOLE] * 4,
@@ -196,9 +200,7 @@
         sent = columns_of(lax.bitwise_xor(here, jnp.int32(step)))
         others.append(lax.ppermute(sent, "seq", [(q, q ^ step) for q in range(seq)]))
 
-    parts, arrived, back_hi, back_lo, pair_sum = lax.optimization_barrier(
-        (parts, arrived, back_hi, back_lo, columns_of(here))
-    )
+    parts, back_hi, back_lo, pair_sum = lax.optimization_barrier((parts, back_hi, back_lo, columns_of(here)))
     last = pl.pallas_call(
         middle_kernel,
         out_shape=jax.ShapeDtypeStruct((HALVES * seq, 2 * rows, P_SIZE), jnp.float32),
@@ -207,14 +209,15 @@
         compiler_params=pltpu.CompilerParams(vmem_limit_bytes=8 * 1024 * 1024),
     )(here.reshape(1), parts)
     last = lax.all_to_all(last, ("half", "seq"), 0, 0, tiled=True)
-    grad_weight, grad_right = pl.pallas_call(
+    grad_weight, grad_right, grad_bias = pl.pallas_call(
         lambda *refs: closing_kernel(scale, *refs),
         out_shape=(
             jax.ShapeDtypeStruct((rows, P_SIZE), jnp.float32),
             jax.ShapeDtypeStruct((ROW_DEV, WIDE), jnp.float32),
+            jax.ShapeDtypeStruct((1, P_SIZE), jnp.float32),
         ),
         in_specs=[WHOLE],
-        out_specs=(WHOLE,) * 2,
+        out_specs=(WHOLE,) * 3,
         compiler_params=pltpu.CompilerParams(vmem_limit_bytes=8 * 1024 * 1024),
     )(last)
     for other in others:
@@ -222,8 +225,7 @@
     pair_update = (pair_sum * scale + out_bias).astype(jnp.bfloat16)
     back_hi, back_lo = (term.reshape(ROW_DEV, SEQ_DEV, C, P_SIZE) for term in (back_hi, back_lo))
     grad_left = dot32("isyk,xyk->isx", back_hi, weight) + dot32("isyk,xyk->isx", back_lo, weight)
-    grad_bias = jnp.sum(arrived[:, :, WIDE:], axis=(0, 1), dtype=jnp.float32)
-    return pair_update, (grad_left * scale).reshape(ROW_DEV, WIDE), grad_right, grad_weight, grad_bias
+    return pair_update, (grad_left * scale).reshape(ROW_DEV, WIDE), grad_right, grad_weight, grad_bias[0]
 
 
 def solution(mesh):

time: 77.3 us -> 75.6 us (0.978)
  starting transfers between devices: 49.9 us -> 47.7 us
  waiting for transfers between devices: 15.7 us -> 17.3 us
    ppermute x1, waiting for transfers between devices: 8.86 us -> 4.56 us  [on_device(): got = lax.ppermute(sent, 'half', [(0, 1), (1, 0)])]
    all_to_all x1, waiting for transfers between devices: 1.64 us -> 4.75 us  [on_device(): arrived = lax.all_to_all(opening, ('half', 'plane'), 0, 0, tiled=True)]
    all_to_all x1, starting transfers between devices: 9.07 us -> 6.7 us  [on_device(): parts = lax.all_to_all(message, 'plane', 0, 0, tiled=True)]
    all_to_all x1, waiting for transfers between devices: 3.14 us -> 5.25 us  [on_device(): parts = lax.all_to_all(message, 'plane', 0, 0, tiled=True)]
  transfers between devices with their start and end apart: 7 -> 7, of which waited for: 4 -> 4; matrix products, arithmetic and copies ran while one was open for 4% -> 3% of each run, Pallas kernels for 2% -> 2%
where the time goes in v8:
time: 75.6 us; the launch traced here: 75.1 us
  starting transfers between devices  47.7 us (63%)
  waiting for transfers between devices  17.3 us (23%)
  Pallas kernels  5.53 us (7%)
  local copies, waits for them, and re-layouts  2.39 us (3%)
  between operations  0.82 us (1%)
    all_to_all x1, starting transfers between devices, on_device(): arrived = lax.all_to_all(opening, ('half', 'plane'), 0, 0, tiled=True)  19.4 us
    ppermute x3, starting transfers between devices, on_device(): lax.ppermute(sent, 'seq', [(q, q ^ step) for q in range(seq)])  10.5 us
    all_to_all x1, starting transfers between devices, on_device(): last = lax.all_to_all(last, ('half', 'seq'), 0, 0, tiled=True)  8.28 us
    all_to_all x1, starting transfers between devices, on_device(): parts = lax.all_to_all(message, 'plane', 0, 0, tiled=True)  6.7 us
    all_to_all x1, waiting for transfers between devices, on_device(): parts = lax.all_to_all(message, 'plane', 0, 0, tiled=True)  5.25 us
    all_to_all x1, waiting for transfers between devices, on_device(): arrived = lax.all_to_all(opening, ('half', 'plane'), 0, 0, tiled=True)  4.75 us
    ppermute x1, waiting for transfers between devices, on_device(): got = lax.ppermute(sent, 'half', [(0, 1), (1, 0)])  4.56 us
    ppermute x1, starting transfers between devices, on_device(): got = lax.ppermute(sent, 'half', [(0, 1), (1, 0)])  2.8 us
  transfers between devices with their start and end apart: 7, of which 4 were waited for; matrix products, arithmetic and copies ran while one was open for 3% of the time, Pallas kernels for 2%

profile of v8, /device:TPU:1, one launch (start us, length us, event | category | flops | bytes accessed | tf_op | source)
XLA Modules:
  0.0 75.1 jit_solution(18358092618950595716)
XLA Ops:
  0.6 1.4 %shard_map.92 = bf16[128,2,512]{2,1,0:T(2,128)(2,1)} custom-call(bf16[2,512]{1,0:T(2,128)(2,1)} %right.1), custom_call_target="tpu_custom_call" | custom-call | tf_op jit(solution)/shard_map/pallas_call | solution.py:129
  2.0 0.0 copy-start.2
  2.0 0.0 copy-start.1
  2.0 19.4 %all-to-all-start = ((bf16[128,2,512]{2,1,0:T(2,128)(2,1)}), bf16[128,2,512]{2,1,0:T(2,128)(2,1)S(1)}, u32[]{:S(2)}, u32[]{:S(2)}) async-start(bf16[128,2,512]{2,1,0:T(2,128)(2,1)} %shard_map.92), calls=%async_computation | async-start | bytes 524288 | tf_op jit(solution)/shard_map/all_to_all | solution.py:135
  21.5 0.0 copy-done.2
  21.5 0.1 reshape.56
  21.6 0.0 copy-done.1
  21.6 0.2 fusion.2
  21.8 0.1 copy.19
  21.9 0.0 copy-start
  21.9 0.1 copy.20
  22.0 0.8 %copy-done = bf16[2,256,128]{2,1,0:T(8,128)(2,1)S(1)} copy-done((bf16[2,256,128]{2,1,0:T(8,128)(2,1)S(1)}, bf16[2,256,128]{2,1,0:T(8,128)(2,1)}, u32[]{:S(2)}) %copy-start) | copy-done | bytes 131096
  22.8 0.4 shard_map.93
  23.2 2.8 %collective-permute-start = (bf16[256,256]{1,0:T(8,128)(2,1)S(1)}, bf16[256,256]{1,0:T(8,128)(2,1)S(1)}, u32[]{:S(2)}, u32[]{:S(2)}) collective-permute-start(bf16[256,256]{1,0:T(8,128)(2,1)S(1)} %get-tuple-element.20), channel_id=1, source_target_pairs={{0,256},{256,0},{1,257},{257,1},{2,258},{258,2},{3,259},{259,3},{4... | collective-permute-start | bytes 393224 | tf_op jit(solution)/shard_map/ppermute | solution.py:152
  26.0 0.1 reshape.46
  26.1 0.1 copy.21.left_cols
  26.2 4.6 %collective-permute-done.got = bf16[256,256]{1,0:T(8,128)(2,1)S(1)} collective-permute-done((bf16[256,256]{1,0:T(8,128)(2,1)S(1)}, bf16[256,256]{1,0:T(8,128)(2,1)S(1)}, u32[]{:S(2)}, u32[]{:S(2)}) %collective-permute-start) | collective-permute-done | bytes 131104 | tf_op jit(solution)/shard_map/ppermute | solution.py:152
  30.8 0.1 shard_map.94.grad_right
  30.9 4.8 %all-to-all-done = bf16[128,2,512]{2,1,0:T(2,128)(2,1)S(1)} async-done(((bf16[128,2,512]{2,1,0:T(2,128)(2,1)}), bf16[128,2,512]{2,1,0:T(2,128)(2,1)S(1)}, u32[]{:S(2)}, u32[]{:S(2)}) %all-to-all-start) | async-done | bytes 262176 | tf_op jit(solution)/shard_map/all_to_all | solution.py:135
  35.6 0.1 reshape.45.right
  35.7 1.8 %shard_map.95 = (bf16[64,32,128]{2,1,0:T(8,128)(2,1)}, f32[2,512,128]{2,1,0:T(8,128)S(1)}) custom-call(bf16[256,512]{1,0:T(8,128)(2,1)S(1)} %reshape.45.right, bf16[2,256,128]{2,1,0:T(8,128)(2,1)S(1)} %copy-done, bf16[32,64]{1,0:T(8,128)(2,1)S(1)} %copy.21.left_cols, f32[512,128]{1,0:T(8,128)S(1)} %shard_map.94.grad_right), custom_call_target="tpu_custom_call" | custom-call | flops 200000000 | bytes 2000000 | tf_op jit(solution)/shard_map/pallas_call | solution.py:165
  37.5 6.7 %all-to-all-start.1 = ((bf16[64,32,128]{2,1,0:T(8,128)(2,1)}), bf16[64,32,128]{2,1,0:T(8,128)(2,1)S(1)}, u32[]{:S(2)}, u32[]{:S(2)}) async-start(bf16[64,32,128]{2,1,0:T(8,128)(2,1)} %get-tuple-element.21), calls=%async_computation.1 | async-start | bytes 1048576 | tf_op jit(solution)/shard_map/all_to_all | solution.py:178
  44.3 0.4 shard_map.96
  44.8 3.5 %collective-permute-start.1 = (f32[2,64,128]{2,1,0:T(8,128)S(1)}, f32[2,64,128]{2,1,0:T(8,128)S(1)}, u32[]{:S(2)}, u32[]{:S(2)}) collective-permute-start(f32[2,64,128]{2,1,0:T(8,128)S(1)} %get-tuple-element.35), channel_id=1, source_target_pairs={{0,1},{1,0},{2,3},{3,2},{4,5},{5,4},{6,7},{7,6},{8,9},{9,8},{10,11... | collective-permute-start | bytes 196616 | tf_op jit(solution)/shard_map/ppermute | solution.py:201
  48.3 4.4 %collective-permute-start.2 = (f32[2,64,128]{2,1,0:T(8,128)S(1)}, f32[2,64,128]{2,1,0:T(8,128)S(1)}, u32[]{:S(2)}, u32[]{:S(2)}) collective-permute-start(f32[2,64,128]{2,1,0:T(8,128)S(1)} %get-tuple-element.37), channel_id=1, source_target_pairs={{0,2},{1,3},{2,0},{3,1},{4,6},{5,7},{6,4},{7,5},{8,10},{9,11},{10,... | collective-permute-start | bytes 196616 | tf_op jit(solution)/shard_map/ppermute | solution.py:201
  52.7 2.6 %collective-permute-start.3 = (f32[2,64,128]{2,1,0:T(8,128)S(1)}, f32[2,64,128]{2,1,0:T(8,128)S(1)}, u32[]{:S(2)}, u32[]{:S(2)}) collective-permute-start(f32[2,64,128]{2,1,0:T(8,128)S(1)} %get-tuple-element.36), channel_id=1, source_target_pairs={{0,3},{1,2},{2,1},{3,0},{4,7},{5,6},{6,5},{7,4},{8,11},{9,10},{10,... | collective-permute-start | bytes 196616 | tf_op jit(solution)/shard_map/ppermute | solution.py:201
  55.3 5.2 %all-to-all-done.1.parts = bf16[64,32,128]{2,1,0:T(8,128)(2,1)S(1)} async-done(((bf16[64,32,128]{2,1,0:T(8,128)(2,1)}), bf16[64,32,128]{2,1,0:T(8,128)(2,1)S(1)}, u32[]{:S(2)}, u32[]{:S(2)}) %all-to-all-start.1) | async-done | bytes 524320 | tf_op jit(solution)/shard_map/all_to_all | solution.py:178
  60.5 0.3 convolution_bitcast_fusion
  60.8 0.7 shard_map.97
  61.5 8.3 %all-to-all-start.2 = ((f32[8,16,128]{2,1,0:T(8,128)}), f32[8,16,128]{2,1,0:T(8,128)S(1)}, u32[]{:S(2)}, u32[]{:S(2)}) async-start(f32[8,16,128]{2,1,0:T(8,128)} %shard_map.97), calls=%async_computation.2 | async-start | bytes 131072 | tf_op jit(solution)/shard_map/all_to_all | solution.py:211
  69.8 0.0 copy-start.3
  69.8 0.3 fusion.1
  70.1 0.0 collective-permute-done.1
  70.1 0.0 collective-permute-done.2
  70.1 0.0 collective-permute-done.3
  70.1 0.4 copy-done.3
  70.5 0.6 add_convert_fusion
  71.1 0.7 reshape.54
  71.8 2.7 %all-to-all-done.2.refs_0_ = f32[8,16,128]{2,1,0:T(8,128)S(1)} async-done(((f32[8,16,128]{2,1,0:T(8,128)}), f32[8,16,128]{2,1,0:T(8,128)S(1)}, u32[]{:S(2)}, u32[]{:S(2)}) %all-to-all-start.2) | async-done | bytes 65568 | tf_op jit(solution)/shard_map/all_to_all | solution.py:211
  74.5 0.6 shard_map.98
  (2 shorter events, 0.0 us)
Async XLA Ops:
  2.0 19.4 %copy-start.2 = (bf16[2,512]{1,0:T(2,128)(2,1)S(1)}, bf16[2,512]{1,0:T(2,128)(2,1)}, u32[]{:S(2)}) copy-start(bf16[2,512]{1,0:T(2,128)(2,1)} %param.5) | copy-start | bytes 6148
  2.0 19.5 %copy-start.1 = (bf16[1024,128]{1,0:T(8,128)(2,1)S(1)}, bf16[1024,128]{1,0:T(8,128)(2,1)}, u32[]{:S(2)}) copy-start(bf16[1024,128]{1,0:T(8,128)(2,1)} %param.8) | copy-start | bytes 786436
  2.0 33.6 %all-to-all-start = ((bf16[128,2,512]{2,1,0:T(2,128)(2,1)}), bf16[128,2,512]{2,1,0:T(2,128)(2,1)S(1)}, u32[]{:S(2)}, u32[]{:S(2)}) async-start(bf16[128,2,512]{2,1,0:T(2,128)(2,1)} %shard_map.92), calls=%async_computation | async-start | bytes 524288 | tf_op jit(solution)/shard_map/all_to_all | solution.py:135
  21.9 0.9 %copy-start = (bf16[2,256,128]{2,1,0:T(8,128)(2,1)S(1)}, bf16[2,256,128]{2,1,0:T(8,128)(2,1)}, u32[]{:S(2)}) copy-start(bf16[2,256,128]{2,1,0:T(8,128)(2,1)} %cotan.3) | copy-start | bytes 393220
  23.2 7.5 %collective-permute-start = (bf16[256,256]{1,0:T(8,128)(2,1)S(1)}, bf16[256,256]{1,0:T(8,128)(2,1)S(1)}, u32[]{:S(2)}, u32[]{:S(2)}) collective-permute-start(bf16[256,256]{1,0:T(8,128)(2,1)S(1)} %get-tuple-element.20), channel_id=1, source_target_pairs={{0,256},{256,0},{1,257},{257,1},{2,258},{258,2},{3,259},{259,3},{4... | collective-permute-start | bytes 393224 | tf_op jit(solution)/shard_map/ppermute | solution.py:152
  37.5 23.0 %all-to-all-start.1 = ((bf16[64,32,128]{2,1,0:T(8,128)(2,1)}), bf16[64,32,128]{2,1,0:T(8,128)(2,1)S(1)}, u32[]{:S(2)}, u32[]{:S(2)}) async-start(bf16[64,32,128]{2,1,0:T(8,128)(2,1)} %get-tuple-element.21), calls=%async_computation.1 | async-start | bytes 1048576 | tf_op jit(solution)/shard_map/all_to_all | solution.py:178
  44.8 25.3 %collective-permute-start.1 = (f32[2,64,128]{2,1,0:T(8,128)S(1)}, f32[2,64,128]{2,1,0:T(8,128)S(1)}, u32[]{:S(2)}, u32[]{:S(2)}) collective-permute-start(f32[2,64,128]{2,1,0:T(8,128)S(1)} %get-tuple-element.35), channel_id=1, source_target_pairs={{0,1},{1,0},{2,3},{3,2},{4,5},{5,4},{6,7},{7,6},{8,9},{9,8},{10,11... | collective-permute-start | bytes 196616 | tf_op jit(solution)/shard_map/ppermute | solution.py:201
  48.3 21.8 %collective-permute-start.2 = (f32[2,64,128]{2,1,0:T(8,128)S(1)}, f32[2,64,128]{2,1,0:T(8,128)S(1)}, u32[]{:S(2)}, u32[]{:S(2)}) collective-permute-start(f32[2,64,128]{2,1,0:T(8,128)S(1)} %get-tuple-element.37), channel_id=1, source_target_pairs={{0,2},{1,3},{2,0},{3,1},{4,6},{5,7},{6,4},{7,5},{8,10},{9,11},{10,... | collective-permute-start | bytes 196616 | tf_op jit(solution)/shard_map/ppermute | solution.py:201
  52.7 17.4 %collective-permute-start.3 = (f32[2,64,128]{2,1,0:T(8,128)S(1)}, f32[2,64,128]{2,1,0:T(8,128)S(1)}, u32[]{:S(2)}, u32[]{:S(2)}) collective-permute-start(f32[2,64,128]{2,1,0:T(8,128)S(1)} %get-tuple-element.36), channel_id=1, source_target_pairs={{0,3},{1,2},{2,1},{3,0},{4,7},{5,6},{6,5},{7,4},{8,11},{9,10},{10,... | collective-permute-start | bytes 196616 | tf_op jit(solution)/shard_map/ppermute | solution.py:201
  61.5 13.0 %all-to-all-start.2 = ((f32[8,16,128]{2,1,0:T(8,128)}), f32[8,16,128]{2,1,0:T(8,128)S(1)}, u32[]{:S(2)}, u32[]{:S(2)}) async-start(f32[8,16,128]{2,1,0:T(8,128)} %shard_map.97), calls=%async_computation.2 | async-start | bytes 131072 | tf_op jit(solution)/shard_map/all_to_all | solution.py:211
  69.8 0.7 copy-start.3

commit v9 on v8

--- a/solution.py
+++ b/solution.py
@@ -24,8 +24,16 @@
     return jnp.einsum(form, a, b, preferred_element_type=jnp.float32)
 
 
-def opening_kernel(right, out):
-    out[...] = jnp.broadcast_to(right[...][None], out.shape)
+def opening_kernel(right, out, block, done):
+    block[...] = jnp.broadcast_to(right[...][None], block.shape)
+    size = block.shape[0]
+    copies = [
+        pltpu.make_async_copy(block, out.at[pl.ds(size * n, size)], done.at[n]) for n in range(out.shape[0] // size)
+    ]
+    for copy in copies:
+        copy.start()
+    for copy in copies:
+        copy.wait()
 
 
 def right_kernel(place, cotan, mixed_hi, mixed_lo, kept, sent):
@@ -52,30 +60,40 @@
                 ]
 
 
-def products_kernel(right, cotan, left_cols, grad_right, message, back, weight):
-    rows = right[...]
+def products_kernel(right, cotan, left_cols, grad_right, message, back, weight, own, other, done):
     both = jnp.concatenate([cotan[0], cotan[1]], axis=1)
-    terms = lax.dot_general(rows, both, (((0,), (0,)), ((), ())), preferred_element_type=jnp.float32)
+    planes, lines = own.shape[0], own.shape[1] // 2
+    total = jnp.sum(both.astype(jnp.float32), axis=0, keepdims=True)
+    total = total[:, :P_SIZE] + total[:, P_SIZE:]
+    high = total.astype(jnp.bfloat16).astype(jnp.float32)
+    line = lax.broadcasted_iota(jnp.int32, (lines, P_SIZE), 0)
+    bias = jnp.where(line == 0, high, jnp.where(line == 1, total - high, 0.0))
+    bias = jnp.broadcast_to(bias[None], (planes, lines, P_SIZE))
+    other[...] = jnp.concatenate([grad_right[...].reshape(planes, lines, P_SIZE), bias], axis=1).astype(jnp.bfloat16)
+    first = pltpu.make_async_copy(other, message.at[:, pl.ds(2 * lines, 2 * lines)], done.at[0])
+    first.start()
+
+    terms = lax.dot_general(right[...], both, (((0,), (0,)), ((), ())), preferred_element_type=jnp.float32)
     back[0] = terms[:, :P_SIZE]
     back[1] = terms[:, P_SIZE:]
     lhs = left_cols[...]
-    for y in range(C):
-        parts = []
-        for i in range(ROW_DEV):
-            parts += split_in_two(back[i, pl.ds(y, SEQ_DEV, stride=C), :])
-        weight[pl.ds(y, C, stride=C), :] = jnp.dot(
-            lhs, jnp.concatenate(parts, axis=0), preferred_element_type=jnp.float32
-        )
-    planes = message.shape[0]
-    halves = weight[...].reshape(HALVES, planes, C * C // (HALVES * planes), P_SIZE)
-    own = grad_right[...].reshape(planes, grad_right.shape[0] // planes, P_SIZE)
-    total = jnp.sum(both.astype(jnp.float32), axis=0, keepdims=True)
-    total = total[:, :P_SIZE] + total[:, P_SIZE:]
-    high = total.astype(jnp.bfloat16).astype(jnp.float32)
-    line = lax.broadcasted_iota(jnp.int32, halves.shape[2:], 0)
-    bias = jnp.where(line == 0, high, jnp.where(line == 1, total - high, 0.0))
-    bias = jnp.broadcast_to(bias[None], halves.shape[1:])
-    message[...] = jnp.concatenate([halves[0], halves[1], own, bias], axis=1).astype(jnp.bfloat16)
+    group = 8
+    for y0 in range(0, C, group):
+        columns = []
+        for y in range(y0, y0 + group):
+            parts = []
+            for i in range(ROW_DEV):
+                parts += split_in_two(back[i, pl.ds(y, SEQ_DEV, stride=C), :])
+            columns.append(jnp.concatenate(parts, axis=0))
+        terms = jnp.dot(lhs, jnp.concatenate(columns, axis=1), preferred_element_type=jnp.float32)
+        for n in range(group):
+            weight[pl.ds(y0 + n, C, stride=C), :] = terms[:, n * P_SIZE : (n + 1) * P_SIZE]
+    halves = weight[...].reshape(HALVES, planes, lines, P_SIZE)
+    own[...] = jnp.concatenate([halves[0], halves[1]], axis=1).astype(jnp.bfloat16)
+    second = pltpu.make_async_copy(own, message.at[:, pl.ds(0, 2 * lines)], done.at[1])
+    second.start()
+    first.wait()
+    second.wait()
 
 
 def pair_kernel(right, mixed_hi, mixed_lo, back, pair, back_hi, back_lo):
@@ -130,7 +148,8 @@
         opening_kernel,
         out_shape=jax.ShapeDtypeStruct((res, ROW_DEV, WIDE), jnp.bfloat16),
         in_specs=[WHOLE],
-        out_specs=WHOLE,
+        out_specs=pl.BlockSpec(memory_space=pl.ANY),
+        scratch_shapes=[pltpu.VMEM((16, ROW_DEV, WIDE), jnp.bfloat16), pltpu.SemaphoreType.DMA((res // 16,))],
     )(right_proj)
     arrived = lax.all_to_all(opening, ("half", "plane"), 0, 0, tiled=True)
     right_all = arrived.reshape(columns, WIDE)
@@ -169,8 +188,13 @@
             jax.ShapeDtypeStruct(back, jnp.float32),
         ),
         in_specs=[WHOLE] * 4,
-        out_specs=(WHOLE,) * 2,
-        scratch_shapes=[pltpu.VMEM((C * C, P_SIZE), jnp.float32)],
+        out_specs=(pl.BlockSpec(memory_space=pl.ANY), WHOLE),
+        scratch_shapes=[
+            pltpu.VMEM((C * C, P_SIZE), jnp.float32),
+            pltpu.VMEM((planes, 2 * rows, P_SIZE), jnp.bfloat16),
+            pltpu.VMEM((planes, 2 * rows, P_SIZE), jnp.bfloat16),
+            pltpu.SemaphoreType.DMA((2,)),
+        ],
         compiler_params=pltpu.CompilerParams(vmem_limit_bytes=16 * 1024 * 1024),
         cost_estimate=pl.CostEstimate(flops=200_000_000, bytes_accessed=2_000_000, transcendentals=0),
     )(right_all, pair_cotangent, left_cols, grad_right)
@@ -195,12 +219,16 @@
     def columns_of(owner):
         return lax.dynamic_slice_in_dim(pair, owner * cols, cols, 1)
 
-    others = []
+    pair_sum = columns_of(here)
     for step in range(1, seq):
         sent = columns_of(lax.bitwise_xor(here, jnp.int32(step)))
-        others.append(lax.ppermute(sent, "seq", [(q, q ^ step) for q in range(seq)]))
-
-    parts, back_hi, back_lo, pair_sum = lax.optimization_barrier((parts, back_hi, back_lo, columns_of(here)))
+        pair_sum = pair_sum + lax.ppermute(sent, "seq", [(q, q ^ step) for q in range(seq)])
+    pair_update = (pair_sum * scale + out_bias).astype(jnp.bfloat16)
+    back_hi, back_lo = (term.reshape(ROW_DEV, SEQ_DEV, C, P_SIZE) for term in (back_hi, back_lo))
+    grad_left = dot32("isyk,xyk->isx", back_hi, weight) + dot32("isyk,xyk->isx", back_lo, weight)
+    grad_left = (grad_left * scale).reshape(ROW_DEV, WIDE)
+
+    parts, pair_update, grad_left = lax.optimization_barrier((parts, pair_update, grad_left))
     last = pl.pallas_call(
         middle_kernel,
         out_shape=jax.ShapeDtypeStruct((HALVES * seq, 2 * rows, P_SIZE), jnp.float32),
@@ -220,12 +248,7 @@
         out_specs=(WHOLE,) * 3,
         compiler_params=pltpu.CompilerParams(vmem_limit_bytes=8 * 1024 * 1024),
     )(last)
-    for other in others:
-        pair_sum = pair_sum + other
-    pair_update = (pair_sum * scale + out_bias).astype(jnp.bfloat16)
-    back_hi, back_lo = (term.reshape(ROW_DEV, SEQ_DEV, C, P_SIZE) for term in (back_hi, back_lo))
-    grad_left = dot32("isyk,xyk->isx", back_hi, weight) + dot32("isyk,xyk->isx", back_lo, weight)
-    return pair_update, (grad_left * scale).reshape(ROW_DEV, WIDE), grad_right, grad_weight, grad_bias[0]
+    return pair_update, grad_left, grad_right, grad_weight, grad_bias[0]
 
 
 def solution(mesh):

time: 75.6 us -> 74.5 us (0.985)
  blocking collectives: 0 us -> 13.5 us
  starting transfers between devices: 47.7 us -> 39.5 us
  waiting for transfers between devices: 17.3 us -> 11.4 us
    all_to_all x0 -> x1, blocking collectives: none -> 13.5 us  [on_device(): last = lax.all_to_all(last, ('half', 'seq'), 0, 0, tiled=True)]
    all_to_all x1 -> x0, starting transfers between devices: 8.28 us -> none  [on_device(): last = lax.all_to_all(last, ('half', 'seq'), 0, 0, tiled=True)]
    all_to_all x1, waiting for transfers between devices: 5.25 us -> 1.5 us  [on_device(): parts = lax.all_to_all(message, 'plane', 0, 0, tiled=True)]
    all_to_all x1 -> x0, waiting for transfers between devices: 2.72 us -> none  [on_device(): last = lax.all_to_all(last, ('half', 'seq'), 0, 0, tiled=True)]
    ppermute x3, waiting for transfers between devices: 0.01 us -> 1.23 us  [on_device(): lax.ppermute(sent, 'seq', [(q, q ^ step) for q in range(seq)])]
    all_to_all x1, waiting for transfers between devices: 4.75 us -> 3.96 us  [on_device(): arrived = lax.all_to_all(opening, ('half', 'plane'), 0, 0, tiled=True)]
  transfers between devices with their start and end apart: 7 -> 6, of which waited for: 4 -> 4; matrix products, arithmetic and copies ran while one was open for 3% -> 3% of each run, Pallas kernels for 2% -> 1%
where the time goes in v9:
time: 74.5 us; the launch traced here: 74 us
  starting transfers between devices  39.5 us (53%)
  blocking collectives  13.5 us (18%)
  waiting for transfers between devices  11.4 us (15%)
  Pallas kernels  4.81 us (6%)
  local copies, waits for them, and re-layouts  2.71 us (4%)
  between operations  0.82 us (1%)
  matrix products  0.76 us (1%)
    all_to_all x1, starting transfers between devices, on_device(): arrived = lax.all_to_all(opening, ('half', 'plane'), 0, 0, tiled=True)  19.4 us
    all_to_all x1, blocking collectives, on_device(): last = lax.all_to_all(last, ('half', 'seq'), 0, 0, tiled=True)  13.5 us
    ppermute x3, starting transfers between devices, on_device(): lax.ppermute(sent, 'seq', [(q, q ^ step) for q in range(seq)])  10.6 us
    all_to_all x1, starting transfers between devices, on_device(): parts = lax.all_to_all(message, 'plane', 0, 0, tiled=True)  6.66 us
    ppermute x1, waiting for transfers between devices, on_device(): got = lax.ppermute(sent, 'half', [(0, 1), (1, 0)])  4.67 us
    all_to_all x1, waiting for transfers between devices, on_device(): arrived = lax.all_to_all(opening, ('half', 'plane'), 0, 0, tiled=True)  3.96 us
    ppermute x1, starting transfers between devices, on_device(): got = lax.ppermute(sent, 'half', [(0, 1), (1, 0)])  2.8 us
    pallas_call x1, Pallas kernels, on_device(): pl.pallas_call(products_kernel, out_shape=(jax.ShapeDtypeStruct((planes,...  1.69 us
  transfers between devices with their start and end apart: 6, of which 4 were waited for; matrix products, arithmetic and copies ran while one was open for 3% of the time, Pallas kernels for 1%

profile of v9, /device:TPU:1, one launch (start us, length us, event | category | flops | bytes accessed | tf_op | source)
XLA Modules:
  0.0 74.0 jit_solution(3003078344988935734)
XLA Ops:
  0.6 1.4 %shard_map.92 = bf16[128,2,512]{2,1,0:T(2,128)(2,1)} custom-call(bf16[2,512]{1,0:T(2,128)(2,1)} %right.1), custom_call_target="tpu_custom_call" | custom-call | tf_op jit(solution)/shard_map/pallas_call | solution.py:147
  2.1 0.0 copy-start.1
  2.1 19.4 %all-to-all-start = ((bf16[128,2,512]{2,1,0:T(2,128)(2,1)}), bf16[128,2,512]{2,1,0:T(2,128)(2,1)S(1)}, u32[]{:S(2)}, u32[]{:S(2)}) async-start(bf16[128,2,512]{2,1,0:T(2,128)(2,1)} %shard_map.92), calls=%async_computation | async-start | bytes 524288 | tf_op jit(solution)/shard_map/all_to_all | solution.py:154
  21.5 0.0 copy-start.2
  21.6 0.7 copy-done.2
  22.2 0.1 reshape.56
  22.3 0.0 copy-done.1
  22.3 0.2 fusion.2
  22.6 0.1 copy.19
  22.6 0.0 copy-start
  22.6 0.1 copy.20
  22.7 0.8 %copy-done = bf16[2,256,128]{2,1,0:T(8,128)(2,1)S(1)} copy-done((bf16[2,256,128]{2,1,0:T(8,128)(2,1)S(1)}, bf16[2,256,128]{2,1,0:T(8,128)(2,1)}, u32[]{:S(2)}) %copy-start) | copy-done | bytes 131096
  23.5 0.4 shard_map.93
  24.0 2.8 %collective-permute-start = (bf16[256,256]{1,0:T(8,128)(2,1)S(1)}, bf16[256,256]{1,0:T(8,128)(2,1)S(1)}, u32[]{:S(2)}, u32[]{:S(2)}) collective-permute-start(bf16[256,256]{1,0:T(8,128)(2,1)S(1)} %get-tuple-element.19), channel_id=1, source_target_pairs={{0,256},{256,0},{1,257},{257,1},{2,258},{258,2},{3,259},{259,3},{4... | collective-permute-start | bytes 393224 | tf_op jit(solution)/shard_map/ppermute | solution.py:171
  26.8 0.1 reshape.46
  26.9 0.1 copy.21.left_cols
  27.0 4.7 %collective-permute-done.got = bf16[256,256]{1,0:T(8,128)(2,1)S(1)} collective-permute-done((bf16[256,256]{1,0:T(8,128)(2,1)S(1)}, bf16[256,256]{1,0:T(8,128)(2,1)S(1)}, u32[]{:S(2)}, u32[]{:S(2)}) %collective-permute-start) | collective-permute-done | bytes 131104 | tf_op jit(solution)/shard_map/ppermute | solution.py:171
  31.6 0.1 shard_map.94.grad_right
  31.7 4.0 %all-to-all-done = bf16[128,2,512]{2,1,0:T(2,128)(2,1)S(1)} async-done(((bf16[128,2,512]{2,1,0:T(2,128)(2,1)}), bf16[128,2,512]{2,1,0:T(2,128)(2,1)S(1)}, u32[]{:S(2)}, u32[]{:S(2)}) %all-to-all-start) | async-done | bytes 262176 | tf_op jit(solution)/shard_map/all_to_all | solution.py:154
  35.7 0.1 reshape.45.right
  35.8 1.7 %shard_map.95 = (bf16[64,32,128]{2,1,0:T(8,128)(2,1)}, f32[2,512,128]{2,1,0:T(8,128)S(1)}) custom-call(bf16[256,512]{1,0:T(8,128)(2,1)S(1)} %reshape.45.right, bf16[2,256,128]{2,1,0:T(8,128)(2,1)S(1)} %copy-done, bf16[32,64]{1,0:T(8,128)(2,1)S(1)} %copy.21.left_cols, f32[512,128]{1,0:T(8,128)S(1)} %shard_map.94.grad_right), custom_call_target="tpu_custom_call" | custom-call | flops 200000000 | bytes 2000000 | tf_op jit(solution)/shard_map/pallas_call | solution.py:184
  37.5 6.7 %all-to-all-start.1 = ((bf16[64,32,128]{2,1,0:T(8,128)(2,1)}), bf16[64,32,128]{2,1,0:T(8,128)(2,1)S(1)}, u32[]{:S(2)}, u32[]{:S(2)}) async-start(bf16[64,32,128]{2,1,0:T(8,128)(2,1)} %get-tuple-element.20), calls=%async_computation.1 | async-start | bytes 1048576 | tf_op jit(solution)/shard_map/all_to_all | solution.py:202
  44.2 0.4 shard_map.96
  44.7 6.2 %collective-permute-start.3 = (f32[2,64,128]{2,1,0:T(8,128)S(1)}, f32[2,64,128]{2,1,0:T(8,128)S(1)}, u32[]{:S(2)}, u32[]{:S(2)}) collective-permute-start(f32[2,64,128]{2,1,0:T(8,128)S(1)} %get-tuple-element.34), channel_id=1, source_target_pairs={{0,3},{1,2},{2,1},{3,0},{4,7},{5,6},{6,5},{7,4},{8,11},{9,10},{10,... | collective-permute-start | bytes 196616 | tf_op jit(solution)/shard_map/ppermute | solution.py:225
  50.9 2.4 %collective-permute-start.2 = (f32[2,64,128]{2,1,0:T(8,128)S(1)}, f32[2,64,128]{2,1,0:T(8,128)S(1)}, u32[]{:S(2)}, u32[]{:S(2)}) collective-permute-start(f32[2,64,128]{2,1,0:T(8,128)S(1)} %get-tuple-element.35), channel_id=1, source_target_pairs={{0,2},{1,3},{2,0},{3,1},{4,6},{5,7},{6,4},{7,5},{8,10},{9,11},{10,... | collective-permute-start | bytes 196616 | tf_op jit(solution)/shard_map/ppermute | solution.py:225
  53.3 1.9 %collective-permute-start.1 = (f32[2,64,128]{2,1,0:T(8,128)S(1)}, f32[2,64,128]{2,1,0:T(8,128)S(1)}, u32[]{:S(2)}, u32[]{:S(2)}) collective-permute-start(f32[2,64,128]{2,1,0:T(8,128)S(1)} %get-tuple-element.33), channel_id=1, source_target_pairs={{0,1},{1,0},{2,3},{3,2},{4,5},{5,4},{6,7},{7,6},{8,9},{9,8},{10,11... | collective-permute-start | bytes 196616 | tf_op jit(solution)/shard_map/ppermute | solution.py:225
  55.3 0.3 convolution_bitcast_fusion
  55.5 0.3 fusion.1
  55.8 0.0 copy-start.3
  55.8 0.7 reshape.54
  56.5 0.0 collective-permute-done.3
  56.5 1.2 %collective-permute-done.2 = f32[2,64,128]{2,1,0:T(8,128)S(1)} collective-permute-done((f32[2,64,128]{2,1,0:T(8,128)S(1)}, f32[2,64,128]{2,1,0:T(8,128)S(1)}, u32[]{:S(2)}, u32[]{:S(2)}) %collective-permute-start.2) | collective-permute-done | bytes 65568 | tf_op jit(solution)/shard_map/ppermute | solution.py:225
  57.7 0.0 collective-permute-done.1
  57.7 0.0 copy-done.3
  57.7 0.6 add_convert_fusion
  58.3 1.5 %all-to-all-done.1.parts = bf16[64,32,128]{2,1,0:T(8,128)(2,1)S(1)} async-done(((bf16[64,32,128]{2,1,0:T(8,128)(2,1)}), bf16[64,32,128]{2,1,0:T(8,128)(2,1)S(1)}, u32[]{:S(2)}, u32[]{:S(2)}) %all-to-all-start.1) | async-done | bytes 524320 | tf_op jit(solution)/shard_map/all_to_all | solution.py:202
  59.8 0.1 shard_map.97
  60.0 13.5 %all_to_all.15.refs_0_ = f32[8,16,128]{2,1,0:T(8,128)S(1)} all-to-all(f32[8,16,128]{2,1,0:T(8,128)S(1)} %shard_map.97), channel_id=1, replica_groups=mesh['half'=2,'plane'=64,'seq'=4] {'half','seq'}, dimensions={0} | all-to-all | bytes 131072 | tf_op jit(solution)/shard_map/all_to_all | solution.py:239
  73.4 0.6 shard_map.98
  (2 shorter events, 0.0 us)
Async XLA Ops:
  2.1 20.2 %copy-start.1 = (bf16[1024,128]{1,0:T(8,128)(2,1)S(1)}, bf16[1024,128]{1,0:T(8,128)(2,1)}, u32[]{:S(2)}) copy-start(bf16[1024,128]{1,0:T(8,128)(2,1)} %param.8) | copy-start | bytes 786436
  2.1 33.6 %all-to-all-start = ((bf16[128,2,512]{2,1,0:T(2,128)(2,1)}), bf16[128,2,512]{2,1,0:T(2,128)(2,1)S(1)}, u32[]{:S(2)}, u32[]{:S(2)}) async-start(bf16[128,2,512]{2,1,0:T(2,128)(2,1)} %shard_map.92), calls=%async_computation | async-start | bytes 524288 | tf_op jit(solution)/shard_map/all_to_all | solution.py:154
  21.5 0.7 copy-start.2
  22.6 0.9 %copy-start = (bf16[2,256,128]{2,1,0:T(8,128)(2,1)S(1)}, bf16[2,256,128]{2,1,0:T(8,128)(2,1)}, u32[]{:S(2)}) copy-start(bf16[2,256,128]{2,1,0:T(8,128)(2,1)} %cotan.3) | copy-start | bytes 393220
  24.0 7.7 %collective-permute-start = (bf16[256,256]{1,0:T(8,128)(2,1)S(1)}, bf16[256,256]{1,0:T(8,128)(2,1)S(1)}, u32[]{:S(2)}, u32[]{:S(2)}) collective-permute-start(bf16[256,256]{1,0:T(8,128)(2,1)S(1)} %get-tuple-element.19), channel_id=1, source_target_pairs={{0,256},{256,0},{1,257},{257,1},{2,258},{258,2},{3,259},{259,3},{4... | collective-permute-start | bytes 393224 | tf_op jit(solution)/shard_map/ppermute | solution.py:171
  37.5 22.4 %all-to-all-start.1 = ((bf16[64,32,128]{2,1,0:T(8,128)(2,1)}), bf16[64,32,128]{2,1,0:T(8,128)(2,1)S(1)}, u32[]{:S(2)}, u32[]{:S(2)}) async-start(bf16[64,32,128]{2,1,0:T(8,128)(2,1)} %get-tuple-element.20), calls=%async_computation.1 | async-start | bytes 1048576 | tf_op jit(solution)/shard_map/all_to_all | solution.py:202
  44.7 11.8 %collective-permute-start.3 = (f32[2,64,128]{2,1,0:T(8,128)S(1)}, f32[2,64,128]{2,1,0:T(8,128)S(1)}, u32[]{:S(2)}, u32[]{:S(2)}) collective-permute-start(f32[2,64,128]{2,1,0:T(8,128)S(1)} %get-tuple-element.34), channel_id=1, source_target_pairs={{0,3},{1,2},{2,1},{3,0},{4,7},{5,6},{6,5},{7,4},{8,11},{9,10},{10,... | collective-permute-start | bytes 196616 | tf_op jit(solution)/shard_map/ppermute | solution.py:225
  50.9 6.8 %collective-permute-start.2 = (f32[2,64,128]{2,1,0:T(8,128)S(1)}, f32[2,64,128]{2,1,0:T(8,128)S(1)}, u32[]{:S(2)}, u32[]{:S(2)}) collective-permute-start(f32[2,64,128]{2,1,0:T(8,128)S(1)} %get-tuple-element.35), channel_id=1, source_target_pairs={{0,2},{1,3},{2,0},{3,1},{4,6},{5,7},{6,4},{7,5},{8,10},{9,11},{10,... | collective-permute-start | bytes 196616 | tf_op jit(solution)/shard_map/ppermute | solution.py:225
  53.3 4.4 %collective-permute-start.1 = (f32[2,64,128]{2,1,0:T(8,128)S(1)}, f32[2,64,128]{2,1,0:T(8,128)S(1)}, u32[]{:S(2)}, u32[]{:S(2)}) collective-permute-start(f32[2,64,128]{2,1,0:T(8,128)S(1)} %get-tuple-element.33), channel_id=1, source_target_pairs={{0,1},{1,0},{2,3},{3,2},{4,5},{5,4},{6,7},{7,6},{8,9},{9,8},{10,11... | collective-permute-start | bytes 196616 | tf_op jit(solution)/shard_map/ppermute | solution.py:225
  55.8 1.9 %copy-start.3 = (f32[128]{0:T(128)S(1)}, f32[128]{0:T(128)}, u32[]{:S(2)}) copy-start(f32[128]{0:T(128)} %param.9) | copy-start | bytes 1540

commit v10 on v9

--- a/solution.py
+++ b/solution.py
@@ -12,6 +12,7 @@
 ROW_DEV = 2
 WIDE = SEQ_DEV * C
 HALVES = 2
+SIDE = 8
 WHOLE = pl.BlockSpec(memory_space=pltpu.VMEM)
 
 
@@ -62,15 +63,17 @@
 
 def products_kernel(right, cotan, left_cols, grad_right, message, back, weight, own, other, done):
     both = jnp.concatenate([cotan[0], cotan[1]], axis=1)
-    planes, lines = own.shape[0], own.shape[1] // 2
+    planes, lines = SIDE * SIDE, own.shape[2] // 2
     total = jnp.sum(both.astype(jnp.float32), axis=0, keepdims=True)
     total = total[:, :P_SIZE] + total[:, P_SIZE:]
     high = total.astype(jnp.bfloat16).astype(jnp.float32)
     line = lax.broadcasted_iota(jnp.int32, (lines, P_SIZE), 0)
     bias = jnp.where(line == 0, high, jnp.where(line == 1, total - high, 0.0))
     bias = jnp.broadcast_to(bias[None], (planes, lines, P_SIZE))
-    other[...] = jnp.concatenate([grad_right[...].reshape(planes, lines, P_SIZE), bias], axis=1).astype(jnp.bfloat16)
-    first = pltpu.make_async_copy(other, message.at[:, pl.ds(2 * lines, 2 * lines)], done.at[0])
+    tiles = jnp.concatenate([grad_right[...].reshape(planes, lines, P_SIZE), bias], axis=1).astype(jnp.bfloat16)
+    for z in range(SIDE):
+        other[:, z] = tiles[z * SIDE : (z + 1) * SIDE]
+    first = pltpu.make_async_copy(other, message.at[:, :, pl.ds(2 * lines, 2 * lines)], done.at[0])
     first.start()
 
     terms = lax.dot_general(right[...], both, (((0,), (0,)), ((), ())), preferred_element_type=jnp.float32)
@@ -89,8 +92,10 @@
         for n in range(group):
             weight[pl.ds(y0 + n, C, stride=C), :] = terms[:, n * P_SIZE : (n + 1) * P_SIZE]
     halves = weight[...].reshape(HALVES, planes, lines, P_SIZE)
-    own[...] = jnp.concatenate([halves[0], halves[1]], axis=1).astype(jnp.bfloat16)
-    second = pltpu.make_async_copy(own, message.at[:, pl.ds(0, 2 * lines)], done.at[1])
+    tiles = jnp.concatenate([halves[0], halves[1]], axis=1).astype(jnp.bfloat16)
+    for z in range(SIDE):
+        own[:, z] = tiles[z * SIDE : (z + 1) * SIDE]
+    second = pltpu.make_async_copy(own, message.at[:, :, pl.ds(0, 2 * lines)], done.at[1])
     second.start()
     first.wait()
     second.wait()
@@ -135,7 +140,7 @@
 
 
 def on_device(left_proj, right_proj, pair_cotangent, out_weight, out_bias):
-    planes = lax.axis_size("plane")
+    planes = SIDE * SIDE
     seq = lax.axis_size("seq")
     res = HALVES * planes
     scale = 1.0 / (SEQ_DEV * seq)
@@ -151,8 +156,9 @@
         out_specs=pl.BlockSpec(memory_space=pl.ANY),
         scratch_shapes=[pltpu.VMEM((16, ROW_DEV, WIDE), jnp.bfloat16), pltpu.SemaphoreType.DMA((res // 16,))],
     )(right_proj)
-    arrived = lax.all_to_all(opening, ("half", "plane"), 0, 0, tiled=True)
-    right_all = arrived.reshape(columns, WIDE)
+    arrived = lax.all_to_all(opening, ("y", "z", "half"), 0, 0, tiled=True)
+    cotan_arrived = pair_cotangent.reshape(ROW_DEV, HALVES, SIDE, SIDE, ROW_DEV, P_SIZE)
+    cotan_arrived = cotan_arrived.transpose(0, 3, 2, 1, 4, 5).reshape(pair_cotangent.shape)
 
     mixed = dot32("isx,xyk->isyk", left_rows, weight)
     high = lax.reduce_precision(mixed, 8, 7)
@@ -184,23 +190,25 @@
     message, terms = pl.pallas_call(
         products_kernel,
         out_shape=(
-            jax.ShapeDtypeStruct((planes, 4 * rows, P_SIZE), jnp.bfloat16),
+            jax.ShapeDtypeStruct((SIDE, SIDE, 4 * rows, P_SIZE), jnp.bfloat16),
             jax.ShapeDtypeStruct(back, jnp.float32),
         ),
         in_specs=[WHOLE] * 4,
         out_specs=(pl.BlockSpec(memory_space=pl.ANY), WHOLE),
         scratch_shapes=[
             pltpu.VMEM((C * C, P_SIZE), jnp.float32),
-            pltpu.VMEM((planes, 2 * rows, P_SIZE), jnp.bfloat16),
-            pltpu.VMEM((planes, 2 * rows, P_SIZE), jnp.bfloat16),
+            pltpu.VMEM((SIDE, SIDE, 2 * rows, P_SIZE), jnp.bfloat16),
+            pltpu.VMEM((SIDE, SIDE, 2 * rows, P_SIZE), jnp.bfloat16),
             pltpu.SemaphoreType.DMA((2,)),
         ],
         compiler_params=pltpu.CompilerParams(vmem_limit_bytes=16 * 1024 * 1024),
         cost_estimate=pl.CostEstimate(flops=200_000_000, bytes_accessed=2_000_000, transcendentals=0),
-    )(right_all, pair_cotangent, left_cols, grad_right)
-
-    parts = lax.all_to_all(message, "plane", 0, 0, tiled=True)
-
+    )(arrived.reshape(columns, WIDE), cotan_arrived, left_cols, grad_right)
+
+    parts = lax.all_to_all(message.reshape(planes, 4 * rows, P_SIZE), ("y", "z"), 0, 0, tiled=True)
+
+    terms, arrived = lax.optimization_barrier((terms, arrived))
+    right_all = arrived.reshape(SIDE, SIDE, HALVES, ROW_DEV, WIDE).transpose(2, 1, 0, 3, 4).reshape(columns, WIDE)
     pair, back_hi, back_lo = pl.pallas_call(
         pair_kernel,
         out_shape=(
@@ -253,8 +261,8 @@
 
 def solution(mesh):
     res, seq = mesh.devices.shape
-    fine = Mesh(mesh.devices.reshape(HALVES, res // HALVES, seq), ("half", "plane", "seq"))
-    across = ("half", "plane")
+    fine = Mesh(mesh.devices.reshape(HALVES, SIDE, res // HALVES // SIDE, seq), ("half", "z", "y", "seq"))
+    across = ("half", "z", "y")
     return jax.shard_map(
         on_device,
         mesh=fine,

time: 74.5 us -> 73.9 us (level)
  waiting for transfers between devices: 11.4 us -> 9.01 us
  starting transfers between devices: 39.5 us -> 40.6 us
    all_to_all x2, waiting for transfers between devices: 5.46 us -> 3.05 us  [the longest x1 2.74 us: on_device(): arrived = lax.all_to_all(opening, ('y', 'z', 'half'), 0, 0, tiled=True)]
    all_to_all x2, starting transfers between devices: 26.1 us -> 27 us  [the longest x1 19.4 us: on_device(): arrived = lax.all_to_all(opening, ('y', 'z', 'half'), 0, 0, tiled=True)]
  transfers between devices with their start and end apart: 6 -> 6, of which waited for: 4 -> 4; matrix products, arithmetic and copies ran while one was open for 3% -> 4% of each run, Pallas kernels for 1% -> 1%
where the time goes in v10:
time: 73.9 us; the launch traced here: 73.4 us
  starting transfers between devices  40.6 us (55%)
  blocking collectives  13.6 us (18%)
  waiting for transfers between devices  9.01 us (12%)
  Pallas kernels  4.81 us (7%)
  local copies, waits for them, and re-layouts  3.14 us (4%)
  between operations  0.85 us (1%)
  matrix products  0.76 us (1%)
    all_to_all x1, starting transfers between devices, on_device(): arrived = lax.all_to_all(opening, ('y', 'z', 'half'), 0, 0, tiled=True)  19.4 us
    all_to_all x1, blocking collectives, on_device(): last = lax.all_to_all(last, ('half', 'seq'), 0, 0, tiled=True)  13.6 us
    ppermute x3, starting transfers between devices, on_device(): lax.ppermute(sent, 'seq', [(q, q ^ step) for q in range(seq)])  11.1 us
    all_to_all x1, starting transfers between devices, on_device(): lax.all_to_all(message.reshape(planes, 4 * rows, P_SIZE), ('y', 'z'), 0,...  7.58 us
    ppermute x1, waiting for transfers between devices, on_device(): got = lax.ppermute(sent, 'half', [(0, 1), (1, 0)])  4.73 us
    all_to_all x1, waiting for transfers between devices, on_device(): arrived = lax.all_to_all(opening, ('y', 'z', 'half'), 0, 0, tiled=True)  2.74 us
    ppermute x1, starting transfers between devices, on_device(): got = lax.ppermute(sent, 'half', [(0, 1), (1, 0)])  2.48 us
    pallas_call x1, Pallas kernels, on_device(): pl.pallas_call(products_kernel, out_shape=(jax.ShapeDtypeStruct((SIDE, SI...  1.7 us
  transfers between devices with their start and end apart: 6, of which 4 were waited for; matrix products, arithmetic and copies ran while one was open for 4% of the time, Pallas kernels for 1%

profile of v10, /device:TPU:1, one launch (start us, length us, event | category | flops | bytes accessed | tf_op | source)
XLA Modules:
  0.0 73.4 jit_solution(1054356879203924106)
XLA Ops:
  0.6 1.4 %shard_map.92 = bf16[128,2,512]{2,1,0:T(2,128)(2,1)} custom-call(bf16[2,512]{1,0:T(2,128)(2,1)} %right.1), custom_call_target="tpu_custom_call" | custom-call | tf_op jit(solution)/shard_map/pallas_call | solution.py:152
  2.1 0.0 copy-start.1
  2.1 19.4 %all-to-all-start = ((bf16[128,2,512]{2,1,0:T(2,128)(2,1)}), bf16[128,2,512]{2,1,0:T(2,128)(2,1)S(1)}, u32[]{:S(2)}, u32[]{:S(2)}) async-start(bf16[128,2,512]{2,1,0:T(2,128)(2,1)} %shard_map.92), calls=%async_computation | async-start | bytes 524288 | tf_op jit(solution)/shard_map/all_to_all | solution.py:159
  21.5 0.0 copy-start.2
  21.6 0.7 copy-done.2
  22.2 0.1 reshape.76
  22.3 0.0 copy-done.1
  22.3 0.2 fusion.2
  22.6 0.1 copy.22
  22.6 0.0 copy-start
  22.6 0.1 copy.23
  22.7 0.8 %copy-done = bf16[2,256,128]{2,1,0:T(8,128)(2,1)S(1)} copy-done((bf16[2,256,128]{2,1,0:T(8,128)(2,1)S(1)}, bf16[2,256,128]{2,1,0:T(8,128)(2,1)}, u32[]{:S(2)}) %copy-start) | copy-done | bytes 131096
  23.5 0.4 shard_map.93
  24.0 2.5 %collective-permute-start = (bf16[256,256]{1,0:T(8,128)(2,1)S(1)}, bf16[256,256]{1,0:T(8,128)(2,1)S(1)}, u32[]{:S(2)}, u32[]{:S(2)}) collective-permute-start(bf16[256,256]{1,0:T(8,128)(2,1)S(1)} %get-tuple-element.21), channel_id=1, source_target_pairs={{0,256},{256,0},{1,257},{257,1},{2,258},{258,2},{3,259},{259,3},{4... | collective-permute-start | bytes 393224 | tf_op jit(solution)/shard_map/ppermute | solution.py:177
  26.5 0.1 reshape.63
  26.5 0.1 copy.20
  26.7 0.1 copy.24.left_cols
  26.7 4.7 %collective-permute-done.got = bf16[256,256]{1,0:T(8,128)(2,1)S(1)} collective-permute-done((bf16[256,256]{1,0:T(8,128)(2,1)S(1)}, bf16[256,256]{1,0:T(8,128)(2,1)S(1)}, u32[]{:S(2)}, u32[]{:S(2)}) %collective-permute-start) | collective-permute-done | bytes 131104 | tf_op jit(solution)/shard_map/ppermute | solution.py:177
  31.5 0.1 shard_map.94.grad_right
  31.6 2.7 %all-to-all-done = bf16[128,2,512]{2,1,0:T(2,128)(2,1)S(1)} async-done(((bf16[128,2,512]{2,1,0:T(2,128)(2,1)}), bf16[128,2,512]{2,1,0:T(2,128)(2,1)S(1)}, u32[]{:S(2)}, u32[]{:S(2)}) %all-to-all-start) | async-done | bytes 262176 | tf_op jit(solution)/shard_map/all_to_all | solution.py:159
  34.3 0.1 reshape.60.right
  34.4 1.7 %shard_map.95 = (bf16[8,8,32,128]{3,2,1,0:T(8,128)(2,1)}, f32[2,512,128]{2,1,0:T(8,128)S(1)}) custom-call(bf16[256,512]{1,0:T(8,128)(2,1)S(1)} %reshape.60.right, bf16[2,256,128]{2,1,0:T(8,128)(2,1)S(1)} %bitcast.50, bf16[32,64]{1,0:T(8,128)(2,1)S(1)} %copy.24.left_cols, f32[512,128]{1,0:T(8,128)S(1)} %shard_map.94.grad_right), custom_call_target="tpu_custom_call" | custom-call | flops 200000000 | bytes 2000000 | tf_op jit(solution)/shard_map/pallas_call | solution.py:190
  36.1 7.6 %all-to-all-start.1 = ((bf16[64,32,128]{2,1,0:T(8,128)(2,1)}), bf16[64,32,128]{2,1,0:T(8,128)(2,1)S(1)}, u32[]{:S(2)}, u32[]{:S(2)}) async-start(bf16[64,32,128]{2,1,0:T(8,128)(2,1)} %bitcast.11), calls=%async_computation.1 | async-start | bytes 1048576 | tf_op jit(solution)/shard_map/all_to_all | solution.py:208
  43.7 0.2 copy.52
  44.0 0.1 reshape.71.right
  44.1 0.4 shard_map.96
  44.6 6.8 %collective-permute-start.3 = (f32[2,64,128]{2,1,0:T(8,128)S(1)}, f32[2,64,128]{2,1,0:T(8,128)S(1)}, u32[]{:S(2)}, u32[]{:S(2)}) collective-permute-start(f32[2,64,128]{2,1,0:T(8,128)S(1)} %get-tuple-element.38), channel_id=1, source_target_pairs={{0,3},{1,2},{2,1},{3,0},{4,7},{5,6},{6,5},{7,4},{8,11},{9,10},{10,... | collective-permute-start | bytes 196616 | tf_op jit(solution)/shard_map/ppermute | solution.py:233
  51.3 2.4 %collective-permute-start.2 = (f32[2,64,128]{2,1,0:T(8,128)S(1)}, f32[2,64,128]{2,1,0:T(8,128)S(1)}, u32[]{:S(2)}, u32[]{:S(2)}) collective-permute-start(f32[2,64,128]{2,1,0:T(8,128)S(1)} %get-tuple-element.39), channel_id=1, source_target_pairs={{0,2},{1,3},{2,0},{3,1},{4,6},{5,7},{6,4},{7,5},{8,10},{9,11},{10,... | collective-permute-start | bytes 196616 | tf_op jit(solution)/shard_map/ppermute | solution.py:233
  53.8 1.9 %collective-permute-start.1 = (f32[2,64,128]{2,1,0:T(8,128)S(1)}, f32[2,64,128]{2,1,0:T(8,128)S(1)}, u32[]{:S(2)}, u32[]{:S(2)}) collective-permute-start(f32[2,64,128]{2,1,0:T(8,128)S(1)} %get-tuple-element.37), channel_id=1, source_target_pairs={{0,1},{1,0},{2,3},{3,2},{4,5},{5,4},{6,7},{7,6},{8,9},{9,8},{10,11... | collective-permute-start | bytes 196616 | tf_op jit(solution)/shard_map/ppermute | solution.py:233
  55.7 0.3 convolution_bitcast_fusion
  56.0 0.3 fusion.1
  56.2 0.0 copy-start.3
  56.2 0.7 reshape.74
  56.9 0.0 collective-permute-done.3
  56.9 1.2 %collective-permute-done.2 = f32[2,64,128]{2,1,0:T(8,128)S(1)} collective-permute-done((f32[2,64,128]{2,1,0:T(8,128)S(1)}, f32[2,64,128]{2,1,0:T(8,128)S(1)}, u32[]{:S(2)}, u32[]{:S(2)}) %collective-permute-start.2) | collective-permute-done | bytes 65568 | tf_op jit(solution)/shard_map/ppermute | solution.py:233
  58.1 0.0 collective-permute-done.1
  58.2 0.0 copy-done.3
  58.2 0.6 add_convert_fusion
  58.8 0.3 all-to-all-done.1.parts
  59.1 0.1 shard_map.97
  59.2 13.6 %all_to_all.15.refs_0_ = f32[8,16,128]{2,1,0:T(8,128)S(1)} all-to-all(f32[8,16,128]{2,1,0:T(8,128)S(1)} %shard_map.97), channel_id=1, replica_groups=mesh['half'=2,'z'=8,'y'=8,'seq'=4] {'half','seq'}, dimensions={0} | all-to-all | bytes 131072 | tf_op jit(solution)/shard_map/all_to_all | solution.py:247
  72.8 0.6 shard_map.98
  (2 shorter events, 0.0 us)
Async XLA Ops:
  2.1 20.2 %copy-start.1 = (bf16[1024,128]{1,0:T(8,128)(2,1)S(1)}, bf16[1024,128]{1,0:T(8,128)(2,1)}, u32[]{:S(2)}) copy-start(bf16[1024,128]{1,0:T(8,128)(2,1)} %param.8) | copy-start | bytes 786436
  2.1 32.2 %all-to-all-start = ((bf16[128,2,512]{2,1,0:T(2,128)(2,1)}), bf16[128,2,512]{2,1,0:T(2,128)(2,1)S(1)}, u32[]{:S(2)}, u32[]{:S(2)}) async-start(bf16[128,2,512]{2,1,0:T(2,128)(2,1)} %shard_map.92), calls=%async_computation | async-start | bytes 524288 | tf_op jit(solution)/shard_map/all_to_all | solution.py:159
  21.5 0.7 copy-start.2
  22.6 0.9 %copy-start = (bf16[2,256,128]{2,1,0:T(8,128)(2,1)S(1)}, bf16[2,256,128]{2,1,0:T(8,128)(2,1)}, u32[]{:S(2)}) copy-start(bf16[2,256,128]{2,1,0:T(8,128)(2,1)} %cotan.1) | copy-start | bytes 393220
  24.0 7.5 %collective-permute-start = (bf16[256,256]{1,0:T(8,128)(2,1)S(1)}, bf16[256,256]{1,0:T(8,128)(2,1)S(1)}, u32[]{:S(2)}, u32[]{:S(2)}) collective-permute-start(bf16[256,256]{1,0:T(8,128)(2,1)S(1)} %get-tuple-element.21), channel_id=1, source_target_pairs={{0,256},{256,0},{1,257},{257,1},{2,258},{258,2},{3,259},{259,3},{4... | collective-permute-start | bytes 393224 | tf_op jit(solution)/shard_map/ppermute | solution.py:177
  36.1 23.0 %all-to-all-start.1 = ((bf16[64,32,128]{2,1,0:T(8,128)(2,1)}), bf16[64,32,128]{2,1,0:T(8,128)(2,1)S(1)}, u32[]{:S(2)}, u32[]{:S(2)}) async-start(bf16[64,32,128]{2,1,0:T(8,128)(2,1)} %bitcast.11), calls=%async_computation.1 | async-start | bytes 1048576 | tf_op jit(solution)/shard_map/all_to_all | solution.py:208
  44.6 12.4 %collective-permute-start.3 = (f32[2,64,128]{2,1,0:T(8,128)S(1)}, f32[2,64,128]{2,1,0:T(8,128)S(1)}, u32[]{:S(2)}, u32[]{:S(2)}) collective-permute-start(f32[2,64,128]{2,1,0:T(8,128)S(1)} %get-tuple-element.38), channel_id=1, source_target_pairs={{0,3},{1,2},{2,1},{3,0},{4,7},{5,6},{6,5},{7,4},{8,11},{9,10},{10,... | collective-permute-start | bytes 196616 | tf_op jit(solution)/shard_map/ppermute | solution.py:233
  51.3 6.8 %collective-permute-start.2 = (f32[2,64,128]{2,1,0:T(8,128)S(1)}, f32[2,64,128]{2,1,0:T(8,128)S(1)}, u32[]{:S(2)}, u32[]{:S(2)}) collective-permute-start(f32[2,64,128]{2,1,0:T(8,128)S(1)} %get-tuple-element.39), channel_id=1, source_target_pairs={{0,2},{1,3},{2,0},{3,1},{4,6},{5,7},{6,4},{7,5},{8,10},{9,11},{10,... | collective-permute-start | bytes 196616 | tf_op jit(solution)/shard_map/ppermute | solution.py:233
  53.8 4.4 %collective-permute-start.1 = (f32[2,64,128]{2,1,0:T(8,128)S(1)}, f32[2,64,128]{2,1,0:T(8,128)S(1)}, u32[]{:S(2)}, u32[]{:S(2)}) collective-permute-start(f32[2,64,128]{2,1,0:T(8,128)S(1)} %get-tuple-element.37), channel_id=1, source_target_pairs={{0,1},{1,0},{2,3},{3,2},{4,5},{5,4},{6,7},{7,6},{8,9},{9,8},{10,11... | collective-permute-start | bytes 196616 | tf_op jit(solution)/shard_map/ppermute | solution.py:233
  56.2 1.9 %copy-start.3 = (f32[128]{0:T(128)S(1)}, f32[128]{0:T(128)}, u32[]{:S(2)}) copy-start(f32[128]{0:T(128)} %param.9) | copy-start | bytes 1540

commit v11 on v10

--- a/solution.py
+++ b/solution.py
@@ -72,7 +72,7 @@
     bias = jnp.broadcast_to(bias[None], (planes, lines, P_SIZE))
     tiles = jnp.concatenate([grad_right[...].reshape(planes, lines, P_SIZE), bias], axis=1).astype(jnp.bfloat16)
     for z in range(SIDE):
-        other[:, z] = tiles[z * SIDE : (z + 1) * SIDE]
+        other[z] = tiles[z * SIDE : (z + 1) * SIDE]
     first = pltpu.make_async_copy(other, message.at[:, :, pl.ds(2 * lines, 2 * lines)], done.at[0])
     first.start()
 
@@ -94,7 +94,7 @@
     halves = weight[...].reshape(HALVES, planes, lines, P_SIZE)
     tiles = jnp.concatenate([halves[0], halves[1]], axis=1).astype(jnp.bfloat16)
     for z in range(SIDE):
-        own[:, z] = tiles[z * SIDE : (z + 1) * SIDE]
+        own[z] = tiles[z * SIDE : (z + 1) * SIDE]
     second = pltpu.make_async_copy(own, message.at[:, :, pl.ds(0, 2 * lines)], done.at[1])
     second.start()
     first.wait()
@@ -205,7 +205,7 @@
         cost_estimate=pl.CostEstimate(flops=200_000_000, bytes_accessed=2_000_000, transcendentals=0),
     )(arrived.reshape(columns, WIDE), cotan_arrived, left_cols, grad_right)
 
-    parts = lax.all_to_all(message.reshape(planes, 4 * rows, P_SIZE), ("y", "z"), 0, 0, tiled=True)
+    parts = lax.all_to_all(message.reshape(planes, 4 * rows, P_SIZE), ("z", "y"), 0, 0, tiled=True)
 
     terms, arrived = lax.optimization_barrier((terms, arrived))
     right_all = arrived.reshape(SIDE, SIDE, HALVES, ROW_DEV, WIDE).transpose(2, 1, 0, 3, 4).reshape(columns, WIDE)

time: 73.9 us -> 74 us (level)
  no operation moved by 1% of the time
where the time goes in v11:
time: 74 us; the launch traced here: 73.5 us
  starting transfers between devices  40.6 us (55%)
  blocking collectives  13.7 us (19%)
  waiting for transfers between devices  9.01 us (12%)
  Pallas kernels  4.8 us (6%)
  local copies, waits for them, and re-layouts  3.14 us (4%)
  between operations  0.85 us (1%)
  matrix products  0.76 us (1%)
    all_to_all x1, starting transfers between devices, on_device(): arrived = lax.all_to_all(opening, ('y', 'z', 'half'), 0, 0, tiled=True)  19.4 us
    all_to_all x1, blocking collectives, on_device(): last = lax.all_to_all(last, ('half', 'seq'), 0, 0, tiled=True)  13.7 us
    ppermute x3, starting transfers between devices, on_device(): lax.ppermute(sent, 'seq', [(q, q ^ step) for q in range(seq)])  11.1 us
    all_to_all x1, starting transfers between devices, on_device(): lax.all_to_all(message.reshape(planes, 4 * rows, P_SIZE), ('z', 'y'), 0,...  7.58 us
    ppermute x1, waiting for transfers between devices, on_device(): got = lax.ppermute(sent, 'half', [(0, 1), (1, 0)])  4.73 us
    all_to_all x1, waiting for transfers between devices, on_device(): arrived = lax.all_to_all(opening, ('y', 'z', 'half'), 0, 0, tiled=True)  2.74 us
    ppermute x1, starting transfers between devices, on_device(): got = lax.ppermute(sent, 'half', [(0, 1), (1, 0)])  2.48 us
    pallas_call x1, Pallas kernels, on_device(): pl.pallas_call(products_kernel, out_shape=(jax.ShapeDtypeStruct((SIDE, SI...  1.69 us
  transfers between devices with their start and end apart: 6, of which 4 were waited for; matrix products, arithmetic and copies ran while one was open for 4% of the time, Pallas kernels for 1%

profile of v11, /device:TPU:1, one launch (start us, length us, event | category | flops | bytes accessed | tf_op | source)
XLA Modules:
  0.0 73.5 jit_solution(17537996417158926806)
XLA Ops:
  0.6 1.4 %shard_map.92 = bf16[128,2,512]{2,1,0:T(2,128)(2,1)} custom-call(bf16[2,512]{1,0:T(2,128)(2,1)} %right.1), custom_call_target="tpu_custom_call" | custom-call | tf_op jit(solution)/shard_map/pallas_call | solution.py:152
  2.1 0.0 copy-start.1
  2.1 19.4 %all-to-all-start = ((bf16[128,2,512]{2,1,0:T(2,128)(2,1)}), bf16[128,2,512]{2,1,0:T(2,128)(2,1)S(1)}, u32[]{:S(2)}, u32[]{:S(2)}) async-start(bf16[128,2,512]{2,1,0:T(2,128)(2,1)} %shard_map.92), calls=%async_computation | async-start | bytes 524288 | tf_op jit(solution)/shard_map/all_to_all | solution.py:159
  21.5 0.0 copy-start.2
  21.6 0.7 copy-done.2
  22.2 0.1 reshape.76
  22.3 0.0 copy-done.1
  22.3 0.2 fusion.2
  22.6 0.1 copy.22
  22.6 0.0 copy-start
  22.6 0.1 copy.23
  22.7 0.8 %copy-done = bf16[2,256,128]{2,1,0:T(8,128)(2,1)S(1)} copy-done((bf16[2,256,128]{2,1,0:T(8,128)(2,1)S(1)}, bf16[2,256,128]{2,1,0:T(8,128)(2,1)}, u32[]{:S(2)}) %copy-start) | copy-done | bytes 131096
  23.5 0.4 shard_map.93
  24.0 2.5 %collective-permute-start = (bf16[256,256]{1,0:T(8,128)(2,1)S(1)}, bf16[256,256]{1,0:T(8,128)(2,1)S(1)}, u32[]{:S(2)}, u32[]{:S(2)}) collective-permute-start(bf16[256,256]{1,0:T(8,128)(2,1)S(1)} %get-tuple-element.21), channel_id=1, source_target_pairs={{0,256},{256,0},{1,257},{257,1},{2,258},{258,2},{3,259},{259,3},{4... | collective-permute-start | bytes 393224 | tf_op jit(solution)/shard_map/ppermute | solution.py:177
  26.5 0.1 reshape.63
  26.5 0.1 copy.20
  26.7 0.1 copy.24.left_cols
  26.7 4.7 %collective-permute-done.got = bf16[256,256]{1,0:T(8,128)(2,1)S(1)} collective-permute-done((bf16[256,256]{1,0:T(8,128)(2,1)S(1)}, bf16[256,256]{1,0:T(8,128)(2,1)S(1)}, u32[]{:S(2)}, u32[]{:S(2)}) %collective-permute-start) | collective-permute-done | bytes 131104 | tf_op jit(solution)/shard_map/ppermute | solution.py:177
  31.5 0.1 shard_map.94.grad_right
  31.6 2.7 %all-to-all-done = bf16[128,2,512]{2,1,0:T(2,128)(2,1)S(1)} async-done(((bf16[128,2,512]{2,1,0:T(2,128)(2,1)}), bf16[128,2,512]{2,1,0:T(2,128)(2,1)S(1)}, u32[]{:S(2)}, u32[]{:S(2)}) %all-to-all-start) | async-done | bytes 262176 | tf_op jit(solution)/shard_map/all_to_all | solution.py:159
  34.3 0.1 reshape.60.right
  34.4 1.7 %shard_map.95 = (bf16[8,8,32,128]{3,2,1,0:T(8,128)(2,1)}, f32[2,512,128]{2,1,0:T(8,128)S(1)}) custom-call(bf16[256,512]{1,0:T(8,128)(2,1)S(1)} %reshape.60.right, bf16[2,256,128]{2,1,0:T(8,128)(2,1)S(1)} %bitcast.50, bf16[32,64]{1,0:T(8,128)(2,1)S(1)} %copy.24.left_cols, f32[512,128]{1,0:T(8,128)S(1)} %shard_map.94.grad_right), custom_call_target="tpu_custom_call" | custom-call | flops 200000000 | bytes 2000000 | tf_op jit(solution)/shard_map/pallas_call | solution.py:190
  36.1 7.6 %all-to-all-start.1 = ((bf16[64,32,128]{2,1,0:T(8,128)(2,1)}), bf16[64,32,128]{2,1,0:T(8,128)(2,1)S(1)}, u32[]{:S(2)}, u32[]{:S(2)}) async-start(bf16[64,32,128]{2,1,0:T(8,128)(2,1)} %bitcast.11), calls=%async_computation.1 | async-start | bytes 1048576 | tf_op jit(solution)/shard_map/all_to_all | solution.py:208
  43.7 0.2 copy.52
  44.0 0.1 reshape.71.right
  44.1 0.4 shard_map.96
  44.5 6.8 %collective-permute-start.3 = (f32[2,64,128]{2,1,0:T(8,128)S(1)}, f32[2,64,128]{2,1,0:T(8,128)S(1)}, u32[]{:S(2)}, u32[]{:S(2)}) collective-permute-start(f32[2,64,128]{2,1,0:T(8,128)S(1)} %get-tuple-element.38), channel_id=1, source_target_pairs={{0,3},{1,2},{2,1},{3,0},{4,7},{5,6},{6,5},{7,4},{8,11},{9,10},{10,... | collective-permute-start | bytes 196616 | tf_op jit(solution)/shard_map/ppermute | solution.py:233
  51.3 2.4 %collective-permute-start.2 = (f32[2,64,128]{2,1,0:T(8,128)S(1)}, f32[2,64,128]{2,1,0:T(8,128)S(1)}, u32[]{:S(2)}, u32[]{:S(2)}) collective-permute-start(f32[2,64,128]{2,1,0:T(8,128)S(1)} %get-tuple-element.39), channel_id=1, source_target_pairs={{0,2},{1,3},{2,0},{3,1},{4,6},{5,7},{6,4},{7,5},{8,10},{9,11},{10,... | collective-permute-start | bytes 196616 | tf_op jit(solution)/shard_map/ppermute | solution.py:233
  53.8 1.9 %collective-permute-start.1 = (f32[2,64,128]{2,1,0:T(8,128)S(1)}, f32[2,64,128]{2,1,0:T(8,128)S(1)}, u32[]{:S(2)}, u32[]{:S(2)}) collective-permute-start(f32[2,64,128]{2,1,0:T(8,128)S(1)} %get-tuple-element.37), channel_id=1, source_target_pairs={{0,1},{1,0},{2,3},{3,2},{4,5},{5,4},{6,7},{7,6},{8,9},{9,8},{10,11... | collective-permute-start | bytes 196616 | tf_op jit(solution)/shard_map/ppermute | solution.py:233
  55.7 0.3 convolution_bitcast_fusion
  56.0 0.3 fusion.1
  56.2 0.0 copy-start.3
  56.2 0.7 reshape.74
  56.9 0.0 collective-permute-done.3
  56.9 1.2 %collective-permute-done.2 = f32[2,64,128]{2,1,0:T(8,128)S(1)} collective-permute-done((f32[2,64,128]{2,1,0:T(8,128)S(1)}, f32[2,64,128]{2,1,0:T(8,128)S(1)}, u32[]{:S(2)}, u32[]{:S(2)}) %collective-permute-start.2) | collective-permute-done | bytes 65568 | tf_op jit(solution)/shard_map/ppermute | solution.py:233
  58.1 0.0 collective-permute-done.1
  58.1 0.0 copy-done.3
  58.1 0.6 add_convert_fusion
  58.8 0.3 all-to-all-done.1.parts
  59.1 0.1 shard_map.97
  59.2 13.7 %all_to_all.15.refs_0_ = f32[8,16,128]{2,1,0:T(8,128)S(1)} all-to-all(f32[8,16,128]{2,1,0:T(8,128)S(1)} %shard_map.97), channel_id=1, replica_groups=mesh['half'=2,'z'=8,'y'=8,'seq'=4] {'half','seq'}, dimensions={0} | all-to-all | bytes 131072 | tf_op jit(solution)/shard_map/all_to_all | solution.py:247
  72.9 0.6 shard_map.98
  (2 shorter events, 0.0 us)
Async XLA Ops:
  2.1 20.2 %copy-start.1 = (bf16[1024,128]{1,0:T(8,128)(2,1)S(1)}, bf16[1024,128]{1,0:T(8,128)(2,1)}, u32[]{:S(2)}) copy-start(bf16[1024,128]{1,0:T(8,128)(2,1)} %param.8) | copy-start | bytes 786436
  2.1 32.2 %all-to-all-start = ((bf16[128,2,512]{2,1,0:T(2,128)(2,1)}), bf16[128,2,512]{2,1,0:T(2,128)(2,1)S(1)}, u32[]{:S(2)}, u32[]{:S(2)}) async-start(bf16[128,2,512]{2,1,0:T(2,128)(2,1)} %shard_map.92), calls=%async_computation | async-start | bytes 524288 | tf_op jit(solution)/shard_map/all_to_all | solution.py:159
  21.5 0.7 copy-start.2
  22.6 0.9 %copy-start = (bf16[2,256,128]{2,1,0:T(8,128)(2,1)S(1)}, bf16[2,256,128]{2,1,0:T(8,128)(2,1)}, u32[]{:S(2)}) copy-start(bf16[2,256,128]{2,1,0:T(8,128)(2,1)} %cotan.1) | copy-start | bytes 393220
  24.0 7.5 %collective-permute-start = (bf16[256,256]{1,0:T(8,128)(2,1)S(1)}, bf16[256,256]{1,0:T(8,128)(2,1)S(1)}, u32[]{:S(2)}, u32[]{:S(2)}) collective-permute-start(bf16[256,256]{1,0:T(8,128)(2,1)S(1)} %get-tuple-element.21), channel_id=1, source_target_pairs={{0,256},{256,0},{1,257},{257,1},{2,258},{258,2},{3,259},{259,3},{4... | collective-permute-start | bytes 393224 | tf_op jit(solution)/shard_map/ppermute | solution.py:177
  36.1 23.0 %all-to-all-start.1 = ((bf16[64,32,128]{2,1,0:T(8,128)(2,1)}), bf16[64,32,128]{2,1,0:T(8,128)(2,1)S(1)}, u32[]{:S(2)}, u32[]{:S(2)}) async-start(bf16[64,32,128]{2,1,0:T(8,128)(2,1)} %bitcast.11), calls=%async_computation.1 | async-start | bytes 1048576 | tf_op jit(solution)/shard_map/all_to_all | solution.py:208
  44.5 12.4 %collective-permute-start.3 = (f32[2,64,128]{2,1,0:T(8,128)S(1)}, f32[2,64,128]{2,1,0:T(8,128)S(1)}, u32[]{:S(2)}, u32[]{:S(2)}) collective-permute-start(f32[2,64,128]{2,1,0:T(8,128)S(1)} %get-tuple-element.38), channel_id=1, source_target_pairs={{0,3},{1,2},{2,1},{3,0},{4,7},{5,6},{6,5},{7,4},{8,11},{9,10},{10,... | collective-permute-start | bytes 196616 | tf_op jit(solution)/shard_map/ppermute | solution.py:233
  51.3 6.8 %collective-permute-start.2 = (f32[2,64,128]{2,1,0:T(8,128)S(1)}, f32[2,64,128]{2,1,0:T(8,128)S(1)}, u32[]{:S(2)}, u32[]{:S(2)}) collective-permute-start(f32[2,64,128]{2,1,0:T(8,128)S(1)} %get-tuple-element.39), channel_id=1, source_target_pairs={{0,2},{1,3},{2,0},{3,1},{4,6},{5,7},{6,4},{7,5},{8,10},{9,11},{10,... | collective-permute-start | bytes 196616 | tf_op jit(solution)/shard_map/ppermute | solution.py:233
  53.8 4.4 %collective-permute-start.1 = (f32[2,64,128]{2,1,0:T(8,128)S(1)}, f32[2,64,128]{2,1,0:T(8,128)S(1)}, u32[]{:S(2)}, u32[]{:S(2)}) collective-permute-start(f32[2,64,128]{2,1,0:T(8,128)S(1)} %get-tuple-element.37), channel_id=1, source_target_pairs={{0,1},{1,0},{2,3},{3,2},{4,5},{5,4},{6,7},{7,6},{8,9},{9,8},{10,11... | collective-permute-start | bytes 196616 | tf_op jit(solution)/shard_map/ppermute | solution.py:233
  56.2 1.9 %copy-start.3 = (f32[128]{0:T(128)S(1)}, f32[128]{0:T(128)}, u32[]{:S(2)}) copy-start(f32[128]{0:T(128)} %param.9) | copy-start | bytes 1540

commit v12 on v11

--- a/solution.py
+++ b/solution.py
@@ -119,15 +119,15 @@
     for half in range(HALVES):
         mine = total[half * rows : (half + 1) * rows]
         for q in range(seq):
-            out[half * seq + q, :rows] = mine
+            out[q * HALVES + half, :rows] = mine
             mine_too = jnp.where(place[0] == q, rights[half], 0.0)
-            out[half * seq + q, rows:] = jnp.concatenate([mine_too, bias], axis=0)
+            out[q * HALVES + half, rows:] = jnp.concatenate([mine_too, bias], axis=0)
 
 
 def closing_kernel(scale, parts, weight, right, bias):
     rows = weight.shape[0]
     seq = parts.shape[0] // HALVES
-    sums = [jnp.sum(parts[half * seq : (half + 1) * seq], axis=0) * scale for half in range(HALVES)]
+    sums = [sum(parts[q * HALVES + half] for q in range(seq)) * scale for half in range(HALVES)]
     weight[...] = sums[0][:rows] + sums[1][:rows]
     pieces = (sums[0] + sums[1])[rows + rows // 2 :]
     bias[...] = (pieces[0:1] + pieces[1:2]) * (1.0 / (scale * seq))
@@ -244,7 +244,7 @@
         out_specs=WHOLE,
         compiler_params=pltpu.CompilerParams(vmem_limit_bytes=8 * 1024 * 1024),
     )(here.reshape(1), parts)
-    last = lax.all_to_all(last, ("half", "seq"), 0, 0, tiled=True)
+    last = lax.all_to_all(last, ("seq", "half"), 0, 0, tiled=True)
     grad_weight, grad_right, grad_bias = pl.pallas_call(
         lambda *refs: closing_kernel(scale, *refs),
         out_shape=(

time: 74 us -> 74.2 us (level)
  no operation moved by 1% of the time
where the time goes in v12:
time: 74.2 us; the launch traced here: 73.7 us
  starting transfers between devices  40.6 us (55%)
  blocking collectives  13.9 us (19%)
  waiting for transfers between devices  9.01 us (12%)
  Pallas kernels  4.8 us (6%)
  local copies, waits for them, and re-layouts  3.14 us (4%)
  between operations  0.85 us (1%)
  matrix products  0.76 us (1%)
    all_to_all x1, starting transfers between devices, on_device(): arrived = lax.all_to_all(opening, ('y', 'z', 'half'), 0, 0, tiled=True)  19.4 us
    all_to_all x1, blocking collectives, on_device(): last = lax.all_to_all(last, ('seq', 'half'), 0, 0, tiled=True)  13.9 us
    ppermute x3, starting transfers between devices, on_device(): lax.ppermute(sent, 'seq', [(q, q ^ step) for q in range(seq)])  11.1 us
    all_to_all x1, starting transfers between devices, on_device(): lax.all_to_all(message.reshape(planes, 4 * rows, P_SIZE), ('z', 'y'), 0,...  7.58 us
    ppermute x1, waiting for transfers between devices, on_device(): got = lax.ppermute(sent, 'half', [(0, 1), (1, 0)])  4.73 us
    all_to_all x1, waiting for transfers between devices, on_device(): arrived = lax.all_to_all(opening, ('y', 'z', 'half'), 0, 0, tiled=True)  2.74 us
    ppermute x1, starting transfers between devices, on_device(): got = lax.ppermute(sent, 'half', [(0, 1), (1, 0)])  2.48 us
    pallas_call x1, Pallas kernels, on_device(): pl.pallas_call(products_kernel, out_shape=(jax.ShapeDtypeStruct((SIDE, SI...  1.69 us
  transfers between devices with their start and end apart: 6, of which 4 were waited for; matrix products, arithmetic and copies ran while one was open for 4% of the time, Pallas kernels for 1%

profile of v12, /device:TPU:1, one launch (start us, length us, event | category | flops | bytes accessed | tf_op | source)
XLA Modules:
  0.0 73.7 jit_solution(15599400148860875579)
XLA Ops:
  0.6 1.4 %shard_map.92 = bf16[128,2,512]{2,1,0:T(2,128)(2,1)} custom-call(bf16[2,512]{1,0:T(2,128)(2,1)} %right.1), custom_call_target="tpu_custom_call" | custom-call | tf_op jit(solution)/shard_map/pallas_call | solution.py:152
  2.1 0.0 copy-start.1
  2.1 19.4 %all-to-all-start = ((bf16[128,2,512]{2,1,0:T(2,128)(2,1)}), bf16[128,2,512]{2,1,0:T(2,128)(2,1)S(1)}, u32[]{:S(2)}, u32[]{:S(2)}) async-start(bf16[128,2,512]{2,1,0:T(2,128)(2,1)} %shard_map.92), calls=%async_computation | async-start | bytes 524288 | tf_op jit(solution)/shard_map/all_to_all | solution.py:159
  21.5 0.0 copy-start.2
  21.6 0.7 copy-done.2
  22.2 0.1 reshape.76
  22.3 0.0 copy-done.1
  22.3 0.2 fusion.2
  22.6 0.1 copy.22
  22.6 0.0 copy-start
  22.6 0.1 copy.23
  22.7 0.8 %copy-done = bf16[2,256,128]{2,1,0:T(8,128)(2,1)S(1)} copy-done((bf16[2,256,128]{2,1,0:T(8,128)(2,1)S(1)}, bf16[2,256,128]{2,1,0:T(8,128)(2,1)}, u32[]{:S(2)}) %copy-start) | copy-done | bytes 131096
  23.5 0.4 shard_map.93
  24.0 2.5 %collective-permute-start = (bf16[256,256]{1,0:T(8,128)(2,1)S(1)}, bf16[256,256]{1,0:T(8,128)(2,1)S(1)}, u32[]{:S(2)}, u32[]{:S(2)}) collective-permute-start(bf16[256,256]{1,0:T(8,128)(2,1)S(1)} %get-tuple-element.21), channel_id=1, source_target_pairs={{0,256},{256,0},{1,257},{257,1},{2,258},{258,2},{3,259},{259,3},{4... | collective-permute-start | bytes 393224 | tf_op jit(solution)/shard_map/ppermute | solution.py:177
  26.5 0.1 reshape.63
  26.5 0.1 copy.20
  26.7 0.1 copy.24.left_cols
  26.7 4.7 %collective-permute-done.got = bf16[256,256]{1,0:T(8,128)(2,1)S(1)} collective-permute-done((bf16[256,256]{1,0:T(8,128)(2,1)S(1)}, bf16[256,256]{1,0:T(8,128)(2,1)S(1)}, u32[]{:S(2)}, u32[]{:S(2)}) %collective-permute-start) | collective-permute-done | bytes 131104 | tf_op jit(solution)/shard_map/ppermute | solution.py:177
  31.5 0.1 shard_map.94.grad_right
  31.6 2.7 %all-to-all-done = bf16[128,2,512]{2,1,0:T(2,128)(2,1)S(1)} async-done(((bf16[128,2,512]{2,1,0:T(2,128)(2,1)}), bf16[128,2,512]{2,1,0:T(2,128)(2,1)S(1)}, u32[]{:S(2)}, u32[]{:S(2)}) %all-to-all-start) | async-done | bytes 262176 | tf_op jit(solution)/shard_map/all_to_all | solution.py:159
  34.3 0.1 reshape.60.right
  34.4 1.7 %shard_map.95 = (bf16[8,8,32,128]{3,2,1,0:T(8,128)(2,1)}, f32[2,512,128]{2,1,0:T(8,128)S(1)}) custom-call(bf16[256,512]{1,0:T(8,128)(2,1)S(1)} %reshape.60.right, bf16[2,256,128]{2,1,0:T(8,128)(2,1)S(1)} %bitcast.50, bf16[32,64]{1,0:T(8,128)(2,1)S(1)} %copy.24.left_cols, f32[512,128]{1,0:T(8,128)S(1)} %shard_map.94.grad_right), custom_call_target="tpu_custom_call" | custom-call | flops 200000000 | bytes 2000000 | tf_op jit(solution)/shard_map/pallas_call | solution.py:190
  36.1 7.6 %all-to-all-start.1 = ((bf16[64,32,128]{2,1,0:T(8,128)(2,1)}), bf16[64,32,128]{2,1,0:T(8,128)(2,1)S(1)}, u32[]{:S(2)}, u32[]{:S(2)}) async-start(bf16[64,32,128]{2,1,0:T(8,128)(2,1)} %bitcast.11), calls=%async_computation.1 | async-start | bytes 1048576 | tf_op jit(solution)/shard_map/all_to_all | solution.py:208
  43.7 0.2 copy.52
  44.0 0.1 reshape.71.right
  44.1 0.4 shard_map.96
  44.5 6.8 %collective-permute-start.3 = (f32[2,64,128]{2,1,0:T(8,128)S(1)}, f32[2,64,128]{2,1,0:T(8,128)S(1)}, u32[]{:S(2)}, u32[]{:S(2)}) collective-permute-start(f32[2,64,128]{2,1,0:T(8,128)S(1)} %get-tuple-element.38), channel_id=1, source_target_pairs={{0,3},{1,2},{2,1},{3,0},{4,7},{5,6},{6,5},{7,4},{8,11},{9,10},{10,... | collective-permute-start | bytes 196616 | tf_op jit(solution)/shard_map/ppermute | solution.py:233
  51.3 2.4 %collective-permute-start.2 = (f32[2,64,128]{2,1,0:T(8,128)S(1)}, f32[2,64,128]{2,1,0:T(8,128)S(1)}, u32[]{:S(2)}, u32[]{:S(2)}) collective-permute-start(f32[2,64,128]{2,1,0:T(8,128)S(1)} %get-tuple-element.39), channel_id=1, source_target_pairs={{0,2},{1,3},{2,0},{3,1},{4,6},{5,7},{6,4},{7,5},{8,10},{9,11},{10,... | collective-permute-start | bytes 196616 | tf_op jit(solution)/shard_map/ppermute | solution.py:233
  53.8 1.9 %collective-permute-start.1 = (f32[2,64,128]{2,1,0:T(8,128)S(1)}, f32[2,64,128]{2,1,0:T(8,128)S(1)}, u32[]{:S(2)}, u32[]{:S(2)}) collective-permute-start(f32[2,64,128]{2,1,0:T(8,128)S(1)} %get-tuple-element.37), channel_id=1, source_target_pairs={{0,1},{1,0},{2,3},{3,2},{4,5},{5,4},{6,7},{7,6},{8,9},{9,8},{10,11... | collective-permute-start | bytes 196616 | tf_op jit(solution)/shard_map/ppermute | solution.py:233
  55.7 0.3 convolution_bitcast_fusion
  56.0 0.3 fusion.1
  56.2 0.0 copy-start.3
  56.2 0.7 reshape.74
  56.9 0.0 collective-permute-done.3
  56.9 1.2 %collective-permute-done.2 = f32[2,64,128]{2,1,0:T(8,128)S(1)} collective-permute-done((f32[2,64,128]{2,1,0:T(8,128)S(1)}, f32[2,64,128]{2,1,0:T(8,128)S(1)}, u32[]{:S(2)}, u32[]{:S(2)}) %collective-permute-start.2) | collective-permute-done | bytes 65568 | tf_op jit(solution)/shard_map/ppermute | solution.py:233
  58.1 0.0 collective-permute-done.1
  58.1 0.0 copy-done.3
  58.1 0.6 add_convert_fusion
  58.8 0.3 all-to-all-done.1.parts
  59.1 0.1 shard_map.97
  59.2 13.9 %all_to_all.15.refs_0_ = f32[8,16,128]{2,1,0:T(8,128)S(1)} all-to-all(f32[8,16,128]{2,1,0:T(8,128)S(1)} %shard_map.97), channel_id=1, replica_groups=mesh['half'=2,'z'=8,'y'=8,'seq'=4] {'seq','half'}, dimensions={0} | all-to-all | bytes 131072 | tf_op jit(solution)/shard_map/all_to_all | solution.py:247
  73.1 0.6 shard_map.98
  (2 shorter events, 0.0 us)
Async XLA Ops:
  2.1 20.2 %copy-start.1 = (bf16[1024,128]{1,0:T(8,128)(2,1)S(1)}, bf16[1024,128]{1,0:T(8,128)(2,1)}, u32[]{:S(2)}) copy-start(bf16[1024,128]{1,0:T(8,128)(2,1)} %param.8) | copy-start | bytes 786436
  2.1 32.2 %all-to-all-start = ((bf16[128,2,512]{2,1,0:T(2,128)(2,1)}), bf16[128,2,512]{2,1,0:T(2,128)(2,1)S(1)}, u32[]{:S(2)}, u32[]{:S(2)}) async-start(bf16[128,2,512]{2,1,0:T(2,128)(2,1)} %shard_map.92), calls=%async_computation | async-start | bytes 524288 | tf_op jit(solution)/shard_map/all_to_all | solution.py:159
  21.5 0.7 copy-start.2
  22.6 0.9 %copy-start = (bf16[2,256,128]{2,1,0:T(8,128)(2,1)S(1)}, bf16[2,256,128]{2,1,0:T(8,128)(2,1)}, u32[]{:S(2)}) copy-start(bf16[2,256,128]{2,1,0:T(8,128)(2,1)} %cotan.1) | copy-start | bytes 393220
  24.0 7.5 %collective-permute-start = (bf16[256,256]{1,0:T(8,128)(2,1)S(1)}, bf16[256,256]{1,0:T(8,128)(2,1)S(1)}, u32[]{:S(2)}, u32[]{:S(2)}) collective-permute-start(bf16[256,256]{1,0:T(8,128)(2,1)S(1)} %get-tuple-element.21), channel_id=1, source_target_pairs={{0,256},{256,0},{1,257},{257,1},{2,258},{258,2},{3,259},{259,3},{4... | collective-permute-start | bytes 393224 | tf_op jit(solution)/shard_map/ppermute | solution.py:177
  36.1 23.0 %all-to-all-start.1 = ((bf16[64,32,128]{2,1,0:T(8,128)(2,1)}), bf16[64,32,128]{2,1,0:T(8,128)(2,1)S(1)}, u32[]{:S(2)}, u32[]{:S(2)}) async-start(bf16[64,32,128]{2,1,0:T(8,128)(2,1)} %bitcast.11), calls=%async_computation.1 | async-start | bytes 1048576 | tf_op jit(solution)/shard_map/all_to_all | solution.py:208
  44.5 12.4 %collective-permute-start.3 = (f32[2,64,128]{2,1,0:T(8,128)S(1)}, f32[2,64,128]{2,1,0:T(8,128)S(1)}, u32[]{:S(2)}, u32[]{:S(2)}) collective-permute-start(f32[2,64,128]{2,1,0:T(8,128)S(1)} %get-tuple-element.38), channel_id=1, source_target_pairs={{0,3},{1,2},{2,1},{3,0},{4,7},{5,6},{6,5},{7,4},{8,11},{9,10},{10,... | collective-permute-start | bytes 196616 | tf_op jit(solution)/shard_map/ppermute | solution.py:233
  51.3 6.8 %collective-permute-start.2 = (f32[2,64,128]{2,1,0:T(8,128)S(1)}, f32[2,64,128]{2,1,0:T(8,128)S(1)}, u32[]{:S(2)}, u32[]{:S(2)}) collective-permute-start(f32[2,64,128]{2,1,0:T(8,128)S(1)} %get-tuple-element.39), channel_id=1, source_target_pairs={{0,2},{1,3},{2,0},{3,1},{4,6},{5,7},{6,4},{7,5},{8,10},{9,11},{10,... | collective-permute-start | bytes 196616 | tf_op jit(solution)/shard_map/ppermute | solution.py:233
  53.8 4.4 %collective-permute-start.1 = (f32[2,64,128]{2,1,0:T(8,128)S(1)}, f32[2,64,128]{2,1,0:T(8,128)S(1)}, u32[]{:S(2)}, u32[]{:S(2)}) collective-permute-start(f32[2,64,128]{2,1,0:T(8,128)S(1)} %get-tuple-element.37), channel_id=1, source_target_pairs={{0,1},{1,0},{2,3},{3,2},{4,5},{5,4},{6,7},{7,6},{8,9},{9,8},{10,11... | collective-permute-start | bytes 196616 | tf_op jit(solution)/shard_map/ppermute | solution.py:233
  56.2 1.9 %copy-start.3 = (f32[128]{0:T(128)S(1)}, f32[128]{0:T(128)}, u32[]{:S(2)}) copy-start(f32[128]{0:T(128)} %param.9) | copy-start | bytes 1540

commit v13 on v11

--- a/solution.py
+++ b/solution.py
@@ -154,7 +154,7 @@
         out_shape=jax.ShapeDtypeStruct((res, ROW_DEV, WIDE), jnp.bfloat16),
         in_specs=[WHOLE],
         out_specs=pl.BlockSpec(memory_space=pl.ANY),
-        scratch_shapes=[pltpu.VMEM((16, ROW_DEV, WIDE), jnp.bfloat16), pltpu.SemaphoreType.DMA((res // 16,))],
+        scratch_shapes=[pltpu.VMEM((32, ROW_DEV, WIDE), jnp.bfloat16), pltpu.SemaphoreType.DMA((res // 32,))],
     )(right_proj)
     arrived = lax.all_to_all(opening, ("y", "z", "half"), 0, 0, tiled=True)
     cotan_arrived = pair_cotangent.reshape(ROW_DEV, HALVES, SIDE, SIDE, ROW_DEV, P_SIZE)

time: 74 us -> 74 us (level)
  no operation moved by 1% of the time
where the time goes in v13:
time: 74 us; the launch traced here: 73.5 us
  starting transfers between devices  40.6 us (55%)
  blocking collectives  13.7 us (19%)
  waiting for transfers between devices  9.02 us (12%)
  Pallas kernels  4.77 us (6%)
  local copies, waits for them, and re-layouts  3.14 us (4%)
  between operations  0.85 us (1%)
  matrix products  0.76 us (1%)
    all_to_all x1, starting transfers between devices, on_device(): arrived = lax.all_to_all(opening, ('y', 'z', 'half'), 0, 0, tiled=True)  19.4 us
    all_to_all x1, blocking collectives, on_device(): last = lax.all_to_all(last, ('half', 'seq'), 0, 0, tiled=True)  13.7 us
    ppermute x3, starting transfers between devices, on_device(): lax.ppermute(sent, 'seq', [(q, q ^ step) for q in range(seq)])  11.1 us
    all_to_all x1, starting transfers between devices, on_device(): lax.all_to_all(message.reshape(planes, 4 * rows, P_SIZE), ('z', 'y'), 0,...  7.58 us
    ppermute x1, waiting for transfers between devices, on_device(): got = lax.ppermute(sent, 'half', [(0, 1), (1, 0)])  4.73 us
    all_to_all x1, waiting for transfers between devices, on_device(): arrived = lax.all_to_all(opening, ('y', 'z', 'half'), 0, 0, tiled=True)  2.74 us
    ppermute x1, starting transfers between devices, on_device(): got = lax.ppermute(sent, 'half', [(0, 1), (1, 0)])  2.48 us
    pallas_call x1, Pallas kernels, on_device(): pl.pallas_call(products_kernel, out_shape=(jax.ShapeDtypeStruct((SIDE, SI...  1.69 us
  transfers between devices with their start and end apart: 6, of which 4 were waited for; matrix products, arithmetic and copies ran while one was open for 4% of the time, Pallas kernels for 1%

profile of v13, /device:TPU:1, one launch (start us, length us, event | category | flops | bytes accessed | tf_op | source)
XLA Modules:
  0.0 73.5 jit_solution(11243369643696114125)
XLA Ops:
  0.6 1.4 %shard_map.92 = bf16[128,2,512]{2,1,0:T(2,128)(2,1)} custom-call(bf16[2,512]{1,0:T(2,128)(2,1)} %right.1), custom_call_target="tpu_custom_call" | custom-call | tf_op jit(solution)/shard_map/pallas_call | solution.py:152
  2.1 0.0 copy-start.1
  2.1 19.4 %all-to-all-start = ((bf16[128,2,512]{2,1,0:T(2,128)(2,1)}), bf16[128,2,512]{2,1,0:T(2,128)(2,1)S(1)}, u32[]{:S(2)}, u32[]{:S(2)}) async-start(bf16[128,2,512]{2,1,0:T(2,128)(2,1)} %shard_map.92), calls=%async_computation | async-start | bytes 524288 | tf_op jit(solution)/shard_map/all_to_all | solution.py:159
  21.5 0.0 copy-start.2
  21.5 0.7 copy-done.2
  22.2 0.1 reshape.76
  22.3 0.0 copy-done.1
  22.3 0.2 fusion.2
  22.5 0.1 copy.22
  22.6 0.0 copy-start
  22.6 0.1 copy.23
  22.7 0.8 %copy-done = bf16[2,256,128]{2,1,0:T(8,128)(2,1)S(1)} copy-done((bf16[2,256,128]{2,1,0:T(8,128)(2,1)S(1)}, bf16[2,256,128]{2,1,0:T(8,128)(2,1)}, u32[]{:S(2)}) %copy-start) | copy-done | bytes 131096
  23.5 0.4 shard_map.93
  23.9 2.5 %collective-permute-start = (bf16[256,256]{1,0:T(8,128)(2,1)S(1)}, bf16[256,256]{1,0:T(8,128)(2,1)S(1)}, u32[]{:S(2)}, u32[]{:S(2)}) collective-permute-start(bf16[256,256]{1,0:T(8,128)(2,1)S(1)} %get-tuple-element.21), channel_id=1, source_target_pairs={{0,256},{256,0},{1,257},{257,1},{2,258},{258,2},{3,259},{259,3},{4... | collective-permute-start | bytes 393224 | tf_op jit(solution)/shard_map/ppermute | solution.py:177
  26.4 0.1 reshape.63
  26.5 0.1 copy.20
  26.6 0.1 copy.24.left_cols
  26.7 4.7 %collective-permute-done.got = bf16[256,256]{1,0:T(8,128)(2,1)S(1)} collective-permute-done((bf16[256,256]{1,0:T(8,128)(2,1)S(1)}, bf16[256,256]{1,0:T(8,128)(2,1)S(1)}, u32[]{:S(2)}, u32[]{:S(2)}) %collective-permute-start) | collective-permute-done | bytes 131104 | tf_op jit(solution)/shard_map/ppermute | solution.py:177
  31.4 0.1 shard_map.94.grad_right
  31.5 2.7 %all-to-all-done = bf16[128,2,512]{2,1,0:T(2,128)(2,1)S(1)} async-done(((bf16[128,2,512]{2,1,0:T(2,128)(2,1)}), bf16[128,2,512]{2,1,0:T(2,128)(2,1)S(1)}, u32[]{:S(2)}, u32[]{:S(2)}) %all-to-all-start) | async-done | bytes 262176 | tf_op jit(solution)/shard_map/all_to_all | solution.py:159
  34.3 0.1 reshape.60.right
  34.4 1.7 %shard_map.95 = (bf16[8,8,32,128]{3,2,1,0:T(8,128)(2,1)}, f32[2,512,128]{2,1,0:T(8,128)S(1)}) custom-call(bf16[256,512]{1,0:T(8,128)(2,1)S(1)} %reshape.60.right, bf16[2,256,128]{2,1,0:T(8,128)(2,1)S(1)} %bitcast.50, bf16[32,64]{1,0:T(8,128)(2,1)S(1)} %copy.24.left_cols, f32[512,128]{1,0:T(8,128)S(1)} %shard_map.94.grad_right), custom_call_target="tpu_custom_call" | custom-call | flops 200000000 | bytes 2000000 | tf_op jit(solution)/shard_map/pallas_call | solution.py:190
  36.1 7.6 %all-to-all-start.1 = ((bf16[64,32,128]{2,1,0:T(8,128)(2,1)}), bf16[64,32,128]{2,1,0:T(8,128)(2,1)S(1)}, u32[]{:S(2)}, u32[]{:S(2)}) async-start(bf16[64,32,128]{2,1,0:T(8,128)(2,1)} %bitcast.11), calls=%async_computation.1 | async-start | bytes 1048576 | tf_op jit(solution)/shard_map/all_to_all | solution.py:208
  43.7 0.2 copy.52
  43.9 0.1 reshape.71.right
  44.0 0.4 shard_map.96
  44.5 6.8 %collective-permute-start.3 = (f32[2,64,128]{2,1,0:T(8,128)S(1)}, f32[2,64,128]{2,1,0:T(8,128)S(1)}, u32[]{:S(2)}, u32[]{:S(2)}) collective-permute-start(f32[2,64,128]{2,1,0:T(8,128)S(1)} %get-tuple-element.38), channel_id=1, source_target_pairs={{0,3},{1,2},{2,1},{3,0},{4,7},{5,6},{6,5},{7,4},{8,11},{9,10},{10,... | collective-permute-start | bytes 196616 | tf_op jit(solution)/shard_map/ppermute | solution.py:233
  51.3 2.4 %collective-permute-start.2 = (f32[2,64,128]{2,1,0:T(8,128)S(1)}, f32[2,64,128]{2,1,0:T(8,128)S(1)}, u32[]{:S(2)}, u32[]{:S(2)}) collective-permute-start(f32[2,64,128]{2,1,0:T(8,128)S(1)} %get-tuple-element.39), channel_id=1, source_target_pairs={{0,2},{1,3},{2,0},{3,1},{4,6},{5,7},{6,4},{7,5},{8,10},{9,11},{10,... | collective-permute-start | bytes 196616 | tf_op jit(solution)/shard_map/ppermute | solution.py:233
  53.7 1.9 %collective-permute-start.1 = (f32[2,64,128]{2,1,0:T(8,128)S(1)}, f32[2,64,128]{2,1,0:T(8,128)S(1)}, u32[]{:S(2)}, u32[]{:S(2)}) collective-permute-start(f32[2,64,128]{2,1,0:T(8,128)S(1)} %get-tuple-element.37), channel_id=1, source_target_pairs={{0,1},{1,0},{2,3},{3,2},{4,5},{5,4},{6,7},{7,6},{8,9},{9,8},{10,11... | collective-permute-start | bytes 196616 | tf_op jit(solution)/shard_map/ppermute | solution.py:233
  55.7 0.3 convolution_bitcast_fusion
  55.9 0.3 fusion.1
  56.2 0.0 copy-start.3
  56.2 0.7 reshape.74
  56.9 0.0 collective-permute-done.3
  56.9 1.2 %collective-permute-done.2 = f32[2,64,128]{2,1,0:T(8,128)S(1)} collective-permute-done((f32[2,64,128]{2,1,0:T(8,128)S(1)}, f32[2,64,128]{2,1,0:T(8,128)S(1)}, u32[]{:S(2)}, u32[]{:S(2)}) %collective-permute-start.2) | collective-permute-done | bytes 65568 | tf_op jit(solution)/shard_map/ppermute | solution.py:233
  58.1 0.0 collective-permute-done.1
  58.1 0.0 copy-done.3
  58.1 0.6 add_convert_fusion
  58.8 0.3 all-to-all-done.1.parts
  59.1 0.1 shard_map.97
  59.2 13.7 %all_to_all.15.refs_0_ = f32[8,16,128]{2,1,0:T(8,128)S(1)} all-to-all(f32[8,16,128]{2,1,0:T(8,128)S(1)} %shard_map.97), channel_id=1, replica_groups=mesh['half'=2,'z'=8,'y'=8,'seq'=4] {'half','seq'}, dimensions={0} | all-to-all | bytes 131072 | tf_op jit(solution)/shard_map/all_to_all | solution.py:247
  72.9 0.6 shard_map.98
  (2 shorter events, 0.0 us)
Async XLA Ops:
  2.1 20.2 %copy-start.1 = (bf16[1024,128]{1,0:T(8,128)(2,1)S(1)}, bf16[1024,128]{1,0:T(8,128)(2,1)}, u32[]{:S(2)}) copy-start(bf16[1024,128]{1,0:T(8,128)(2,1)} %param.8) | copy-start | bytes 786436
  2.1 32.2 %all-to-all-start = ((bf16[128,2,512]{2,1,0:T(2,128)(2,1)}), bf16[128,2,512]{2,1,0:T(2,128)(2,1)S(1)}, u32[]{:S(2)}, u32[]{:S(2)}) async-start(bf16[128,2,512]{2,1,0:T(2,128)(2,1)} %shard_map.92), calls=%async_computation | async-start | bytes 524288 | tf_op jit(solution)/shard_map/all_to_all | solution.py:159
  21.5 0.7 copy-start.2
  22.6 0.9 %copy-start = (bf16[2,256,128]{2,1,0:T(8,128)(2,1)S(1)}, bf16[2,256,128]{2,1,0:T(8,128)(2,1)}, u32[]{:S(2)}) copy-start(bf16[2,256,128]{2,1,0:T(8,128)(2,1)} %cotan.1) | copy-start | bytes 393220
  23.9 7.5 %collective-permute-start = (bf16[256,256]{1,0:T(8,128)(2,1)S(1)}, bf16[256,256]{1,0:T(8,128)(2,1)S(1)}, u32[]{:S(2)}, u32[]{:S(2)}) collective-permute-start(bf16[256,256]{1,0:T(8,128)(2,1)S(1)} %get-tuple-element.21), channel_id=1, source_target_pairs={{0,256},{256,0},{1,257},{257,1},{2,258},{258,2},{3,259},{259,3},{4... | collective-permute-start | bytes 393224 | tf_op jit(solution)/shard_map/ppermute | solution.py:177
  36.1 23.0 %all-to-all-start.1 = ((bf16[64,32,128]{2,1,0:T(8,128)(2,1)}), bf16[64,32,128]{2,1,0:T(8,128)(2,1)S(1)}, u32[]{:S(2)}, u32[]{:S(2)}) async-start(bf16[64,32,128]{2,1,0:T(8,128)(2,1)} %bitcast.11), calls=%async_computation.1 | async-start | bytes 1048576 | tf_op jit(solution)/shard_map/all_to_all | solution.py:208
  44.5 12.4 %collective-permute-start.3 = (f32[2,64,128]{2,1,0:T(8,128)S(1)}, f32[2,64,128]{2,1,0:T(8,128)S(1)}, u32[]{:S(2)}, u32[]{:S(2)}) collective-permute-start(f32[2,64,128]{2,1,0:T(8,128)S(1)} %get-tuple-element.38), channel_id=1, source_target_pairs={{0,3},{1,2},{2,1},{3,0},{4,7},{5,6},{6,5},{7,4},{8,11},{9,10},{10,... | collective-permute-start | bytes 196616 | tf_op jit(solution)/shard_map/ppermute | solution.py:233
  51.3 6.8 %collective-permute-start.2 = (f32[2,64,128]{2,1,0:T(8,128)S(1)}, f32[2,64,128]{2,1,0:T(8,128)S(1)}, u32[]{:S(2)}, u32[]{:S(2)}) collective-permute-start(f32[2,64,128]{2,1,0:T(8,128)S(1)} %get-tuple-element.39), channel_id=1, source_target_pairs={{0,2},{1,3},{2,0},{3,1},{4,6},{5,7},{6,4},{7,5},{8,10},{9,11},{10,... | collective-permute-start | bytes 196616 | tf_op jit(solution)/shard_map/ppermute | solution.py:233
  53.7 4.4 %collective-permute-start.1 = (f32[2,64,128]{2,1,0:T(8,128)S(1)}, f32[2,64,128]{2,1,0:T(8,128)S(1)}, u32[]{:S(2)}, u32[]{:S(2)}) collective-permute-start(f32[2,64,128]{2,1,0:T(8,128)S(1)} %get-tuple-element.37), channel_id=1, source_target_pairs={{0,1},{1,0},{2,3},{3,2},{4,5},{5,4},{6,7},{7,6},{8,9},{9,8},{10,11... | collective-permute-start | bytes 196616 | tf_op jit(solution)/shard_map/ppermute | solution.py:233
  56.2 1.9 %copy-start.3 = (f32[128]{0:T(128)S(1)}, f32[128]{0:T(128)}, u32[]{:S(2)}) copy-start(f32[128]{0:T(128)} %param.9) | copy-start | bytes 1540
